TPU v7x, 128 devices: a whole 4x4x4 slice. The times are simulated.
128 devices in a mesh: ctx: 64 (over y_lo, x, z, core), ch: 2 (over y_hi).
Axes of the slice: x: 4, y: 4 (y_hi: 2, y_lo: 2; y = y_hi * 2 + y_lo), z: 4, core: 2. Of those that a mesh axis runs over, the one named last changes fastest.
Arguments:
- tokens: bfloat16 [32768, 8192], P('ctx', 'ch'), may hold values from -6 to 6
- in_weight: bfloat16 [8192, 1024], P('ch'), may hold values from -0.0625 to 0.0625
- filter_taps: float32 [32768, 1024], P('ctx', 'ch'), may hold values from -0.03125 to 0.03125
- skip_gain: float32 [1024], P('ch'), may hold values from 0.25 to 1.75
- out_weight: bfloat16 [1024, 8192], P('ch'), may hold values from -0.1875 to 0.1875
Outputs:
- mixed: bfloat16 [32768, 8192], P('ctx', 'ch')
All inputs are finite; a program needn't handle non-finite values.
Results may differ from a plain program's by a relative error of at most 0.0049.
Values may be sent and summed in bfloat16 or wider, within the bound.
No kernel may reach another device: no remote copies, remote signals or barrier semaphores. Data moves between devices by JAX's collectives and lax.ppermute only.
A program may use at most 128 MiB of HBM per device.

v0:
```python
import jax
import jax.numpy as jnp
from jax import lax
from jax.sharding import PartitionSpec as P

highest = lax.Precision.HIGHEST


def phase_table(row_count, col_count, period, col_offset):
    row_index = lax.broadcasted_iota(jnp.int32, (row_count, col_count), 0)
    col_index = lax.broadcasted_iota(jnp.int32, (row_count, col_count), 1) + col_offset
    angles = (row_index * col_index % period).astype(jnp.float32) * (2.0 * jnp.pi / period)
    return (jnp.cos(angles), jnp.sin(angles))


def complex_product(first_real, first_imag, second_real, second_imag):
    return (
        first_real * second_real - first_imag * second_imag,
        first_real * second_imag + first_imag * second_real,
    )


def four_step(projected, filter_taps, devices, position, channels):
    freq_groups = 2 * devices
    stride = position // devices
    period = position * freq_groups
    stacked = jnp.stack([projected, filter_taps]).reshape(2, 1, position, channels)
    columns = lax.all_to_all(stacked, "ctx", split_axis=2, concat_axis=1, tiled=True)
    group_cos, group_sin = phase_table(freq_groups, devices, freq_groups, 0)
    group_table = jnp.concatenate([group_cos, -group_sin], axis=0)
    mixed_groups = jnp.einsum("kr,arjc->akjc", group_table, columns, precision=highest)
    first_real = mixed_groups[:, :freq_groups]
    first_imag = mixed_groups[:, freq_groups:]
    twist_cos, twist_sin = phase_table(freq_groups, stride, period, lax.axis_index("ctx") * stride)
    twist_cos = twist_cos[None, :, :, None]
    twist_sin = twist_sin[None, :, :, None]
    turned_real = first_real * twist_cos + first_imag * twist_sin
    turned_imag = first_imag * twist_cos - first_real * twist_sin
    spread = jnp.stack([turned_real, turned_imag], axis=1)
    gathered = lax.all_to_all(spread, "ctx", split_axis=2, concat_axis=3, tiled=True)
    line_cos, line_sin = phase_table(position, position, position, 0)
    line_table = jnp.stack([line_cos, line_sin])
    line_spec = jnp.einsum("tkj,abqjc->tabqkc", line_table, gathered, precision=highest)
    spec_real = line_spec[0, :, 0] + line_spec[1, :, 1]
    spec_imag = line_spec[0, :, 1] - line_spec[1, :, 0]
    spectra = jnp.stack([spec_real, spec_imag], axis=1)
    blocked = lax.all_to_all(spectra, "ctx", split_axis=3, concat_axis=2, tiled=True)
    prod_real, prod_imag = complex_product(
        blocked[0, 0], blocked[0, 1], blocked[1, 0], blocked[1, 1]
    )
    product = lax.all_to_all(
        jnp.stack([prod_real, prod_imag]), "ctx", split_axis=1, concat_axis=2, tiled=True
    )
    unlined = jnp.einsum("tjk,aqkc->taqjc", line_table, product, precision=highest)
    back_real = unlined[0, 0] - unlined[1, 1]
    back_imag = unlined[0, 1] + unlined[1, 0]
    returned = lax.all_to_all(
        jnp.stack([back_real, back_imag]), "ctx", split_axis=2, concat_axis=1, tiled=True
    )
    unturned_real = returned[0] * twist_cos[0] - returned[1] * twist_sin[0]
    unturned_imag = returned[1] * twist_cos[0] + returned[0] * twist_sin[0]
    back_cos, back_sin = phase_table(devices, freq_groups, freq_groups, 0)
    back_table = jnp.concatenate([back_cos, -back_sin], axis=1) * (1.0 / period)
    stacked_back = jnp.concatenate([unturned_real, unturned_imag], axis=0)
    pieces = jnp.einsum("rk,kjc->rjc", back_table, stacked_back, precision=highest)
    return lax.all_to_all(pieces, "ctx", split_axis=0, concat_axis=1, tiled=True).reshape(
        position, channels
    )


def shards(tokens, in_weight, filter_taps, skip_gain, out_weight):
    devices = lax.axis_size("ctx")
    position = tokens.shape[0]
    partial_value = jnp.dot(tokens, in_weight, preferred_element_type=jnp.float32)
    projected = lax.psum_scatter(partial_value, "ch", scatter_dimension=1, tiled=True)
    channels = projected.shape[1]
    convolved = four_step(projected, filter_taps, devices, position, channels)
    mixed_in = (convolved + skip_gain[None, :] * projected).astype(jnp.bfloat16)
    out_terms = jnp.dot(mixed_in, out_weight, preferred_element_type=jnp.float32)
    result = lax.psum_scatter(out_terms, "ch", scatter_dimension=1, tiled=True)
    return result.astype(jnp.bfloat16)


def solution(mesh):
    return jax.shard_map(
        shards,
        mesh=mesh,
        in_specs=(P("ctx", "ch"), P("ch", None), P("ctx", "ch"), P("ch"), P("ch", None)),
        out_specs=P("ctx", "ch"),
        check_vma=False,
    )
```

profile of v0, /device:TPU:1, one launch (start us, length us, event | category | flops | bytes accessed | tf_op | source)
XLA Modules:
  0.0 848.9 jit_solution(5477460065351902264)
XLA Ops:
  6.5 10.5 %fusion.72 = f32[512,1024]{1,0:T(8,128)} fusion(bf16[512,4096]{1,0:T(8,128)(2,1)} %param.5, bf16[4096,1024]{1,0:T(8,128)(2,1)} %param.6), kind=kOutput, calls=%fused_computation.105 | convolution fusion | flops 4294967296 | bytes 14680064 | tf_op jit(solution)/shard_map/dot_general | solution.py:74
  17.1 39.3 %reduce-scatter.3.cloned.1.call-done = f32[512,512]{1,0:T(8,128)} async-done(((f32[512,1024]{1,0:T(8,128)}), f32[512,512]{1,0:T(8,128)}) %reduce-scatter.3.cloned.1.call-update) | async-done | bytes 1048592 | tf_op jit(solution)/shard_map/reduce_scatter | solution.py:75
  56.4 1.4 maximum_bitcast_fusion
  57.8 2.9 copy.52
  60.7 8.4 all-to-all-start
  69.1 0.1 sine_negate_fusion
  69.2 0.1 fusion.65
  69.4 28.1 %all-to-all-done = f32[2,1,512,512]{3,0,1,2:T(2,128)S(1)} async-done(((f32[2,1,512,512]{3,0,1,2:T(2,128)}), f32[2,1,512,512]{3,0,1,2:T(2,128)S(1)}, u32[]{:S(2)}, u32[]{:S(2)}) %all-to-all-start) | async-done | bytes 2097184 | tf_op jit(solution)/shard_map/all_to_all | solution.py:28
  97.5 7.3 convolution_bitcast_fusion
  104.8 1.2 add_bitcast_fusion
  106.0 3.8 pad_maximum_fusion
  109.8 10.4 %copy.55 = f32[2,2,128,8,512]{4,3,0,1,2:T(8,128)} copy(f32[2,2,128,8,512]{2,4,3,0,1:T(8,128)} %pad_maximum_fusion) | data formatting | bytes 16777216 | tf_op jit(solution)/shard_map/stack | solution.py:39
  120.2 5.9 all-to-all-start.1
  126.1 4.1 fusion.35
  130.2 104.2 %all-to-all-done.1 = f32[2,2,128,8,512]{4,3,0,1,2:T(8,128)} async-done(((f32[2,2,128,8,512]{4,3,0,1,2:T(8,128)}), f32[2,2,128,8,512]{4,3,0,1,2:T(8,128)}, u32[]{:S(2)}, u32[]{:S(2)}) %all-to-all-start.1) | async-done | bytes 8388640 | tf_op jit(solution)/shard_map/all_to_all | solution.py:40
  234.4 56.8 %fusion.3 = f32[2,2,2,2,512,512]{4,5,0,3,2,1:T(8,128)S(1)} fusion(f32[2,2,2,64,8,512]{5,4,0,1,2,3:T(8,128)} %bitcast.12, f32[1,512,512]{2,1,0:T(8,128)S(1)} %get-tuple-element.17, f32[1,512,512]{2,1,0:T(8,128)S(1)} %get-tuple-element.18), kind=kOutput, calls=%fused_computation.6 | convolution fusion | flops 25770328064 | bytes 27262976 | tf_op jit(solution)/shard_map/tkj,abqjc->tabqkc/dot_general | solution.py:43
  291.2 1.0 fusion.6
  292.3 1.0 fusion.8
  293.3 4.2 pad_maximum_fusion.1
  297.5 13.2 %copy.61 = f32[2,2,2,512,512]{4,2,0,1,3:T(2,128)} copy(f32[2,2,2,512,512]{3,4,2,0,1:T(8,128)} %pad_maximum_fusion.1) | data formatting | bytes 16777216 | tf_op jit(solution)/shard_map/stack | solution.py:46
  310.7 108.9 %all_to_all.90 = f32[2,2,2,512,512]{4,2,0,1,3:T(2,128)S(1)} all-to-all(f32[2,2,2,512,512]{4,2,0,1,3:T(2,128)} %copy.61), channel_id=1, replica_groups=mesh['ctx'=64,'ch'=2] {'ctx'}, dimensions={3} | all-to-all | bytes 16777216 | tf_op jit(solution)/shard_map/all_to_all | solution.py:47
  419.6 4.9 copy.108
  424.5 1.5 copy.63
  425.9 1.0 subtract_bitcast_fusion.1
  427.0 0.4 pad_maximum_fusion.2
  427.4 0.6 copy.64
  428.1 59.3 %all_to_all.91 = f32[2,128,8,512]{3,2,0,1:T(8,128)S(1)} all-to-all(f32[2,128,8,512]{3,2,0,1:T(8,128)S(1)} %copy.64), channel_id=1, replica_groups=mesh['ctx'=64,'ch'=2] {'ctx'}, dimensions={1} | all-to-all | bytes 8388608 | tf_op jit(solution)/shard_map/all_to_all | solution.py:51
  487.4 27.5 %fusion.16 = f32[2,2,2,512,512]{3,4,0,2,1:T(8,128)S(1)} fusion(f32[2,2,64,8,512]{4,3,0,1,2:T(8,128)S(1)} %bitcast.116, f32[1,512,512]{2,1,0:T(8,128)S(1)} %get-tuple-element.17, f32[1,512,512]{2,1,0:T(8,128)S(1)} %get-tuple-element.18), kind=kOutput, calls=%fused_computation.25 | convolution fusion | flops 12885426176 | bytes 14680064 | tf_op jit(solution)/shard_map/tjk,aqkc->taqjc/dot_general | solution.py:54
  514.8 0.5 fusion.19
  515.3 0.5 fusion.21
  515.8 2.5 pad_maximum_fusion.3
  518.3 7.3 copy.70
  525.6 8.5 %all-to-all-start.4 = ((f32[2,2,512,512]{3,1,0,2:T(2,128)}), f32[2,2,512,512]{3,1,0,2:T(2,128)}, u32[]{:S(2)}, u32[]{:S(2)}) async-start(f32[2,2,512,512]{3,1,0,2:T(2,128)} %copy.70), calls=%async_computation.5 | async-start | bytes 8388608 | tf_op jit(solution)/shard_map/all_to_all | solution.py:57
  534.2 0.1 sine_negate_fusion.1
  534.3 52.5 %all-to-all-done.4 = f32[2,2,512,512]{3,1,0,2:T(2,128)} async-done(((f32[2,2,512,512]{3,1,0,2:T(2,128)}), f32[2,2,512,512]{3,1,0,2:T(2,128)}, u32[]{:S(2)}, u32[]{:S(2)}) %all-to-all-start.4) | async-done | bytes 4194336 | tf_op jit(solution)/shard_map/all_to_all | solution.py:57
  586.8 3.5 copy.109
  590.4 2.0 fusion.71
  592.4 3.0 copy.72
  595.3 2.7 squeeze.4
  598.0 4.5 copy.73
  602.6 3.6 squeeze.5
  606.2 2.3 multiply_subtract_fusion
  608.5 2.6 fusion.9
  611.2 0.6 copy.74
  611.8 25.6 %all_to_all.92 = f32[64,8,512]{2,1,0:T(8,128)S(1)} all-to-all(f32[64,8,512]{2,1,0:T(8,128)S(1)} %copy.74), channel_id=1, replica_groups=mesh['ctx'=64,'ch'=2] {'ctx'}, dimensions={0} | all-to-all | bytes 2097152 | tf_op jit(solution)/shard_map/all_to_all | solution.py:66
  637.4 8.1 fusion.32
  645.5 190.3 %reduce-scatter.5.cloned.1.call-done = f32[512,4096]{1,0:T(8,128)} async-done(((f32[512,8192]{1,0:T(8,128)}), f32[512,4096]{1,0:T(8,128)}) %reduce-scatter.5.cloned.1.call-update) | async-done | bytes 8388624 | tf_op jit(solution)/shard_map/reduce_scatter | solution.py:80
  835.8 6.0 convert_element_type.54
  (16 shorter events, 0.1 us)
Async XLA Ops:
  6.5 49.8 %copy-start.1 = (f32[512,512]{1,0:T(8,128)S(1)}, f32[512,512]{1,0:T(8,128)}, u32[]{:S(2)}) copy-start(f32[512,512]{1,0:T(8,128)} %param.7) | copy-start | bytes 3145732
  6.5 49.8 %reduce-scatter.3.cloned.1.call-start = ((), (), s32[]{:S(2)}) async-start(), calls=%async_computation.8 | async-start | bytes 3145728 | tf_op jit(solution)/shard_map/reduce_scatter | solution.py:75
  60.7 36.8 %all-to-all-start = ((f32[2,1,512,512]{3,0,1,2:T(2,128)}), f32[2,1,512,512]{3,0,1,2:T(2,128)S(1)}, u32[]{:S(2)}, u32[]{:S(2)}) async-start(f32[2,1,512,512]{3,0,1,2:T(2,128)} %copy.52), calls=%async_computation.1 | async-start | bytes 4194304 | tf_op jit(solution)/shard_map/all_to_all | solution.py:28
  120.2 114.2 %all-to-all-start.1 = ((f32[2,2,128,8,512]{4,3,0,1,2:T(8,128)}), f32[2,2,128,8,512]{4,3,0,1,2:T(8,128)}, u32[]{:S(2)}, u32[]{:S(2)}) async-start(f32[2,2,128,8,512]{4,3,0,1,2:T(8,128)} %copy.55), calls=%async_computation.2 | async-start | bytes 16777216 | tf_op jit(solution)/shard_map/all_to_all | solution.py:40
  525.6 61.3 %all-to-all-start.4 = ((f32[2,2,512,512]{3,1,0,2:T(2,128)}), f32[2,2,512,512]{3,1,0,2:T(2,128)}, u32[]{:S(2)}, u32[]{:S(2)}) async-start(f32[2,2,512,512]{3,1,0,2:T(2,128)} %copy.70), calls=%async_computation.5 | async-start | bytes 8388608 | tf_op jit(solution)/shard_map/all_to_all | solution.py:57
  534.1 301.7 %reduce-scatter.5.cloned.1.call-start = ((), (), s32[]{:S(2)}) async-start(), calls=%async_computation.9 | async-start | bytes 25165824 | tf_op jit(solution)/shard_map/reduce_scatter | solution.py:80
  606.2 31.2 %slice-start = ((s8[8388608]{0:T(1024)(128)(4,1)}), s8[4194304]{0:T(1024)(128)(4,1)S(1)}, s32[]{:S(2)}) async-start(s8[8388608]{0:T(1024)(128)(4,1)} %bitcast.114), calls=%async_computation.10 | async-start | bytes 8388608
  608.5 28.9 %slice-start.1 = ((s8[8388608]{0:T(1024)(128)(4,1)}), s8[4194304]{0:T(1024)(128)(4,1)S(1)}, s32[]{:S(2)}) async-start(s8[8388608]{0:T(1024)(128)(4,1)} %bitcast.114), calls=%async_computation.11 | async-start | bytes 8388608
  608.5 28.9 %copy-start = (f32[512,512]{1,0:T(8,128)S(1)}, f32[512,512]{1,0:T(8,128)}, u32[]{:S(2)}) copy-start(f32[512,512]{1,0:T(8,128)} %reduce-scatter.3.cloned.1.call-done) | copy-start | bytes 3145732
  608.5 28.9 %copy-start.2 = (f32[512]{0:T(512)S(1)}, f32[512]{0:T(512)}, u32[]{:S(2)}) copy-start(f32[512]{0:T(512)} %param.8) | copy-start | bytes 6148
Sparse Core Ops, SparseCore 0:
  17.2 39.0 reduce-scatter.2
  645.7 190.1 reduce-scatter.4
where the time goes:
time: 855 us; the launch traced here: 849 us
  waiting for transfers between devices  414 us (48%)
  blocking collectives  194 us (23%)
  matrix products  113 us (13%)
  local copies, waits for them, and re-layouts  60.8 us (7%)
  other arithmetic  30.4 us (4%)
  starting transfers between devices  22.9 us (3%)
  between operations  13.8 us (2%)
    reduce_scatter x1, waiting for transfers between devices, shards(): result = lax.psum_scatter(out_terms, 'ch', scatter_dimension=1, tiled=True)  190 us
    all_to_all x1, blocking collectives, four_step(): lax.all_to_all(spectra, 'ctx', split_axis=3, concat_axis=2, tiled=True)  109 us
    all_to_all x1, waiting for transfers between devices, four_step(): lax.all_to_all(spread, 'ctx', split_axis=2, concat_axis=3, tiled=True)  104 us
    all_to_all x1, blocking collectives, four_step(): lax.all_to_all(jnp.stack([prod_real, prod_imag]), 'ctx', split_axis=1, co...  59.3 us
    dot_general x1, matrix products, four_step(): jnp.einsum('tkj,abqjc->tabqkc', line_table, gathered, precision=highest)  56.8 us
    all_to_all x1, waiting for transfers between devices, four_step(): lax.all_to_all(jnp.stack([back_real, back_imag]), 'ctx', split_axis=2, co...  52.5 us
    reduce_scatter x1, waiting for transfers between devices, shards(): lax.psum_scatter(partial_value, 'ch', scatter_dimension=1, tiled=True)  39.3 us
    all_to_all x1, waiting for transfers between devices, four_step(): lax.all_to_all(stacked, 'ctx', split_axis=2, concat_axis=1, tiled=True)  28.1 us
  transfers between devices with their start and end apart: 5, of which 5 were waited for; matrix products, arithmetic and copies ran while one was open for 1% of the time, Pallas kernels for 0%

commit v1 on v0

v1 whole, which is shorter than its diff:
```python
import numpy as np
import ml_dtypes
import jax
import jax.numpy as jnp
from jax import lax
from jax.experimental import pallas as pl
from jax.experimental.pallas import tpu as pltpu
from jax.sharding import PartitionSpec as P

bf16 = jnp.bfloat16
f32 = jnp.float32
LINES = 72
MIB = 1024 * 1024


def split_table(table):
    high = table.astype(ml_dtypes.bfloat16)
    low = (table - high.astype(np.float64)).astype(ml_dtypes.bfloat16)
    return high, low


def tables(blocks, width):
    period = 2 * blocks * width
    half = width // 2
    freq = np.arange(LINES)[:, None]
    live = (freq <= blocks).astype(np.float64)
    angle = 2.0 * np.pi * (freq * np.arange(blocks)[None, :] % (2 * blocks)) / (2 * blocks)
    lead = np.concatenate([np.cos(angle) * live, -np.sin(angle) * live], axis=0)
    lead_high, lead_low = split_table(lead)
    lead_signal = np.concatenate([lead_high, lead_high, lead_low], axis=1)
    lead_taps = np.concatenate([lead_high, lead_low], axis=1)
    weight = np.where((freq == 0) | (freq == blocks), 1.0, 2.0) * live / period
    tail = np.concatenate([np.cos(angle) * weight, -np.sin(angle) * weight], axis=0).T
    tail_high, tail_low = split_table(tail)
    rows = 6 * LINES
    tail3 = np.concatenate(
        [tail_high, tail_high, tail_low, np.zeros((blocks, -rows % 256), ml_dtypes.bfloat16)], axis=1
    )
    turn = 2.0 * np.pi * freq * np.arange(width)[None, :] / period
    twist = np.stack([np.cos(turn), np.sin(turn)]).astype(np.float32)
    fold = 2.0 * np.pi * np.arange(half) / width
    fold = np.stack([np.cos(fold), np.sin(fold)]).astype(np.float32)
    index = np.arange(half)
    line = 2.0 * np.pi * (index[:, None] * index[None, :] % half) / half
    cos, sin = np.cos(line), np.sin(line)
    forward = np.block([[cos, -sin], [sin, cos]])
    forward_high, forward_low = split_table(forward)
    return dict(
        lead_signal=lead_signal,
        lead_taps=lead_taps,
        tail=tail3,
        twist=twist,
        fold=fold,
        forward=np.stack([forward_high, forward_low]),
        backward=np.stack([forward_high.T, forward_low.T]),
    )


def dot(a, b):
    return jnp.dot(a, b, preferred_element_type=f32)


def split(a):
    high = a.astype(bf16)
    return high, (a - high.astype(f32)).astype(bf16)


def three_products(a, table_ref):
    high, low = split(a)
    first = table_ref[0]
    return dot(high, first) + dot(low, first) + dot(high, table_ref[1])


def spread(lines, twist_ref, fold_ref):
    half = lines.shape[1] // 2
    real, imag = lines[:LINES], lines[LINES:]
    cos, sin = twist_ref[0], twist_ref[1]
    turned_real = real * cos + imag * sin
    turned_imag = imag * cos - real * sin
    even_real = turned_real[:, :half] + turned_real[:, half:]
    even_imag = turned_imag[:, :half] + turned_imag[:, half:]
    diff_real = turned_real[:, :half] - turned_real[:, half:]
    diff_imag = turned_imag[:, :half] - turned_imag[:, half:]
    fold_cos, fold_sin = fold_ref[0:1], fold_ref[1:2]
    odd_real = diff_real * fold_cos + diff_imag * fold_sin
    odd_imag = diff_imag * fold_cos - diff_real * fold_sin
    return jnp.concatenate(
        [
            jnp.concatenate([even_real, even_imag], axis=1),
            jnp.concatenate([odd_real, odd_imag], axis=1),
        ],
        axis=0,
    )


def gather_back(rows, twist_ref, fold_ref):
    half = rows.shape[1] // 2
    even_real, even_imag = rows[:LINES, :half], rows[:LINES, half:]
    odd_real, odd_imag = rows[LINES:, :half], rows[LINES:, half:]
    fold_cos, fold_sin = fold_ref[0:1], fold_ref[1:2]
    rest_real = odd_real * fold_cos - odd_imag * fold_sin
    rest_imag = odd_imag * fold_cos + odd_real * fold_sin
    real = jnp.concatenate([even_real + rest_real, even_real - rest_real], axis=1)
    imag = jnp.concatenate([even_imag + rest_imag, even_imag - rest_imag], axis=1)
    cos, sin = twist_ref[0], twist_ref[1]
    return jnp.concatenate([real * cos - imag * sin, imag * cos + real * sin], axis=0)


def fill(flat, planes):
    blocks, channels, width = planes.shape
    rows = planes.reshape(blocks * channels, width)
    for q in range(width // 128):
        flat[q] = rows[:, 128 * q : 128 * (q + 1)]


def channel_of(flat, channel, blocks, channels):
    place = pl.ds(channel, blocks, stride=channels)
    return jnp.concatenate([flat[q, place, :] for q in range(flat.shape[0])], axis=1)


def taps_kernel(taps_ref, lead_ref, twist_ref, fold_ref, forward_ref, spec_ref, flat):
    blocks, channels, width = taps_ref.shape
    fill(flat, taps_ref[...].astype(f32))

    def body(pair, carry):
        rows = []
        for k in range(2):
            plane = channel_of(flat, 2 * pair + k, blocks, channels).astype(bf16)
            lines = dot(lead_ref[...], jnp.concatenate([plane, plane], axis=0))
            rows.append(spread(lines, twist_ref, fold_ref))
        spec_ref[pair] = three_products(jnp.concatenate(rows, axis=0), forward_ref)
        return carry

    lax.fori_loop(0, channels // 2, body, 0)


def conv_kernel(
    gain_ref, parts_ref, spec_ref, lead_ref, tail_ref, twist_ref, fold_ref, forward_ref, backward_ref,
    out_ref, flat, mixed,
):
    _, blocks, channels, width = parts_ref.shape
    half = width // 2
    fill(flat, parts_ref[0].astype(f32) + parts_ref[1].astype(f32))
    spare = tail_ref.shape[1] - 6 * LINES

    def body(pair, carry):
        rows = []
        for k in range(2):
            high, low = split(channel_of(flat, 2 * pair + k, blocks, channels))
            lines = dot(lead_ref[...], jnp.concatenate([high, low, high], axis=0))
            rows.append(spread(lines, twist_ref, fold_ref))
        signal = three_products(jnp.concatenate(rows, axis=0), forward_ref)
        taps = spec_ref[pair]
        real, imag = signal[:, :half], signal[:, half:]
        taps_real, taps_imag = taps[:, :half], taps[:, half:]
        product = jnp.concatenate(
            [real * taps_real - imag * taps_imag, real * taps_imag + imag * taps_real], axis=1
        )
        back = three_products(product, backward_ref)
        for k in range(2):
            lines = gather_back(back[2 * LINES * k : 2 * LINES * (k + 1)], twist_ref, fold_ref)
            high, low = split(lines)
            pad = jnp.zeros((spare, width), bf16)
            value = dot(tail_ref[...], jnp.concatenate([high, low, high, pad], axis=0))
            place = pl.ds(2 * pair + k, blocks, stride=channels)
            gain = gain_ref[2 * pair + k]
            for q in range(width // 128):
                part = value[:, 128 * q : 128 * (q + 1)]
                mixed[q, place, :] = part + gain * flat[q, place, :]
        return carry

    lax.fori_loop(0, channels // 2, body, 0)
    for q in range(width // 128):
        result = mixed[q].astype(bf16).reshape(blocks, channels, 128)
        for copy in range(out_ref.shape[0]):
            out_ref[copy, :, :, 128 * q : 128 * (q + 1)] = result


def project_kernel(tokens_ref, weight_ref, out_ref):
    out_ref[...] = dot(tokens_ref[...], weight_ref[...]).T.astype(bf16)


def out_kernel(place_ref, mixed_ref, own_ref, near_ref, far_ref, out_ref, turned):
    group, core = place_ref[0], place_ref[1]
    rows = own_ref.shape[0]
    part = near_ref.shape[0]

    @pl.when(pl.program_id(0) == 0)
    def _():
        other = (1 - group) * rows
        starts = [group * rows, other + core * part, other + (1 - core) * part]
        at = 0
        for start, size in zip(starts, [rows, part, part]):
            piece = mixed_ref[pl.ds(pl.multiple_of(start, part), size), :]
            turned[:, at : at + size] = piece.T
            at += size

    value = dot(turned[:, :rows], own_ref[...])
    value += dot(turned[:, rows : rows + part], near_ref[...])
    value += dot(turned[:, rows + part :], far_ref[...])
    out_ref[...] = value.astype(bf16)


def vmem(limit):
    return pltpu.CompilerParams(vmem_limit_bytes=limit * MIB)


def whole():
    return pl.BlockSpec(memory_space=pltpu.VMEM)


def permutes(x_size, z_size):
    def place(y, x, z, core):
        return (((y % 2 * x_size + x) * z_size + z) * 2 + core) * 2 + y // 2

    across, cores = [], []
    for y in range(4):
        for x in range(x_size):
            for z in range(z_size):
                for core in range(2):
                    across.append((place(y, x, z, core), place(3 - y, x, z, core)))
                    cores.append((place(y, x, z, core), place(y, x, z, 1 - core)))
    return across, cores


def shards(tokens, in_weight, filter_taps, skip_gain, out_weight):
    ctx, ch = lax.axis_size("ctx"), lax.axis_size("ch")
    devices = ctx * ch
    position, features = tokens.shape
    width = in_weight.shape[1]
    channels = width // devices
    here, group = lax.axis_index("ctx"), lax.axis_index("ch")
    core = here % 2
    table = {k: jnp.asarray(v) for k, v in tables(ctx, position).items()}

    rows = out_weight.shape[0]
    across, cores = permutes(4, 4)
    wanted = lax.dynamic_slice(
        out_weight, (core * (rows // 2), (1 - group) * features), (rows // 2, features)
    )
    near = lax.ppermute(wanted, ("ctx", "ch"), across)
    far = lax.ppermute(near, ("ctx", "ch"), cores)

    taps = filter_taps.T.astype(bf16).reshape(ctx, channels, position)
    taps = lax.all_to_all(taps, "ctx", split_axis=0, concat_axis=0, tiled=True)

    block = 256
    partial_value = pl.pallas_call(
        project_kernel,
        grid=(width // block,),
        in_specs=[
            pl.BlockSpec((position, features), lambda i: (0, 0)),
            pl.BlockSpec((features, block), lambda i: (0, i)),
        ],
        out_specs=pl.BlockSpec((block, position), lambda i: (i, 0)),
        out_shape=jax.ShapeDtypeStruct((width, position), bf16),
        compiler_params=vmem(40),
        cost_estimate=pl.CostEstimate(
            flops=2 * position * features * width, bytes_accessed=13 * MIB, transcendentals=0
        ),
    )(tokens, in_weight)

    line_rows = 4 * LINES
    lanes = (position // 128, ctx * channels, 128)
    spec = pl.pallas_call(
        taps_kernel,
        in_specs=[whole()] * 5,
        out_specs=whole(),
        out_shape=jax.ShapeDtypeStruct((channels // 2, line_rows, position), f32),
        scratch_shapes=[pltpu.VMEM(lanes, f32)],
        compiler_params=vmem(40),
        cost_estimate=pl.CostEstimate(flops=4 * 10**9, bytes_accessed=4 * MIB, transcendentals=0),
    )(taps, table["lead_taps"], table["twist"], table["fold"], table["forward"])

    parts = lax.all_to_all(
        partial_value.reshape(devices, channels, position),
        ("ch", "ctx"), split_axis=0, concat_axis=0, tiled=True,
    ).reshape(ch, ctx, channels, position)

    gain = lax.dynamic_slice(skip_gain, (here * channels,), (channels,))
    mixed = pl.pallas_call(
        conv_kernel,
        in_specs=[pl.BlockSpec(memory_space=pltpu.SMEM)] + [whole()] * 8,
        out_specs=whole(),
        out_shape=jax.ShapeDtypeStruct((ch, ctx, channels, position), bf16),
        scratch_shapes=[pltpu.VMEM(lanes, f32)] * 2,
        compiler_params=vmem(40),
        cost_estimate=pl.CostEstimate(flops=8 * 10**9, bytes_accessed=8 * MIB, transcendentals=0),
    )(
        gain, parts, spec, table["lead_signal"], table["tail"], table["twist"], table["fold"],
        table["forward"], table["backward"],
    )

    mixed = lax.all_to_all(
        mixed.reshape(devices, channels, position),
        ("ch", "ctx"), split_axis=0, concat_axis=0, tiled=True,
    ).reshape(width, position)

    step = 512
    steps = features // step
    return pl.pallas_call(
        out_kernel,
        grid_spec=pltpu.PrefetchScalarGridSpec(
            num_scalar_prefetch=1,
            grid=(steps,),
            in_specs=[
                pl.BlockSpec((width, position), lambda i, place: (0, 0)),
                pl.BlockSpec((rows, step), lambda i, place: (0, place[0] * steps + i)),
                pl.BlockSpec((rows // 2, step), lambda i, place: (0, i)),
                pl.BlockSpec((rows // 2, step), lambda i, place: (0, i)),
            ],
            out_specs=pl.BlockSpec((position, step), lambda i, place: (0, i)),
            scratch_shapes=[pltpu.VMEM((position, width), bf16)],
        ),
        out_shape=jax.ShapeDtypeStruct((position, features), bf16),
        compiler_params=vmem(40),
        cost_estimate=pl.CostEstimate(
            flops=2 * position * features * width, bytes_accessed=13 * MIB, transcendentals=0
        ),
    )(jnp.stack([group, core]).astype(jnp.int32), mixed, out_weight, near, far)


def solution(mesh):
    return jax.shard_map(
        shards,
        mesh=mesh,
        in_specs=(P("ctx", "ch"), P("ch", None), P("ctx", "ch"), P("ch"), P("ch", None)),
        out_specs=P("ctx", "ch"),
        check_vma=False,
    )
```

time: 855 us -> 130 us (0.15)
  waiting for transfers between devices: 414 us -> 41.4 us
  blocking collectives: 194 us -> 0 us
  matrix products: 113 us -> 0 us
  local copies, waits for them, and re-layouts: 60.8 us -> 26.7 us
  other arithmetic: 30.4 us -> 0.14 us
  Pallas kernels: 0 us -> 27.9 us
  between operations: 13.8 us -> 0.11 us
  starting transfers between devices: 22.9 us -> 32.7 us
    reduce_scatter x2 -> x0, waiting for transfers between devices: 230 us -> none  [the longest x1 190 us: shards(): result = lax.psum_scatter(out_terms, 'ch', scatter_dimension=1, tiled=True)]
    all_to_all x3 -> x0, blocking collectives: 194 us -> none  [the longest x1 109 us: four_step(): lax.all_to_all(spectra, 'ctx', split_axis=3, concat_axis=2, tiled=True)]
    all_to_all x3, waiting for transfers between devices: 185 us -> 19.1 us  [the longest x1 19.1 us: shards(): lax.all_to_all(mixed.reshape(devices, channels, position), ('ch', 'ctx'),...]
    dot_general x6 -> x0, matrix products: 113 us -> none  [the longest x1 56.8 us: four_step(): jnp.einsum('tkj,abqjc->tabqkc', line_table, gathered, precision=highest)]
    another operation x4 -> x0, local copies, waits for them, and re-layouts: 31.6 us -> none  [the longest x1 13.2 us: four_step(): spectra = jnp.stack([spec_real, spec_imag], axis=1)]
    pallas_call x0 -> x4, Pallas kernels: none -> 27.9 us  [the longest x1 9.86 us: shards(): pl.pallas_call(out_kernel, grid_spec=pltpu.PrefetchScalarGridSpec(num_sca...]
    ppermute x0 -> x2, waiting for transfers between devices: none -> 22.3 us  [the longest x1 22.3 us: shards(): near = lax.ppermute(wanted, ('ctx', 'ch'), across)]
    unnamed x10 -> x38, local copies, waits for them, and re-layouts: 0.03 us -> 21.7 us
  transfers between devices with their start and end apart: 5 -> 5, of which waited for: 5 -> 2; matrix products, arithmetic and copies ran while one was open for 1% -> 1% of each run, Pallas kernels for 0% -> 14%
where the time goes in v1:
time: 130 us; the launch traced here: 129 us
  waiting for transfers between devices  41.4 us (32%)
  starting transfers between devices  32.7 us (25%)
  Pallas kernels  27.9 us (21%)
  local copies, waits for them, and re-layouts  26.7 us (21%)
    ppermute x1, waiting for transfers between devices, shards(): near = lax.ppermute(wanted, ('ctx', 'ch'), across)  22.3 us
    unnamed x38, local copies, waits for them, and re-layouts  21.7 us
    all_to_all x1, waiting for transfers between devices, shards(): lax.all_to_all(mixed.reshape(devices, channels, position), ('ch', 'ctx'),...  19.1 us
    pallas_call x1, Pallas kernels, shards(): pl.pallas_call(out_kernel, grid_spec=pltpu.PrefetchScalarGridSpec(num_sca...  9.86 us
    all_to_all x1, starting transfers between devices, shards(): lax.all_to_all(mixed.reshape(devices, channels, position), ('ch', 'ctx'),...  9.85 us
    all_to_all x1, starting transfers between devices, shards(): taps = lax.all_to_all(taps, 'ctx', split_axis=0, concat_axis=0, tiled=True)  9.28 us
    pallas_call x1, Pallas kernels, shards(): pl.pallas_call(conv_kernel, in_specs=[pl.BlockSpec(memory_space=pltpu.SME...  7.99 us
    all_to_all x1, starting transfers between devices, shards(): lax.all_to_all(partial_value.reshape(devices, channels, position), ('ch',...  7.93 us
  transfers between devices with their start and end apart: 5, of which 2 were waited for; matrix products, arithmetic and copies ran while one was open for 1% of the time, Pallas kernels for 14%

profile of v1, /device:TPU:1, one launch (start us, length us, event | category | flops | bytes accessed | tf_op | source)
XLA Modules:
  0.0 129.0 jit_solution(80926029380694744)
XLA Ops:
  0.0 3.2 %dynamic_slice.7 = bf16[256,4096]{1,0:T(8,128)(2,1)} dynamic-slice(bf16[512,8192]{1,0:T(8,128)(2,1)} %own_ref.1, s32[]{:T(128)S(6)} %select_n.18, s32[]{:T(128)S(6)} %select_n.19), dynamic_slice_sizes={256,4096} | dynamic-slice | bytes 4194308 | tf_op jit(solution)/shard_map/dynamic_slice | solution.py:238
  3.2 3.6 %collective-permute-start = (bf16[256,4096]{1,0:T(8,128)(2,1)}, bf16[256,4096]{1,0:T(8,128)(2,1)S(1)}, u32[]{:S(2)}, u32[]{:S(2)}) collective-permute-start(bf16[256,4096]{1,0:T(8,128)(2,1)} %dynamic_slice.7), channel_id=1, source_target_pairs={{0,65},{2,67},{4,69},{6,71},{8,73},{10,75},{12,77},{14,79},{16,81}... | collective-permute-start | bytes 6291464 | tf_op jit(solution)/shard_map/ppermute | solution.py:241
  6.8 0.0 copy-done.18
  6.8 0.1 convert_bitcast_fusion
  6.9 1.0 copy.13
  7.9 9.3 %all-to-all-start.1 = ((bf16[64,8,512]{2,1,0:T(8,128)(2,1)}), bf16[64,8,512]{2,1,0:T(8,128)(2,1)S(1)}, u32[]{:S(2)}, u32[]{:S(2)}) async-start(bf16[64,8,512]{2,1,0:T(8,128)(2,1)} %bitcast.5), calls=%async_computation.1 | async-start | bytes 1048576 | tf_op jit(solution)/shard_map/all_to_all | solution.py:245
  17.2 0.0 copy-start.5
  17.2 3.4 %copy-done.5 = bf16[4096,1024]{1,0:T(8,128)(2,1)S(1)} copy-done((bf16[4096,1024]{1,0:T(8,128)(2,1)S(1)}, bf16[4096,1024]{1,0:T(8,128)(2,1)}, u32[]{:S(2)}) %copy-start.5) | copy-done | bytes 8388632
  20.5 0.0 copy-start.6
  20.5 2.2 %copy-done.6 = bf16[512,4096]{1,0:T(8,128)(2,1)S(1)} copy-done((bf16[512,4096]{1,0:T(8,128)(2,1)S(1)}, bf16[512,4096]{1,0:T(8,128)(2,1)}, u32[]{:S(2)}) %copy-start.6) | copy-done | bytes 4194328
  22.7 0.0 copy-start.10
  22.7 0.0 copy-start.13
  22.7 6.4 %shard_map.118 = bf16[1024,512]{1,0:T(8,128)(2,1)S(1)} custom-call(bf16[512,4096]{1,0:T(8,128)(2,1)S(1)} %copy-done.6, bf16[4096,1024]{1,0:T(8,128)(2,1)S(1)} %copy-done.5), custom_call_target="tpu_custom_call" | custom-call | flops 4294967296 | bytes 13631488 | tf_op jit(solution)/shard_map/pallas_call | solution.py:248
  29.2 0.0 copy-start.1
  29.2 1.0 copy-done.1
  30.2 0.0 all-to-all-done.1.taps_ref
  30.2 0.0 copy-start.3
  30.2 0.8 copy-done.3
  31.0 7.9 %all-to-all-start = ((bf16[128,8,512]{2,1,0:T(8,128)(2,1)}), bf16[128,8,512]{2,1,0:T(8,128)(2,1)S(1)}, u32[]{:S(2)}, u32[]{:S(2)}) async-start(bf16[128,8,512]{2,1,0:T(8,128)(2,1)} %bitcast.11), calls=%async_computation | async-start | bytes 2097152 | tf_op jit(solution)/shard_map/all_to_all | solution.py:275
  38.9 0.8 dynamic_slice.6.gain_ref
  39.7 22.3 %collective-permute-done.near_ref = bf16[256,4096]{1,0:T(8,128)(2,1)S(1)} collective-permute-done((bf16[256,4096]{1,0:T(8,128)(2,1)}, bf16[256,4096]{1,0:T(8,128)(2,1)S(1)}, u32[]{:S(2)}, u32[]{:S(2)}) %collective-permute-start) | collective-permute-done | bytes 2097184 | tf_op jit(solution)/shard_map/ppermute | solution.py:241
  62.0 2.1 %collective-permute-start.1 = (bf16[256,4096]{1,0:T(8,128)(2,1)S(1)}, bf16[256,4096]{1,0:T(8,128)(2,1)}, u32[]{:S(2)}, u32[]{:S(2)}) collective-permute-start(bf16[256,4096]{1,0:T(8,128)(2,1)S(1)} %collective-permute-done.near_ref), channel_id=1, source_target_pairs={{0,2},{2,0},{4,6},{6,4},{8,10},{10,8},{12,14},{14,12},{16,18},{18,... | collective-permute-start | bytes 6291464 | tf_op jit(solution)/shard_map/ppermute | solution.py:242
  64.1 0.0 copy-done.10
  64.1 0.0 copy-done.13
  64.1 0.0 copy-start.4
  64.1 1.0 copy-done.4
  65.2 0.0 copy-start.7
  65.2 1.2 copy-done.7
  66.4 0.7 copy-done.14
  67.1 3.6 %shard_map.119.spec_ref = f32[4,288,512]{2,1,0:T(8,128)S(1)} custom-call(bf16[64,8,512]{2,1,0:T(8,128)(2,1)S(1)} %copy-done.4, bf16[144,128]{1,0:T(8,128)(2,1)S(1)} %copy-done.13, f32[2,72,512]{2,1,0:T(8,128)S(1)} %copy-done.10, f32[2,256]{1,0:T(2,128)S(1)} %copy-done.14, bf16[2,512,512]{2,1,0:T(8,128)(2,1)S(1)} %copy-done.7), custom_call_target="tpu_custom_call" | custom-call | flops 4000000000 | bytes 4194304 | tf_op jit(solution)/shard_map/pallas_call | solution.py:265
  70.7 0.0 copy-start.16
  70.7 1.4 %copy-done.16 = f32[4,288,512]{2,1,0:T(8,128)} copy-done((f32[4,288,512]{2,1,0:T(8,128)}, f32[4,288,512]{2,1,0:T(8,128)S(1)}, u32[]{:S(2)}) %copy-start.16) | copy-done | bytes 2359320
  72.1 0.0 all-to-all-done
  72.1 0.0 copy-done.11
  72.1 1.2 copy-done.8
  73.3 1.2 copy-done.9
  74.5 0.8 copy-done.12
  75.4 0.7 copy-done.15
  76.1 1.7 %copy-done.17 = f32[4,288,512]{2,1,0:T(8,128)S(1)} copy-done((f32[4,288,512]{2,1,0:T(8,128)S(1)}, f32[4,288,512]{2,1,0:T(8,128)}, u32[]{:S(2)}) %copy-start.17) | copy-done | bytes 2359320
  77.7 8.0 %shard_map.120 = bf16[2,64,8,512]{3,2,1,0:T(8,128)(2,1)S(1)} custom-call(f32[8]{0:T(128)S(1)} %dynamic_slice.6.gain_ref, bf16[2,64,8,512]{3,2,1,0:T(8,128)(2,1)S(1)} %bitcast.10, f32[4,288,512]{2,1,0:T(8,128)S(1)} %copy-done.17, bf16[144,192]{1,0:T(8,128)(2,1)S(1)} %copy-done.11, bf16[64,512]{1,0:T(8,128)(2,1)S(1)} %copy-done.12, ...), custom_call_target="tpu_custom_call" | custom-call | flops 8000000000 | bytes 8388608 | tf_op jit(solution)/shard_map/pallas_call | solution.py:281
  85.7 0.0 copy-start.2
  85.7 1.0 copy-done.2
  86.7 9.9 %all-to-all-start.2 = ((bf16[128,8,512]{2,1,0:T(8,128)(2,1)}), bf16[128,8,512]{2,1,0:T(8,128)(2,1)S(1)}, u32[]{:S(2)}, u32[]{:S(2)}) async-start(bf16[128,8,512]{2,1,0:T(8,128)(2,1)} %bitcast.12), calls=%async_computation.2 | async-start | bytes 2097152 | tf_op jit(solution)/shard_map/all_to_all | solution.py:294
  96.6 0.1 pad_add_fusion.place_ref
  96.6 19.1 %all-to-all-done.2 = bf16[128,8,512]{2,1,0:T(8,128)(2,1)S(1)} async-done(((bf16[128,8,512]{2,1,0:T(8,128)(2,1)}), bf16[128,8,512]{2,1,0:T(8,128)(2,1)S(1)}, u32[]{:S(2)}, u32[]{:S(2)}) %all-to-all-start.2) | async-done | bytes 1048608 | tf_op jit(solution)/shard_map/all_to_all | solution.py:294
  115.7 0.0 collective-permute-done.1.far_ref
  115.7 3.4 %copy-done = bf16[512,8192]{1,0:T(8,128)(2,1)S(1)} copy-done((bf16[512,8192]{1,0:T(8,128)(2,1)S(1)}, bf16[512,8192]{1,0:T(8,128)(2,1)}, u32[]{:S(2)}) %copy-start) | copy-done | bytes 8388632
  119.1 9.9 %shard_map.121 = bf16[512,4096]{1,0:T(8,128)(2,1)} custom-call(s32[2]{0:T(128)S(1)} %pad_add_fusion.place_ref, bf16[1024,512]{1,0:T(8,128)(2,1)S(1)} %bitcast.9, bf16[512,8192]{1,0:T(8,128)(2,1)S(1)} %copy-done, bf16[256,4096]{1,0:T(8,128)(2,1)S(1)} %collective-permute-done.near_ref, bf16[256,4096]{1,0:T(8,128)(2,1)} %collective-permute-done.1.far_ref), custom_call_target="tpu_custom_call" | custom-call | flops 4294967296 | bytes 13631488 | tf_op jit(solution)/shard_map/pallas_call | solution.py:301
  (9 shorter events, 0.0 us)
Async XLA Ops:
  0.0 6.8 %copy-start.18 = (f32[512,512]{1,0:T(8,128)S(1)}, f32[512,512]{1,0:T(8,128)}, u32[]{:S(2)}) copy-start(f32[512,512]{1,0:T(8,128)} %param.14) | copy-start | bytes 3145732
  3.2 58.8 %collective-permute-start = (bf16[256,4096]{1,0:T(8,128)(2,1)}, bf16[256,4096]{1,0:T(8,128)(2,1)S(1)}, u32[]{:S(2)}, u32[]{:S(2)}) collective-permute-start(bf16[256,4096]{1,0:T(8,128)(2,1)} %dynamic_slice.7), channel_id=1, source_target_pairs={{0,65},{2,67},{4,69},{6,71},{8,73},{10,75},{12,77},{14,79},{16,81}... | collective-permute-start | bytes 6291464 | tf_op jit(solution)/shard_map/ppermute | solution.py:241
  7.9 22.3 %all-to-all-start.1 = ((bf16[64,8,512]{2,1,0:T(8,128)(2,1)}), bf16[64,8,512]{2,1,0:T(8,128)(2,1)S(1)}, u32[]{:S(2)}, u32[]{:S(2)}) async-start(bf16[64,8,512]{2,1,0:T(8,128)(2,1)} %bitcast.5), calls=%async_computation.1 | async-start | bytes 1048576 | tf_op jit(solution)/shard_map/all_to_all | solution.py:245
  17.2 3.4 %copy-start.5 = (bf16[4096,1024]{1,0:T(8,128)(2,1)S(1)}, bf16[4096,1024]{1,0:T(8,128)(2,1)}, u32[]{:S(2)}) copy-start(bf16[4096,1024]{1,0:T(8,128)(2,1)} %weight_ref.1) | copy-start | bytes 25165828
  20.5 2.2 %copy-start.6 = (bf16[512,4096]{1,0:T(8,128)(2,1)S(1)}, bf16[512,4096]{1,0:T(8,128)(2,1)}, u32[]{:S(2)}) copy-start(bf16[512,4096]{1,0:T(8,128)(2,1)} %tokens_ref.1) | copy-start | bytes 12582916
  22.7 41.4 %copy-start.10 = (f32[2,72,512]{2,1,0:T(8,128)S(1)}, f32[2,72,512]{2,1,0:T(8,128)}, u32[]{:S(2)}) copy-start(f32[2,72,512]{2,1,0:T(8,128)} %constant.50.clone.twist_ref) | copy-start | bytes 884740
  22.7 41.4 %copy-start.13 = (bf16[144,128]{1,0:T(8,128)(2,1)S(1)}, bf16[144,128]{1,0:T(8,128)(2,1)}, u32[]{:S(2)}) copy-start(bf16[144,128]{1,0:T(8,128)(2,1)} %constant.48.clone.lead_ref) | copy-start | bytes 110596
  29.2 1.0 copy-start.1
  30.2 0.8 copy-start.3
  31.0 41.1 %all-to-all-start = ((bf16[128,8,512]{2,1,0:T(8,128)(2,1)}), bf16[128,8,512]{2,1,0:T(8,128)(2,1)S(1)}, u32[]{:S(2)}, u32[]{:S(2)}) async-start(bf16[128,8,512]{2,1,0:T(8,128)(2,1)} %bitcast.11), calls=%async_computation | async-start | bytes 2097152 | tf_op jit(solution)/shard_map/all_to_all | solution.py:275
  62.0 53.7 %collective-permute-start.1 = (bf16[256,4096]{1,0:T(8,128)(2,1)S(1)}, bf16[256,4096]{1,0:T(8,128)(2,1)}, u32[]{:S(2)}, u32[]{:S(2)}) collective-permute-start(bf16[256,4096]{1,0:T(8,128)(2,1)S(1)} %collective-permute-done.near_ref), channel_id=1, source_target_pairs={{0,2},{2,0},{4,6},{6,4},{8,10},{10,8},{12,14},{14,12},{16,18},{18,... | collective-permute-start | bytes 6291464 | tf_op jit(solution)/shard_map/ppermute | solution.py:242
  64.1 1.0 copy-start.4
  65.2 1.2 copy-start.7
  66.4 0.7 copy-start.14
  67.1 5.0 %copy-start.11 = (bf16[144,192]{1,0:T(8,128)(2,1)S(1)}, bf16[144,192]{1,0:T(8,128)(2,1)}, u32[]{:S(2)}) copy-start(bf16[144,192]{1,0:T(8,128)(2,1)} %constant.47.clone.lead_ref) | copy-start | bytes 165892
  70.7 1.4 %copy-start.16 = (f32[4,288,512]{2,1,0:T(8,128)}, f32[4,288,512]{2,1,0:T(8,128)S(1)}, u32[]{:S(2)}) copy-start(f32[4,288,512]{2,1,0:T(8,128)S(1)} %shard_map.119.spec_ref) | copy-start | bytes 7077892
  72.1 1.2 copy-start.8
  73.3 1.2 copy-start.9
  74.5 0.8 copy-start.12
  75.4 0.7 copy-start.15
  76.1 1.7 %copy-start.17 = (f32[4,288,512]{2,1,0:T(8,128)S(1)}, f32[4,288,512]{2,1,0:T(8,128)}, u32[]{:S(2)}) copy-start(f32[4,288,512]{2,1,0:T(8,128)} %copy-done.16) | copy-start | bytes 7077892
  85.7 1.0 copy-start.2
  86.7 29.0 %all-to-all-start.2 = ((bf16[128,8,512]{2,1,0:T(8,128)(2,1)}), bf16[128,8,512]{2,1,0:T(8,128)(2,1)S(1)}, u32[]{:S(2)}, u32[]{:S(2)}) async-start(bf16[128,8,512]{2,1,0:T(8,128)(2,1)} %bitcast.12), calls=%async_computation.2 | async-start | bytes 2097152 | tf_op jit(solution)/shard_map/all_to_all | solution.py:294
  115.7 3.4 %copy-start = (bf16[512,8192]{1,0:T(8,128)(2,1)S(1)}, bf16[512,8192]{1,0:T(8,128)(2,1)}, u32[]{:S(2)}) copy-start(bf16[512,8192]{1,0:T(8,128)(2,1)} %own_ref.1) | copy-start | bytes 25165828

commit v2 on v0

v2 whole, which is shorter than its diff:
```python
import numpy as np
import ml_dtypes
import jax
import jax.numpy as jnp
from jax import lax
from jax.experimental import pallas as pl
from jax.experimental.pallas import tpu as pltpu
from jax.sharding import PartitionSpec as P

bf16 = jnp.bfloat16
f32 = jnp.float32
MIB = 1024 * 1024
LINES = 72
GROUP = 4
CHUNK = 512
PIECES = 4


def split_table(table):
    high = table.astype(ml_dtypes.bfloat16)
    low = (table - high.astype(np.float64)).astype(ml_dtypes.bfloat16)
    return high, low


def tables(blocks, width):
    period = 2 * blocks * width
    quarter = width // 4
    freq = np.arange(LINES)[:, None]
    live = (freq <= blocks).astype(np.float64)
    angle = 2.0 * np.pi * (freq * np.arange(blocks)[None, :] % (2 * blocks)) / (2 * blocks)
    lead = np.concatenate([np.cos(angle) * live, -np.sin(angle) * live], axis=0)
    lead_high, lead_low = split_table(lead)
    weight = np.where((freq == 0) | (freq == blocks), 1.0, 2.0) * live / period
    tail = np.concatenate([np.cos(angle) * weight, np.sin(angle) * weight], axis=0).T
    tail_high, tail_low = split_table(tail)
    spare = np.zeros((blocks, -6 * LINES % 256), ml_dtypes.bfloat16)
    turn = 2.0 * np.pi * freq * np.arange(width)[None, :] / period
    fold = 2.0 * np.pi * np.arange(4)[:, None] * np.arange(quarter)[None, :] / width
    index = np.arange(quarter)
    line = 2.0 * np.pi * (index[:, None] * index[None, :] % quarter) / quarter
    cos, sin = np.cos(line), np.sin(line)
    line_high, line_low = split_table(np.block([[cos, -sin], [sin, cos]]))
    return dict(
        lead_signal=np.concatenate([lead_high, lead_high, lead_low], axis=1),
        lead_taps=np.concatenate([lead_high, lead_low], axis=1),
        tail=np.concatenate([tail_high, tail_high, tail_low, spare], axis=1),
        twist=np.stack([np.cos(turn), np.sin(turn)]).astype(np.float32),
        fold=np.concatenate([np.cos(fold), np.sin(fold)]).astype(np.float32),
        line=np.concatenate([line_high, line_high, line_low], axis=0),
    )


def dot(a, b):
    return jnp.dot(a, b, preferred_element_type=f32)


def split(a):
    high = a.astype(bf16)
    return high, (a - high.astype(f32)).astype(bf16)


def line_transform(rows, line_ref):
    high, low = split(rows)
    return dot(jnp.concatenate([high, low, high], axis=1), line_ref[...])


def turn_back(real, imag, cos, sin):
    return real * cos + imag * sin, imag * cos - real * sin


def butterfly(parts):
    (ar, ai), (br, bi), (cr, ci), (dr, di) = parts
    sr, si, er, ei = ar + cr, ai + ci, ar - cr, ai - ci
    tr, ti, fr, fi = br + dr, bi + di, br - dr, bi - di
    return [(sr + tr, si + ti), (er + fi, ei - fr), (sr - tr, si - ti), (er - fi, ei + fr)]


def spread(lines, twist_ref, fold_ref):
    quarter = lines.shape[1] // 4
    parts = []
    for p in range(4):
        at = slice(quarter * p, quarter * (p + 1))
        parts.append(
            turn_back(lines[:LINES, at], lines[LINES:, at], twist_ref[0, :, at], twist_ref[1, :, at])
        )
    rows = []
    for r, (real, imag) in enumerate(butterfly(parts)):
        if r:
            real, imag = turn_back(real, imag, fold_ref[r : r + 1], fold_ref[r + 4 : r + 5])
        rows.append(jnp.concatenate([real, imag], axis=1))
    return rows


def gather_back(rows, twist_ref, fold_ref):
    quarter = rows.shape[1] // 2
    got = []
    for r in range(4):
        at = slice(LINES * r, LINES * (r + 1))
        real, imag = rows[at, :quarter], rows[at, quarter:]
        if r:
            real, imag = turn_back(real, imag, fold_ref[r : r + 1], fold_ref[r + 4 : r + 5])
        got.append((real, imag))
    reals, imags = [], []
    for p, (real, imag) in enumerate(butterfly(got)):
        at = slice(quarter * p, quarter * (p + 1))
        real, imag = turn_back(real, imag, twist_ref[0, :, at], twist_ref[1, :, at])
        reals.append(real)
        imags.append(imag)
    return jnp.concatenate(
        [jnp.concatenate(reals, axis=1), jnp.concatenate(imags, axis=1)], axis=0
    )


def fill(flat, planes):
    blocks, channels, width = planes.shape
    rows = planes.reshape(blocks * channels, width)
    for q in range(width // 128):
        flat[q] = rows[:, 128 * q : 128 * (q + 1)]


def channel_of(flat, channel, blocks, channels):
    place = pl.ds(channel, blocks, stride=channels)
    return jnp.concatenate([flat[q, place, :] for q in range(flat.shape[0])], axis=1)


def where():
    here = lax.axis_index("ctx")
    return lax.axis_index("ch"), here & 1, (here >> 3 & 1) * 2 + (here >> 1 & 1)


def start_all(pairs, sems):
    copies = [pltpu.make_async_copy(a, b, sems.at[i]) for i, (a, b) in enumerate(pairs)]
    for copy in copies:
        copy.start()
    return copies


def spectrum_kernel(
    taps_ref, lead_hbm, twist_hbm, fold_hbm, line_hbm, spec_hbm,
    lead_ref, twist_ref, fold_ref, line_ref, flat, spec_ref, sems, out_sems,
):
    blocks, channels, width = taps_ref.shape
    copies = start_all(
        [(lead_hbm, lead_ref), (twist_hbm, twist_ref), (fold_hbm, fold_ref), (line_hbm, line_ref)],
        sems,
    )
    fill(flat, taps_ref[...].astype(f32))
    for copy in copies:
        copy.wait()
    stores = []
    for step in range(channels // GROUP):
        rows = []
        for c in range(GROUP * step, GROUP * (step + 1)):
            plane = channel_of(flat, c, blocks, channels).astype(bf16)
            lines = dot(lead_ref[...], jnp.concatenate([plane, plane], axis=0))
            rows += spread(lines, twist_ref, fold_ref)
        spec_ref[step] = line_transform(jnp.concatenate(rows, axis=0), line_ref)
        store = pltpu.make_async_copy(spec_ref.at[step], spec_hbm.at[step], out_sems.at[step])
        store.start()
        stores.append(store)
    for store in stores:
        store.wait()


def conv_kernel(
    gain_ref, parts_ref, spec_hbm, lead_hbm, tail_hbm, twist_hbm, fold_hbm, line_hbm,
    out_hbm,
    spec_ref, lead_ref, tail_ref, twist_ref, fold_ref, line_ref,
    flat, mixed, out_ref, sems, out_sems,
):
    _, blocks, channels, width = parts_ref.shape
    quarter = width // 4
    first_gain = lax.axis_index("ctx") * channels
    copies = start_all(
        [
            (lead_hbm, lead_ref), (twist_hbm, twist_ref), (fold_hbm, fold_ref),
            (line_hbm, line_ref), (spec_hbm, spec_ref), (tail_hbm, tail_ref),
        ],
        sems,
    )
    fill(flat, parts_ref[0].astype(f32) + parts_ref[1].astype(f32))
    for copy in copies[:4]:
        copy.wait()
    spare = tail_ref.shape[1] - 6 * LINES
    size = 4 * LINES

    for step in range(channels // GROUP):
        held = range(GROUP * step, GROUP * (step + 1))
        rows = []
        for c in held:
            high, low = split(channel_of(flat, c, blocks, channels))
            lines = dot(lead_ref[...], jnp.concatenate([high, low, high], axis=0))
            rows += spread(lines, twist_ref, fold_ref)
        spec = line_transform(jnp.concatenate(rows, axis=0), line_ref)
        if step == 0:
            for copy in copies[4:]:
                copy.wait()
        products = []
        for k, c in enumerate(held):
            at = slice(size * k, size * (k + 1))
            real, imag = spec[at, :quarter], spec[at, quarter:]
            taps_real = spec_ref[step, at, :quarter] + gain_ref[first_gain + c]
            taps_imag = spec_ref[step, at, quarter:]
            products.append(
                jnp.concatenate(
                    [real * taps_real - imag * taps_imag, -(real * taps_imag + imag * taps_real)],
                    axis=1,
                )
            )
        back = line_transform(jnp.concatenate(products, axis=0), line_ref)
        for k, c in enumerate(held):
            lines = gather_back(back[size * k : size * (k + 1)], twist_ref, fold_ref)
            high, low = split(lines)
            pad = jnp.zeros((spare, width), bf16)
            value = dot(tail_ref[...], jnp.concatenate([high, low, high, pad], axis=0))
            place = pl.ds(c, blocks, stride=channels)
            for q in range(width // 128):
                mixed[q, place, :] = value[:, 128 * q : 128 * (q + 1)]

    for q in range(width // 128):
        result = mixed[q].astype(bf16).reshape(blocks, channels, 128)
        out_ref[:, :, 128 * q : 128 * (q + 1)] = result
    for copy in start_all([(out_ref, out_hbm.at[k]) for k in range(out_hbm.shape[0])], out_sems):
        copy.wait()


def prepare_kernel(
    taps_hbm, weight_hbm, taps_out_hbm, first_hbm, last_hbm, taps_ref, taps_out_ref, pieces_ref, sems
):
    group, core, first = where()
    taps_load = pltpu.make_async_copy(taps_hbm, taps_ref, sems.at[0])
    taps_load.start()
    size, columns = first_hbm.shape
    at = pl.ds(pl.multiple_of((1 - group) * columns, columns), columns)
    loads, stores = [], []
    for i, (piece, which) in enumerate([(first_hbm, first), (last_hbm, first ^ 3)]):
        rows = pl.ds(pl.multiple_of((core * PIECES + which) * size, size), size)
        loads.append(pltpu.make_async_copy(weight_hbm.at[rows, at], pieces_ref.at[i], sems.at[2 + i]))
        stores.append(pltpu.make_async_copy(pieces_ref.at[i], piece, sems.at[4 + i]))
        loads[i].start()
    taps_load.wait()
    taps_out_ref[...] = taps_ref[...].astype(bf16).T
    stores.append(pltpu.make_async_copy(taps_out_ref, taps_out_hbm, sems.at[1]))
    stores[2].start()
    for i in range(2):
        loads[i].wait()
        stores[i].start()
    for store in stores:
        store.wait()


def fence_kernel(value_ref, after_ref, out_ref):
    pass


def project_kernel(
    tokens_hbm, weight_hbm, out_hbm, tokens_ref, weight_ref, total, out_ref,
    token_sems, weight_sems, out_sems,
):
    features = tokens_ref.shape[1]
    width = weight_ref.shape[1]
    steps = features // CHUNK
    parts = 4
    loads = []
    for i in range(steps):
        at = pl.ds(i * CHUNK, CHUNK)
        pair = (
            pltpu.make_async_copy(tokens_hbm.at[:, at], tokens_ref.at[:, at], token_sems.at[i]),
            pltpu.make_async_copy(weight_hbm.at[at], weight_ref.at[at], weight_sems.at[i]),
        )
        for copy in pair:
            copy.start()
        loads.append(pair)
    stores = []
    for i in range(steps):
        for copy in loads[i]:
            copy.wait()
        at = slice(i * CHUNK, (i + 1) * CHUNK)
        for c in range(parts):
            cols = slice(c * width // parts, (c + 1) * width // parts)
            term = dot(tokens_ref[:, at], weight_ref[at, cols])
            if i == 0:
                total[:, cols] = term
            elif i < steps - 1:
                total[:, cols] += term
            else:
                out_ref[cols, :] = (total[:, cols] + term).astype(bf16).T
                rows = pl.ds(c * width // parts, width // parts)
                store = pltpu.make_async_copy(out_ref.at[rows], out_hbm.at[rows], out_sems.at[c])
                store.start()
                stores.append(store)
    for store in stores:
        store.wait()


def weights_kernel(own_hbm, *rest):
    pieces, (out_hbm, held_ref, sems, out_sems) = rest[:-4], rest[-4:]
    rows = own_hbm.shape[0]
    blocks, _, columns = out_hbm.shape
    size = rows // len(pieces)
    group = where()[0]
    at = pl.ds(pl.multiple_of(group * (blocks * columns), columns), blocks * columns)
    pairs = [(own_hbm.at[:, at], held_ref.at[pl.ds(0, rows)])]
    for i, piece in enumerate(pieces):
        pairs.append((piece, held_ref.at[pl.ds(rows + i * size, size)]))
    for copy in start_all(pairs, sems):
        copy.wait()
    stores = start_all(
        [(held_ref.at[:, pl.ds(b * columns, columns)], out_hbm.at[b]) for b in range(blocks)],
        out_sems,
    )
    for copy in stores:
        copy.wait()


def out_kernel(mixed_ref, weight_hbm, out_hbm, turned, weight_ref, out_ref, sems, out_sems):
    steps, _, columns = weight_ref.shape
    loads = start_all([(weight_hbm.at[i], weight_ref.at[i]) for i in range(steps)], sems)
    group, core, first = where()
    width, position = mixed_ref.shape
    rows = width // 2
    size = rows // (2 * PIECES)
    own = mixed_ref[pl.ds(pl.multiple_of(group * rows, rows), rows), :]
    turned[:, :rows] = own.T
    pieces = []
    for half in (core, 1 - core):
        for flip in range(PIECES):
            start = (1 - group) * rows + half * (rows // 2) + (first ^ flip) * size
            pieces.append(mixed_ref[pl.ds(pl.multiple_of(start, size), size), :])
    turned[:, rows:] = jnp.concatenate(pieces, axis=0).T
    stores = []
    for i in range(steps):
        loads[i].wait()
        at = slice(i * columns, (i + 1) * columns)
        out_ref[:, at] = dot(turned[...], weight_ref[i]).astype(bf16)
        span = pl.ds(i * columns, columns)
        store = pltpu.make_async_copy(out_ref.at[:, span], out_hbm.at[:, span], out_sems.at[i])
        store.start()
        stores.append(store)
    for store in stores:
        store.wait()


def vmem(limit):
    return pltpu.CompilerParams(vmem_limit_bytes=limit * MIB)


def cost(flops, size):
    return pl.CostEstimate(flops=flops, bytes_accessed=size, transcendentals=0)


ANY = pl.BlockSpec(memory_space=pl.ANY)
SMEM = pl.BlockSpec(memory_space=pltpu.SMEM)
VMEM = pl.BlockSpec(memory_space=pltpu.VMEM)


def partners(move):
    def place(y, x, z, core):
        return (((y % 2 * 4 + x) * 4 + z) * 2 + core) * 2 + y // 2

    spots = [(y, x, z, c) for y in range(4) for x in range(4) for z in range(4) for c in range(2)]
    return [(place(*spot), place(*move(*spot))) for spot in spots]


def shards(tokens, in_weight, filter_taps, skip_gain, out_weight):
    ctx, ch = lax.axis_size("ctx"), lax.axis_size("ch")
    devices = ctx * ch
    position, features = tokens.shape
    width = in_weight.shape[1]
    channels = width // devices
    rows = out_weight.shape[0]
    table = {k: jnp.asarray(v) for k, v in tables(ctx, position).items()}

    across = partners(lambda y, x, z, c: (3 - y, x, z, c))
    along_x = partners(lambda y, x, z, c: (y, x ^ 1, z, c))
    along_z = partners(lambda y, x, z, c: (y, x, z ^ 1, c))
    other_core = partners(lambda y, x, z, c: (y, x, z, 1 - c))
    both = ("ctx", "ch")
    size = rows // (2 * PIECES)
    piece = jax.ShapeDtypeStruct((size, features), bf16)

    taps, first_piece, last_piece = pl.pallas_call(
        prepare_kernel,
        in_specs=[ANY, ANY],
        out_specs=[ANY] * 3,
        out_shape=[jax.ShapeDtypeStruct((width // ch, position), bf16), piece, piece],
        scratch_shapes=[
            pltpu.VMEM((position, width // ch), f32),
            pltpu.VMEM((width // ch, position), bf16),
            pltpu.VMEM((2, size, features), bf16),
            pltpu.SemaphoreType.DMA((6,)),
        ],
        compiler_params=vmem(60),
        cost_estimate=cost(0, 4 * MIB),
    )(filter_taps, out_weight)

    mine = lax.ppermute(first_piece, both, across)
    taps = lax.all_to_all(
        taps.reshape(ctx, channels, position), "ctx", split_axis=0, concat_axis=0, tiled=True
    )

    partial_value = pl.pallas_call(
        project_kernel,
        in_specs=[ANY] * 2,
        out_specs=ANY,
        out_shape=jax.ShapeDtypeStruct((width, position), bf16),
        scratch_shapes=[
            pltpu.VMEM((position, features), bf16),
            pltpu.VMEM((features, width), bf16),
            pltpu.VMEM((position, width), f32),
            pltpu.VMEM((width, position), bf16),
            pltpu.SemaphoreType.DMA((features // CHUNK,)),
            pltpu.SemaphoreType.DMA((features // CHUNK,)),
            pltpu.SemaphoreType.DMA((4,)),
        ],
        compiler_params=vmem(60),
        cost_estimate=cost(2 * position * features * width, 14 * MIB),
    )(tokens, in_weight)

    partial_value = pl.pallas_call(
        fence_kernel,
        in_specs=[ANY] * 2,
        out_specs=ANY,
        out_shape=jax.ShapeDtypeStruct((width, position), bf16),
        input_output_aliases={0: 0},
        compiler_params=vmem(60),
    )(partial_value, mine)

    parts = lax.all_to_all(
        partial_value.reshape(devices, channels, position),
        ("ch", "ctx"), split_axis=0, concat_axis=0, tiled=True,
    ).reshape(ch, ctx, channels, position)

    by_x = lax.ppermute(mine, both, along_x)
    by_z = lax.ppermute(mine, both, along_z)
    last = lax.ppermute(last_piece, both, across)
    pieces = [mine, by_z, by_x, last]
    pieces = pieces + [lax.ppermute(p, both, other_core) for p in pieces]

    lanes = (position // 128, ctx * channels, 128)
    spec_shape = (channels // GROUP, GROUP * 4 * LINES, position // 2)
    used = [table[k] for k in ("lead_taps", "twist", "fold", "line")]
    spec = pl.pallas_call(
        spectrum_kernel,
        in_specs=[VMEM] + [ANY] * 4,
        out_specs=ANY,
        out_shape=jax.ShapeDtypeStruct(spec_shape, f32),
        scratch_shapes=[
            *[pltpu.VMEM(t.shape, t.dtype) for t in used],
            pltpu.VMEM(lanes, f32),
            pltpu.VMEM(spec_shape, f32),
            pltpu.SemaphoreType.DMA((4,)),
            pltpu.SemaphoreType.DMA((channels // GROUP,)),
        ],
        compiler_params=vmem(58),
        cost_estimate=cost(4 * 10**9, 4 * MIB),
    )(taps, *used)

    used = [table[k] for k in ("lead_signal", "tail", "twist", "fold", "line")]
    mixed = pl.pallas_call(
        conv_kernel,
        in_specs=[SMEM, VMEM] + [ANY] * 6,
        out_specs=ANY,
        out_shape=jax.ShapeDtypeStruct((ch, ctx, channels, position), bf16),
        scratch_shapes=[
            pltpu.VMEM(spec_shape, f32),
            *[pltpu.VMEM(t.shape, t.dtype) for t in used],
            pltpu.VMEM(lanes, f32),
            pltpu.VMEM(lanes, f32),
            pltpu.VMEM((ctx, channels, position), bf16),
            pltpu.SemaphoreType.DMA((6,)),
            pltpu.SemaphoreType.DMA((ch,)),
        ],
        compiler_params=vmem(58),
        cost_estimate=cost(8 * 10**9, 6 * MIB),
    )(skip_gain, parts, spec, *used)

    mixed = lax.all_to_all(
        mixed.reshape(devices, channels, position),
        ("ch", "ctx"), split_axis=0, concat_axis=0, tiled=True,
    ).reshape(width, position)

    steps = features // 512
    weights = pl.pallas_call(
        weights_kernel,
        in_specs=[ANY] * (1 + 2 * PIECES),
        out_specs=ANY,
        out_shape=jax.ShapeDtypeStruct((steps, width, features // steps), bf16),
        scratch_shapes=[
            pltpu.VMEM((width, features), bf16),
            pltpu.SemaphoreType.DMA((1 + 2 * PIECES,)),
            pltpu.SemaphoreType.DMA((steps,)),
        ],
        compiler_params=vmem(60),
        cost_estimate=cost(0, 16 * MIB),
    )(out_weight, *pieces)

    return pl.pallas_call(
        out_kernel,
        in_specs=[VMEM, ANY],
        out_specs=ANY,
        out_shape=jax.ShapeDtypeStruct((position, features), bf16),
        scratch_shapes=[
            pltpu.VMEM((position, width), bf16),
            pltpu.VMEM((steps, width, features // steps), bf16),
            pltpu.VMEM((position, features), bf16),
            pltpu.SemaphoreType.DMA((steps,)),
            pltpu.SemaphoreType.DMA((steps,)),
        ],
        compiler_params=vmem(58),
        cost_estimate=cost(2 * position * features * width, 13 * MIB),
    )(mixed, weights)


def solution(mesh):
    return jax.shard_map(
        shards,
        mesh=mesh,
        in_specs=(P("ctx", "ch"), P("ch", None), P("ctx", "ch"), P("ch"), P("ch", None)),
        out_specs=P("ctx", "ch"),
        check_vma=False,
    )
```

time: 855 us -> 96 us (0.11)
  waiting for transfers between devices: 414 us -> 21.8 us
  blocking collectives: 194 us -> 0 us
  matrix products: 113 us -> 0 us
  local copies, waits for them, and re-layouts: 60.8 us -> 3.81 us
  Pallas kernels: 0 us -> 40.1 us
  other arithmetic: 30.4 us -> 0 us
  between operations: 13.8 us -> 0.29 us
    reduce_scatter x2 -> x0, waiting for transfers between devices: 230 us -> none  [the longest x1 190 us: shards(): result = lax.psum_scatter(out_terms, 'ch', scatter_dimension=1, tiled=True)]
    all_to_all x3 -> x0, blocking collectives: 194 us -> none  [the longest x1 109 us: four_step(): lax.all_to_all(spectra, 'ctx', split_axis=3, concat_axis=2, tiled=True)]
    all_to_all x3, waiting for transfers between devices: 185 us -> 18.7 us  [the longest x1 8.39 us: shards(): lax.all_to_all(partial_value.reshape(devices, channels, position), ('ch',...]
    dot_general x6 -> x0, matrix products: 113 us -> none  [the longest x1 56.8 us: four_step(): jnp.einsum('tkj,abqjc->tabqkc', line_table, gathered, precision=highest)]
    pallas_call x0 -> x7, Pallas kernels: none -> 40.1 us  [the longest x1 9.08 us: shards(): pl.pallas_call(out_kernel, in_specs=[VMEM, ANY], out_specs=ANY, out_shape...]
    another operation x4 -> x0, local copies, waits for them, and re-layouts: 31.6 us -> none  [the longest x1 13.2 us: four_step(): spectra = jnp.stack([spec_real, spec_imag], axis=1)]
    another operation x5 -> x0, other arithmetic: 12.1 us -> none  [the longest x2 5.01 us: four_step(): spread = jnp.stack([turned_real, turned_imag], axis=1)]
    ppermute x0 -> x8, starting transfers between devices: none -> 11 us  [the longest x1 3.64 us: shards(): mine = lax.ppermute(first_piece, both, across)]
  transfers between devices with their start and end apart: 5 -> 11, of which waited for: 5 -> 6; matrix products, arithmetic and copies ran while one was open for 1% -> 0% of each run, Pallas kernels for 0% -> 30%
where the time goes in v2:
time: 96 us; the launch traced here: 95.5 us
  Pallas kernels  40.1 us (42%)
  starting transfers between devices  29.4 us (31%)
  waiting for transfers between devices  21.8 us (23%)
  local copies, waits for them, and re-layouts  3.81 us (4%)
    all_to_all x1, starting transfers between devices, shards(): lax.all_to_all(taps.reshape(ctx, channels, position), 'ctx', split_axis=0...  9.28 us
    pallas_call x1, Pallas kernels, shards(): pl.pallas_call(out_kernel, in_specs=[VMEM, ANY], out_specs=ANY, out_shape...  9.08 us
    pallas_call x1, Pallas kernels, shards(): pl.pallas_call(conv_kernel, in_specs=[SMEM, VMEM] + [ANY] * 6, out_specs=...  9.01 us
    all_to_all x1, waiting for transfers between devices, shards(): lax.all_to_all(partial_value.reshape(devices, channels, position), ('ch',...  8.39 us
    pallas_call x1, Pallas kernels, shards(): pl.pallas_call(project_kernel, in_specs=[ANY] * 2, out_specs=ANY, out_sha...  7.32 us
    pallas_call x1, Pallas kernels, shards(): pl.pallas_call(weights_kernel, in_specs=[ANY] * (1 + 2 * PIECES), out_spe...  6.79 us
    all_to_all x1, waiting for transfers between devices, shards(): lax.all_to_all(mixed.reshape(devices, channels, position), ('ch', 'ctx'),...  6.48 us
    pallas_call x1, Pallas kernels, shards(): pl.pallas_call(spectrum_kernel, in_specs=[VMEM] + [ANY] * 4, out_specs=AN...  5.33 us
  transfers between devices with their start and end apart: 11, of which 6 were waited for; matrix products, arithmetic and copies ran while one was open for 0% of the time, Pallas kernels for 30%

profile of v2, /device:TPU:1, one launch (start us, length us, event | category | flops | bytes accessed | tf_op | source)
XLA Modules:
  0.0 95.5 jit_solution(8910354825605820529)
XLA Ops:
  0.0 2.6 %shard_map.110 = (bf16[512,512]{1,0:T(8,128)(2,1)}, bf16[64,4096]{1,0:T(8,128)(2,1)}, bf16[64,4096]{1,0:T(8,128)(2,1)}) custom-call(f32[512,512]{1,0:T(8,128)} %taps_hbm.1, bf16[512,8192]{1,0:T(8,128)(2,1)} %own_hbm.1), custom_call_target="tpu_custom_call" | custom-call | bytes 4194304 | tf_op jit(solution)/shard_map/pallas_call | solution.py:382
  2.6 3.6 %collective-permute-start = (bf16[64,4096]{1,0:T(8,128)(2,1)}, bf16[64,4096]{1,0:T(8,128)(2,1)S(1)}, u32[]{:S(2)}, u32[]{:S(2)}) collective-permute-start(bf16[64,4096]{1,0:T(8,128)(2,1)} %get-tuple-element.8), channel_id=1, source_target_pairs={{0,65},{2,67},{4,69},{6,71},{8,73},{10,75},{12,77},{14,79},{16,81}... | collective-permute-start | bytes 1572872 | tf_op jit(solution)/shard_map/ppermute | solution.py:397
  6.3 9.3 %all-to-all-start.1 = ((bf16[64,8,512]{2,1,0:T(8,128)(2,1)}), bf16[64,8,512]{2,1,0:T(8,128)(2,1)S(1)}, u32[]{:S(2)}, u32[]{:S(2)}) async-start(bf16[64,8,512]{2,1,0:T(8,128)(2,1)} %bitcast.9), calls=%async_computation.1 | async-start | bytes 1048576 | tf_op jit(solution)/shard_map/all_to_all | solution.py:398
  15.6 7.3 %shard_map.109.value_ref = bf16[1024,512]{1,0:T(8,128)(2,1)} custom-call(bf16[512,4096]{1,0:T(8,128)(2,1)} %tokens_hbm.1, bf16[4096,1024]{1,0:T(8,128)(2,1)} %weight_hbm.2), custom_call_target="tpu_custom_call" | custom-call | flops 4294967296 | bytes 14680064 | tf_op jit(solution)/shard_map/pallas_call | solution.py:402
  22.9 0.0 collective-permute-done.after_ref.rest_0_
  22.9 0.0 copy-start
  22.9 0.8 copy-done
  23.7 3.8 %all-to-all-done.1.taps_ref = bf16[64,8,512]{2,1,0:T(8,128)(2,1)S(1)} async-done(((bf16[64,8,512]{2,1,0:T(8,128)(2,1)}), bf16[64,8,512]{2,1,0:T(8,128)(2,1)S(1)}, u32[]{:S(2)}, u32[]{:S(2)}) %all-to-all-start.1) | async-done | bytes 524320 | tf_op jit(solution)/shard_map/all_to_all | solution.py:398
  27.5 0.0 copy-start.10
  27.5 4.1 %all-to-all-start = ((bf16[128,8,512]{2,1,0:T(8,128)(2,1)}), bf16[128,8,512]{2,1,0:T(8,128)(2,1)S(1)}, u32[]{:S(2)}, u32[]{:S(2)}) async-start(bf16[128,8,512]{2,1,0:T(8,128)(2,1)} %bitcast.5), calls=%async_computation | async-start | bytes 2097152 | tf_op jit(solution)/shard_map/all_to_all | solution.py:429
  31.6 2.7 %collective-permute-start.3 = (bf16[64,4096]{1,0:T(8,128)(2,1)}, bf16[64,4096]{1,0:T(8,128)(2,1)S(1)}, u32[]{:S(2)}, u32[]{:S(2)}) collective-permute-start(bf16[64,4096]{1,0:T(8,128)(2,1)} %get-tuple-element.10), channel_id=1, source_target_pairs={{0,65},{2,67},{4,69},{6,71},{8,73},{10,75},{12,77},{14,79},{16,81}... | collective-permute-start | bytes 1572872 | tf_op jit(solution)/shard_map/ppermute | solution.py:436
  34.4 0.0 copy-done.10
  34.4 5.3 %shard_map.112.spec_hbm = f32[2,1152,256]{2,1,0:T(8,128)} custom-call(bf16[64,8,512]{2,1,0:T(8,128)(2,1)} %copy-done.10, bf16[144,128]{1,0:T(8,128)(2,1)} %constant.13.clone.lead_hbm, f32[2,72,512]{2,1,0:T(8,128)} %constant.15.clone.twist_hbm, f32[8,128]{1,0:T(8,128)} %constant.16.clone.fold_hbm, bf16[768,256]{1,0:T(8,128)(2,1)} %constant.17.clone.line_hbm), custom_call_target="tpu_custom_call" | custom-call | flops 4000000000 | bytes 4194304 | tf_op jit(solution)/shard_map/pallas_call | solution.py:443
  39.7 0.0 copy-done.1
  39.7 1.3 %collective-permute-start.2 = (bf16[64,4096]{1,0:T(8,128)(2,1)S(1)}, bf16[64,4096]{1,0:T(8,128)(2,1)S(1)}, u32[]{:S(2)}, u32[]{:S(2)}) collective-permute-start(bf16[64,4096]{1,0:T(8,128)(2,1)S(1)} %copy-done.1), channel_id=1, source_target_pairs={{0,16},{2,18},{4,20},{6,22},{8,24},{10,26},{12,28},{14,30},{16,0},... | collective-permute-start | bytes 1572872 | tf_op jit(solution)/shard_map/ppermute | solution.py:434
  41.0 1.5 %collective-permute-start.1 = (bf16[64,4096]{1,0:T(8,128)(2,1)S(1)}, bf16[64,4096]{1,0:T(8,128)(2,1)S(1)}, u32[]{:S(2)}, u32[]{:S(2)}) collective-permute-start(bf16[64,4096]{1,0:T(8,128)(2,1)S(1)} %copy-done.1), channel_id=1, source_target_pairs={{0,4},{2,6},{4,0},{6,2},{8,12},{10,14},{12,8},{14,10},{16,20},{18,... | collective-permute-start | bytes 1572872 | tf_op jit(solution)/shard_map/ppermute | solution.py:435
  42.5 8.4 %all-to-all-done = bf16[128,8,512]{2,1,0:T(8,128)(2,1)S(1)} async-done(((bf16[128,8,512]{2,1,0:T(8,128)(2,1)}), bf16[128,8,512]{2,1,0:T(8,128)(2,1)S(1)}, u32[]{:S(2)}, u32[]{:S(2)}) %all-to-all-start) | async-done | bytes 1048608 | tf_op jit(solution)/shard_map/all_to_all | solution.py:429
  50.9 0.0 copy-start.3
  50.9 1.0 %copy-done.3 = bf16[128,8,512]{2,1,0:T(8,128)(2,1)} copy-done((bf16[128,8,512]{2,1,0:T(8,128)(2,1)}, bf16[128,8,512]{2,1,0:T(8,128)(2,1)S(1)}, u32[]{:S(2)}) %copy-start.3) | copy-done | bytes 1048600
  51.9 9.0 %shard_map.113 = bf16[2,64,8,512]{3,2,1,0:T(8,128)(2,1)} custom-call(f32[512]{0:T(512)} %gain_ref.1, bf16[2,64,8,512]{3,2,1,0:T(8,128)(2,1)} %bitcast.8, f32[2,1152,256]{2,1,0:T(8,128)} %shard_map.112.spec_hbm, bf16[144,192]{1,0:T(8,128)(2,1)} %constant.12.clone.lead_hbm, bf16[64,512]{1,0:T(8,128)(2,1)} %constant.14.clone.tail_hbm, ...), custom_call_target="tpu_custom_call" | custom-call | flops 8000000000 | bytes 6291456 | tf_op jit(solution)/shard_map/pallas_call | solution.py:460
  60.9 5.0 %all-to-all-start.2 = ((bf16[128,8,512]{2,1,0:T(8,128)(2,1)}), bf16[128,8,512]{2,1,0:T(8,128)(2,1)S(1)}, u32[]{:S(2)}, u32[]{:S(2)}) async-start(bf16[128,8,512]{2,1,0:T(8,128)(2,1)} %bitcast.6), calls=%async_computation.2 | async-start | bytes 2097152 | tf_op jit(solution)/shard_map/all_to_all | solution.py:478
  65.9 1.3 %collective-permute-start.4 = (bf16[64,4096]{1,0:T(8,128)(2,1)S(1)}, bf16[64,4096]{1,0:T(8,128)(2,1)S(1)}, u32[]{:S(2)}, u32[]{:S(2)}) collective-permute-start(bf16[64,4096]{1,0:T(8,128)(2,1)S(1)} %copy-done.1), channel_id=1, source_target_pairs={{0,2},{2,0},{4,6},{6,4},{8,10},{10,8},{12,14},{14,12},{16,18},{18,... | collective-permute-start | bytes 1572872 | tf_op jit(solution)/shard_map/ppermute | solution.py:438
  67.2 0.0 collective-permute-done.3.rest_3_
  67.2 0.0 copy-start.4
  67.2 0.1 collective-permute-start.7
  67.3 0.0 collective-permute-done.2.rest_2_
  67.3 0.0 copy-start.5
  67.3 0.4 collective-permute-start.6
  67.7 0.0 collective-permute-done.1.rest_1_
  67.7 0.0 copy-start.6
  67.7 0.1 collective-permute-start.5
  67.8 0.9 collective-permute-done.4.rest_4_
  68.7 0.0 copy-start.7
  68.7 1.5 %collective-permute-done.7.rest_7_ = bf16[64,4096]{1,0:T(8,128)(2,1)S(1)} collective-permute-done((bf16[64,4096]{1,0:T(8,128)(2,1)S(1)}, bf16[64,4096]{1,0:T(8,128)(2,1)S(1)}, u32[]{:S(2)}, u32[]{:S(2)}) %collective-permute-start.7) | collective-permute-done | bytes 524320 | tf_op jit(solution)/shard_map/ppermute | solution.py:438
  70.2 0.0 copy-start.8
  70.2 0.7 collective-permute-done.6.rest_6_
  70.9 0.1 copy-done.8
  71.1 0.0 copy-start.9
  71.1 0.8 copy-done.9
  71.9 0.0 collective-permute-done.5.rest_5_
  71.9 0.0 copy-done.4
  71.9 0.0 copy-done.5
  71.9 0.0 copy-done.6
  71.9 0.0 copy-done.7
  71.9 6.8 %shard_map.114.weight_hbm = bf16[8,1024,512]{2,1,0:T(8,128)(2,1)} custom-call(bf16[512,8192]{1,0:T(8,128)(2,1)} %own_hbm.1, bf16[64,4096]{1,0:T(8,128)(2,1)} %copy-done, bf16[64,4096]{1,0:T(8,128)(2,1)} %copy-done.6, bf16[64,4096]{1,0:T(8,128)(2,1)} %copy-done.5, bf16[64,4096]{1,0:T(8,128)(2,1)} %copy-done.4, bf16[64,4096]{1,0:T(8,128)(2,1)} %copy-done.7, ...), custom_call_target="tpu_custom_call" | custom-call | bytes 16777216 | tf_op jit(solution)/shard_map/pallas_call | solution.py:484
  78.7 6.5 %all-to-all-done.2 = bf16[128,8,512]{2,1,0:T(8,128)(2,1)S(1)} async-done(((bf16[128,8,512]{2,1,0:T(8,128)(2,1)}), bf16[128,8,512]{2,1,0:T(8,128)(2,1)S(1)}, u32[]{:S(2)}, u32[]{:S(2)}) %all-to-all-start.2) | async-done | bytes 1048608 | tf_op jit(solution)/shard_map/all_to_all | solution.py:478
  85.2 1.1 %copy-done.2 = bf16[128,8,512]{2,1,0:T(8,128)(2,1)} copy-done((bf16[128,8,512]{2,1,0:T(8,128)(2,1)}, bf16[128,8,512]{2,1,0:T(8,128)(2,1)S(1)}, u32[]{:S(2)}) %copy-start.2) | copy-done | bytes 1048600
  86.3 9.1 %shard_map.115 = bf16[512,4096]{1,0:T(8,128)(2,1)} custom-call(bf16[1024,512]{1,0:T(8,128)(2,1)} %bitcast.7, bf16[8,1024,512]{2,1,0:T(8,128)(2,1)} %shard_map.114.weight_hbm), custom_call_target="tpu_custom_call" | custom-call | flops 4294967296 | bytes 13631488 | tf_op jit(solution)/shard_map/pallas_call | solution.py:498
  (3 shorter events, 0.0 us)
Async XLA Ops:
  2.6 20.3 %collective-permute-start = (bf16[64,4096]{1,0:T(8,128)(2,1)}, bf16[64,4096]{1,0:T(8,128)(2,1)S(1)}, u32[]{:S(2)}, u32[]{:S(2)}) collective-permute-start(bf16[64,4096]{1,0:T(8,128)(2,1)} %get-tuple-element.8), channel_id=1, source_target_pairs={{0,65},{2,67},{4,69},{6,71},{8,73},{10,75},{12,77},{14,79},{16,81}... | collective-permute-start | bytes 1572872 | tf_op jit(solution)/shard_map/ppermute | solution.py:397
  6.3 21.2 %all-to-all-start.1 = ((bf16[64,8,512]{2,1,0:T(8,128)(2,1)}), bf16[64,8,512]{2,1,0:T(8,128)(2,1)S(1)}, u32[]{:S(2)}, u32[]{:S(2)}) async-start(bf16[64,8,512]{2,1,0:T(8,128)(2,1)} %bitcast.9), calls=%async_computation.1 | async-start | bytes 1048576 | tf_op jit(solution)/shard_map/all_to_all | solution.py:398
  22.9 0.8 copy-start
  27.5 6.9 %copy-start.10 = (bf16[64,8,512]{2,1,0:T(8,128)(2,1)}, bf16[64,8,512]{2,1,0:T(8,128)(2,1)S(1)}, u32[]{:S(2)}) copy-start(bf16[64,8,512]{2,1,0:T(8,128)(2,1)S(1)} %all-to-all-done.1.taps_ref) | copy-start | bytes 1572868
  27.5 12.2 %copy-start.1 = (bf16[64,4096]{1,0:T(8,128)(2,1)S(1)}, bf16[64,4096]{1,0:T(8,128)(2,1)}, u32[]{:S(2)}) copy-start(bf16[64,4096]{1,0:T(8,128)(2,1)} %copy-done) | copy-start | bytes 1572868
  27.5 23.3 %all-to-all-start = ((bf16[128,8,512]{2,1,0:T(8,128)(2,1)}), bf16[128,8,512]{2,1,0:T(8,128)(2,1)S(1)}, u32[]{:S(2)}, u32[]{:S(2)}) async-start(bf16[128,8,512]{2,1,0:T(8,128)(2,1)} %bitcast.5), calls=%async_computation | async-start | bytes 2097152 | tf_op jit(solution)/shard_map/all_to_all | solution.py:429
  31.6 35.5 %collective-permute-start.3 = (bf16[64,4096]{1,0:T(8,128)(2,1)}, bf16[64,4096]{1,0:T(8,128)(2,1)S(1)}, u32[]{:S(2)}, u32[]{:S(2)}) collective-permute-start(bf16[64,4096]{1,0:T(8,128)(2,1)} %get-tuple-element.10), channel_id=1, source_target_pairs={{0,65},{2,67},{4,69},{6,71},{8,73},{10,75},{12,77},{14,79},{16,81}... | collective-permute-start | bytes 1572872 | tf_op jit(solution)/shard_map/ppermute | solution.py:436
  39.7 27.5 %collective-permute-start.2 = (bf16[64,4096]{1,0:T(8,128)(2,1)S(1)}, bf16[64,4096]{1,0:T(8,128)(2,1)S(1)}, u32[]{:S(2)}, u32[]{:S(2)}) collective-permute-start(bf16[64,4096]{1,0:T(8,128)(2,1)S(1)} %copy-done.1), channel_id=1, source_target_pairs={{0,16},{2,18},{4,20},{6,22},{8,24},{10,26},{12,28},{14,30},{16,0},... | collective-permute-start | bytes 1572872 | tf_op jit(solution)/shard_map/ppermute | solution.py:434
  41.0 26.7 %collective-permute-start.1 = (bf16[64,4096]{1,0:T(8,128)(2,1)S(1)}, bf16[64,4096]{1,0:T(8,128)(2,1)S(1)}, u32[]{:S(2)}, u32[]{:S(2)}) collective-permute-start(bf16[64,4096]{1,0:T(8,128)(2,1)S(1)} %copy-done.1), channel_id=1, source_target_pairs={{0,4},{2,6},{4,0},{6,2},{8,12},{10,14},{12,8},{14,10},{16,20},{18,... | collective-permute-start | bytes 1572872 | tf_op jit(solution)/shard_map/ppermute | solution.py:435
  50.9 1.0 %copy-start.3 = (bf16[128,8,512]{2,1,0:T(8,128)(2,1)}, bf16[128,8,512]{2,1,0:T(8,128)(2,1)S(1)}, u32[]{:S(2)}) copy-start(bf16[128,8,512]{2,1,0:T(8,128)(2,1)S(1)} %all-to-all-done) | copy-start | bytes 3145732
  60.9 24.3 %all-to-all-start.2 = ((bf16[128,8,512]{2,1,0:T(8,128)(2,1)}), bf16[128,8,512]{2,1,0:T(8,128)(2,1)S(1)}, u32[]{:S(2)}, u32[]{:S(2)}) async-start(bf16[128,8,512]{2,1,0:T(8,128)(2,1)} %bitcast.6), calls=%async_computation.2 | async-start | bytes 2097152 | tf_op jit(solution)/shard_map/all_to_all | solution.py:478
  65.9 2.8 %collective-permute-start.4 = (bf16[64,4096]{1,0:T(8,128)(2,1)S(1)}, bf16[64,4096]{1,0:T(8,128)(2,1)S(1)}, u32[]{:S(2)}, u32[]{:S(2)}) collective-permute-start(bf16[64,4096]{1,0:T(8,128)(2,1)S(1)} %copy-done.1), channel_id=1, source_target_pairs={{0,2},{2,0},{4,6},{6,4},{8,10},{10,8},{12,14},{14,12},{16,18},{18,... | collective-permute-start | bytes 1572872 | tf_op jit(solution)/shard_map/ppermute | solution.py:438
  67.2 4.7 %copy-start.4 = (bf16[64,4096]{1,0:T(8,128)(2,1)}, bf16[64,4096]{1,0:T(8,128)(2,1)S(1)}, u32[]{:S(2)}) copy-start(bf16[64,4096]{1,0:T(8,128)(2,1)S(1)} %collective-permute-done.3.rest_3_) | copy-start | bytes 1572868
  67.2 3.0 %collective-permute-start.7 = (bf16[64,4096]{1,0:T(8,128)(2,1)S(1)}, bf16[64,4096]{1,0:T(8,128)(2,1)S(1)}, u32[]{:S(2)}, u32[]{:S(2)}) collective-permute-start(bf16[64,4096]{1,0:T(8,128)(2,1)S(1)} %collective-permute-done.3.rest_3_), channel_id=1, source_target_pairs={{0,2},{2,0},{4,6},{6,4},{8,10},{10,8},{12,14},{14,12},{16,18},{18,... | collective-permute-start | bytes 1572872 | tf_op jit(solution)/shard_map/ppermute | solution.py:438
  67.3 4.6 %copy-start.5 = (bf16[64,4096]{1,0:T(8,128)(2,1)}, bf16[64,4096]{1,0:T(8,128)(2,1)S(1)}, u32[]{:S(2)}) copy-start(bf16[64,4096]{1,0:T(8,128)(2,1)S(1)} %collective-permute-done.2.rest_2_) | copy-start | bytes 1572868
  67.3 3.7 %collective-permute-start.6 = (bf16[64,4096]{1,0:T(8,128)(2,1)S(1)}, bf16[64,4096]{1,0:T(8,128)(2,1)S(1)}, u32[]{:S(2)}, u32[]{:S(2)}) collective-permute-start(bf16[64,4096]{1,0:T(8,128)(2,1)S(1)} %collective-permute-done.2.rest_2_), channel_id=1, source_target_pairs={{0,2},{2,0},{4,6},{6,4},{8,10},{10,8},{12,14},{14,12},{16,18},{18,... | collective-permute-start | bytes 1572872 | tf_op jit(solution)/shard_map/ppermute | solution.py:438
  67.7 4.2 %copy-start.6 = (bf16[64,4096]{1,0:T(8,128)(2,1)}, bf16[64,4096]{1,0:T(8,128)(2,1)S(1)}, u32[]{:S(2)}) copy-start(bf16[64,4096]{1,0:T(8,128)(2,1)S(1)} %collective-permute-done.1.rest_1_) | copy-start | bytes 1572868
  67.7 4.2 %collective-permute-start.5 = (bf16[64,4096]{1,0:T(8,128)(2,1)S(1)}, bf16[64,4096]{1,0:T(8,128)(2,1)}, u32[]{:S(2)}, u32[]{:S(2)}) collective-permute-start(bf16[64,4096]{1,0:T(8,128)(2,1)S(1)} %collective-permute-done.1.rest_1_), channel_id=1, source_target_pairs={{0,2},{2,0},{4,6},{6,4},{8,10},{10,8},{12,14},{14,12},{16,18},{18,... | collective-permute-start | bytes 1572872 | tf_op jit(solution)/shard_map/ppermute | solution.py:438
  68.7 3.2 %copy-start.7 = (bf16[64,4096]{1,0:T(8,128)(2,1)}, bf16[64,4096]{1,0:T(8,128)(2,1)S(1)}, u32[]{:S(2)}) copy-start(bf16[64,4096]{1,0:T(8,128)(2,1)S(1)} %collective-permute-done.4.rest_4_) | copy-start | bytes 1572868
  70.2 0.9 copy-start.8
  71.1 0.8 copy-start.9
  85.2 1.1 %copy-start.2 = (bf16[128,8,512]{2,1,0:T(8,128)(2,1)}, bf16[128,8,512]{2,1,0:T(8,128)(2,1)S(1)}, u32[]{:S(2)}) copy-start(bf16[128,8,512]{2,1,0:T(8,128)(2,1)S(1)} %all-to-all-done.2) | copy-start | bytes 3145732

commit v3 on v2

v3 whole, which is shorter than its diff:
```python
import numpy as np
import ml_dtypes
import jax
import jax.numpy as jnp
from jax import lax
from jax.experimental import pallas as pl
from jax.experimental.pallas import tpu as pltpu
from jax.sharding import PartitionSpec as P

bf16 = jnp.bfloat16
f32 = jnp.float32
MIB = 1024 * 1024
TILE = 16
GROUP = 4
CHUNK = 512
SPARE = 12
LAST_PARTS = 4
PIECES = 4


def split_table(table):
    high = table.astype(ml_dtypes.bfloat16)
    low = (table - high.astype(np.float64)).astype(ml_dtypes.bfloat16)
    return high, low


def tables(blocks, width):
    period = 2 * blocks * width
    quarter = width // 4
    freq = np.arange(blocks)[:, None]
    angle = 2.0 * np.pi * (freq * np.arange(blocks)[None, :] % (2 * blocks)) / (2 * blocks)
    lead_high, lead_low = split_table(np.concatenate([np.cos(angle), -np.sin(angle)], axis=0))
    weight = np.where(freq == 0, 1.0, 2.0) / period
    cosines, sines = np.cos(angle) * weight, np.sin(angle) * weight
    sines[0] = (1.0 - 2.0 * (np.arange(blocks) % 2)) / period
    tail_high, tail_low = split_table(np.concatenate([cosines, sines], axis=0).T)
    turned = np.concatenate([freq, np.full((TILE, 1), blocks)])
    turn = 2.0 * np.pi * turned * np.arange(width)[None, :] / period
    fold = 2.0 * np.pi * np.arange(4)[:, None] * np.arange(quarter)[None, :] / width
    index = np.arange(quarter)
    line = 2.0 * np.pi * (index[:, None] * index[None, :] % quarter) / quarter
    cos, sin = np.cos(line), np.sin(line)
    line_high, line_low = split_table(np.block([[cos, -sin], [sin, cos]]))
    parts = [
        line_high,
        line_low,
        np.concatenate([lead_high, lead_high, lead_low], axis=1),
        np.concatenate([lead_high, lead_low], axis=1),
        np.block([[tail_high, tail_high], [tail_low, np.zeros_like(tail_low)]]),
        *np.split(np.cos(turn), 2, axis=1),
        *np.split(np.sin(turn), 2, axis=1),
        np.concatenate([np.cos(fold), np.sin(fold)]),
    ]
    columns = line_high.shape[1]
    return np.concatenate(
        [np.pad(p.astype(np.float32), ((0, 0), (0, columns - p.shape[1]))) for p in parts]
    )


def unpack(table_ref, blocks, line_ref, twist_ref):
    columns = line_ref.shape[1]
    line_ref[:columns] = table_ref[:columns].astype(bf16)
    line_ref[columns:] = table_ref[: 2 * columns].astype(bf16)
    at = 2 * columns
    leads = []
    for use in (3 * blocks, 2 * blocks, 4 * blocks):
        leads.append(table_ref[at : at + 2 * blocks, :use].astype(bf16))
        at += 2 * blocks
    rows = twist_ref.shape[1]
    for i in range(2):
        for k in range(2):
            twist_ref[i, :, columns * k : columns * (k + 1)] = table_ref[at : at + rows]
            at += rows
    return (*leads, table_ref[at : at + 8, : columns // 2])


def dot(a, b):
    return jnp.dot(a, b, preferred_element_type=f32)


def split(a):
    high = a.astype(bf16)
    return high, (a - high.astype(f32)).astype(bf16)


def turn_back(real, imag, cos, sin):
    return real * cos + imag * sin, imag * cos - real * sin


def butterfly(parts):
    (ar, ai), (br, bi), (cr, ci), (dr, di) = parts
    sr, si, er, ei = ar + cr, ai + ci, ar - cr, ai - ci
    tr, ti, fr, fi = br + dr, bi + di, br - dr, bi - di
    return [(sr + tr, si + ti), (er + fi, ei - fr), (sr - tr, si - ti), (er - fi, ei + fr)]


def put_rows(rows_ref, at, value):
    high, low = split(value)
    size = value.shape[1]
    span = pl.ds(at, value.shape[0])
    rows_ref[span, :size] = high
    rows_ref[span, size : 2 * size] = low


def transform_rows(rows_ref, at, count, line_ref):
    size = line_ref.shape[1]
    span = pl.ds(at, count)
    both = dot(rows_ref[span, :], line_ref[: 2 * size, :])
    return both + dot(rows_ref[span, :size], line_ref[2 * size :, :])


def spread(real, imag, freqs, rows_ref, at, twist_ref, fold):
    quarter = real.shape[1] // 4
    parts = []
    for p in range(4):
        lanes = slice(quarter * p, quarter * (p + 1))
        cos, sin = twist_ref[0, freqs, lanes], twist_ref[1, freqs, lanes]
        if imag is None:
            parts.append((real[:, lanes] * cos, -real[:, lanes] * sin))
        else:
            parts.append(turn_back(real[:, lanes], imag[:, lanes], cos, sin))
    for r, (a, b) in enumerate(butterfly(parts)):
        if r:
            a, b = turn_back(a, b, fold[r : r + 1], fold[r + 4 : r + 5])
        put_rows(rows_ref, at + TILE * r, jnp.concatenate([a, b], axis=1))


def gather_back(back_ref, at, freqs, twist_ref, fold):
    quarter = back_ref.shape[1] // 2
    got = []
    for r in range(4):
        span = pl.ds(at + TILE * r, TILE)
        a, b = back_ref[span, :quarter], back_ref[span, quarter:]
        if r:
            a, b = turn_back(a, b, fold[r : r + 1], fold[r + 4 : r + 5])
        got.append((a, b))
    reals, imags = [], []
    for p, (a, b) in enumerate(butterfly(got)):
        lanes = slice(quarter * p, quarter * (p + 1))
        a, b = turn_back(a, b, twist_ref[0, freqs, lanes], twist_ref[1, freqs, lanes])
        reals.append(a)
        imags.append(b)
    return jnp.concatenate(reals, axis=1), jnp.concatenate(imags, axis=1)


def where():
    here = lax.axis_index("ctx")
    return lax.axis_index("ch"), here & 1, here >> 3 & 3, here >> 1 & 3


def held_pieces(x, z):
    first = (x & 1) * 2 + (z & 1)
    return [first ^ flip for flip in range(PIECES)]


def start_all(pairs, sems):
    copies = [pltpu.make_async_copy(a, b, sems.at[i]) for i, (a, b) in enumerate(pairs)]
    for copy in copies:
        copy.start()
    return copies


def forward(load, last, lead, lines_ref, rows_ref, spec_ref, twist_ref, fold, line_ref):
    channels = lines_ref.shape[0]
    blocks = lines_ref.shape[1] // 2
    tiles = blocks // TILE
    size = blocks * 4
    end = channels * size
    spread(last, None, pl.ds(blocks, TILE), rows_ref, end, twist_ref, fold)
    for step in range(channels // GROUP):
        held = range(GROUP * step, GROUP * (step + 1))
        for c in held:
            lines_ref[c] = dot(lead, load(c))
        for c in held:
            for t in range(tiles):
                freqs = pl.ds(TILE * t, TILE)
                real = lines_ref[c, freqs, :]
                imag = lines_ref[c, pl.ds(blocks + TILE * t, TILE), :]
                spread(real, imag, freqs, rows_ref, c * size + 4 * TILE * t, twist_ref, fold)
        count = GROUP * size + (4 * TILE if step == channels // GROUP - 1 else 0)
        spec_ref[pl.ds(GROUP * size * step, count), :] = transform_rows(
            rows_ref, GROUP * size * step, count, line_ref
        )


def fill(flat, planes):
    blocks, channels, width = planes.shape
    rows = planes.reshape(blocks * channels, width)
    for q in range(width // 128):
        flat[q, : blocks * channels] = rows[:, 128 * q : 128 * (q + 1)]


def channel_of(flat, channel, blocks, channels):
    place = pl.ds(channel, blocks, stride=channels)
    return jnp.concatenate([flat[q, place, :] for q in range(flat.shape[0])], axis=1)


def alternating(planes):
    pairs = planes.reshape(planes.shape[0] // 2, 2, *planes.shape[1:])
    rows = jnp.sum(pairs[:, 0] - pairs[:, 1], axis=0)
    return jnp.concatenate([rows, jnp.zeros((TILE - rows.shape[0], rows.shape[1]), f32)], axis=0)


def spectrum_kernel(
    taps_ref, table_hbm, spec_hbm,
    table_ref, twist_ref, line_ref, flat, lines_ref, rows_ref, spec_ref, sems,
):
    blocks, channels, _ = taps_ref.shape
    copies = start_all([(table_hbm, table_ref)], sems)
    taps = taps_ref[...].astype(f32)
    fill(flat, taps)
    last = alternating(taps)
    for copy in copies:
        copy.wait()

    def load(c):
        value = channel_of(flat, c, blocks, channels).astype(bf16)
        return jnp.concatenate([value, value], axis=0)

    _, lead, _, fold = unpack(table_ref, blocks, line_ref, twist_ref)
    forward(load, last, lead, lines_ref, rows_ref, spec_ref, twist_ref, fold, line_ref)
    copy = pltpu.make_async_copy(spec_ref, spec_hbm.at[pl.ds(0, spec_ref.shape[0])], sems.at[1])
    copy.start()
    copy.wait()


def conv_kernel(
    gain_ref, parts_ref, spec_hbm, table_hbm, out_hbm,
    taps_spec_ref, table_ref, twist_ref, line_ref,
    flat, lines_ref, rows_ref, spec_ref, packed_ref, mixed_ref, out_ref, sems, out_sems,
):
    _, blocks, channels, width = parts_ref.shape
    lanes = flat.shape[2]
    quarters = width // lanes
    quarter = spec_ref.shape[1] // 2
    tiles = blocks // TILE
    size = blocks * 4
    half = blocks // 2
    copies = start_all([(table_hbm, table_ref), (spec_hbm.at[pl.ds(0, taps_spec_ref.shape[0])], taps_spec_ref)], sems)
    total = parts_ref[0].astype(f32) + parts_ref[1].astype(f32)
    fill(flat, total)
    last = alternating(total)
    copies[0].wait()
    lead, _, tail, fold = unpack(table_ref, blocks, line_ref, twist_ref)

    def load(c):
        high, low = split(channel_of(flat, c, blocks, channels))
        return jnp.concatenate([high, low, high], axis=0)

    forward(load, last, lead, lines_ref, rows_ref, spec_ref, twist_ref, fold, line_ref)
    copies[1].wait()

    def multiply(at, gain):
        span = pl.ds(at, 4 * TILE)
        real, imag = spec_ref[span, :quarter], spec_ref[span, quarter:]
        taps_real, taps_imag = taps_spec_ref[span, :quarter] + gain, taps_spec_ref[span, quarter:]
        put_rows(
            rows_ref, at,
            jnp.concatenate(
                [real * taps_real - imag * taps_imag, -(real * taps_imag + imag * taps_real)], axis=1
            ),
        )

    first_gain = lax.axis_index("ctx") * channels
    gain = [gain_ref[first_gain + c] for c in range(channels)]
    end = channels * size
    row = lax.broadcasted_iota(jnp.int32, (4 * TILE, quarter), 0) % TILE
    all_gains = jnp.zeros((4 * TILE, quarter), f32)
    for c in range(channels):
        all_gains = jnp.where(row == c, gain[c], all_gains)
    multiply(end, all_gains)
    spec_ref[pl.ds(end, 4 * TILE), :] = transform_rows(rows_ref, end, 4 * TILE, line_ref)
    last, _ = gather_back(spec_ref, end, pl.ds(blocks, TILE), twist_ref, fold)
    first_row = lax.broadcasted_iota(jnp.int32, (TILE, width), 0) == 0
    for step in range(channels // GROUP):
        held = range(GROUP * step, GROUP * (step + 1))
        for c in held:
            for t in range(tiles):
                multiply(c * size + 4 * TILE * t, gain[c])
        at = GROUP * size * step
        spec_ref[pl.ds(at, GROUP * size), :] = transform_rows(rows_ref, at, GROUP * size, line_ref)
        for c in held:
            for t in range(tiles):
                real, imag = gather_back(
                    spec_ref, c * size + 4 * TILE * t, pl.ds(TILE * t, TILE), twist_ref, fold
                )
                if t == 0:
                    imag = jnp.where(first_row, last[c : c + 1], imag)
                for at, part in ((TILE * t, real), (blocks + TILE * t, imag)):
                    high, low = split(part)
                    packed_ref[c, pl.ds(at, TILE), :] = high
                    packed_ref[c, pl.ds(2 * blocks + at, TILE), :] = low
            both = dot(tail, packed_ref[c])
            value = both[:blocks] + both[blocks:]
            for q in range(quarters):
                mixed_ref[q, pl.ds(c, blocks, stride=channels), :] = value[:, lanes * q : lanes * (q + 1)]
    stores = []
    for i in range(2):
        span = pl.ds(half * i, half)
        for q in range(quarters):
            result = mixed_ref[q, pl.ds(half * channels * i, half * channels), :].astype(bf16)
            out_ref[span, :, lanes * q : lanes * (q + 1)] = result.reshape(half, channels, lanes)
        for k in range(2):
            stores.append(
                pltpu.make_async_copy(out_ref.at[span], out_hbm.at[k, span], out_sems.at[2 * i + k])
            )
            stores[-1].start()
    for copy in stores:
        copy.wait()


def prepare_kernel(
    taps_hbm, weight_hbm, out_hbm, piece_hbm, taps_ref, out_ref, piece_ref, sems, out_sems
):
    steps = sems.shape[0] - 1
    size = taps_ref.shape[1] // steps
    spans = [pl.ds(i * size, size) for i in range(steps)]
    loads = start_all(
        [(taps_hbm.at[:, s], taps_ref.at[:, s]) for s in spans]
        + [(piece_source(weight_hbm, piece_hbm, 0), piece_ref)],
        sems,
    )
    stores = []
    for i in range(steps):
        loads[i].wait()
        at = slice(i * size, (i + 1) * size)
        out_ref[at, :] = taps_ref[:, at].astype(bf16).T
        stores.append(pltpu.make_async_copy(out_ref.at[spans[i]], out_hbm.at[spans[i]], out_sems.at[i]))
        stores[-1].start()
    loads[steps].wait()
    stores.append(pltpu.make_async_copy(piece_ref, piece_hbm, out_sems.at[steps]))
    stores[-1].start()
    for store in stores:
        store.wait()


def piece_source(weight_hbm, piece_ref, chosen):
    group, core, x, z = where()
    size, columns = piece_ref.shape
    at = pl.ds(pl.multiple_of((1 - group) * columns, columns), columns)
    start = (core * PIECES + held_pieces(x, z)[chosen]) * size
    return weight_hbm.at[pl.ds(pl.multiple_of(start, size), size), at]


def last_piece_kernel(weight_hbm, after_ref, out_hbm, piece_ref, sems):
    source = piece_source(weight_hbm, out_hbm, PIECES - 1)
    for a, b, sem in ((source, piece_ref, sems.at[0]), (piece_ref, out_hbm, sems.at[1])):
        copy = pltpu.make_async_copy(a, b, sem)
        copy.start()
        copy.wait()


def fence_kernel(value_ref, after_ref, out_ref):
    pass


def project_kernel(
    tokens_hbm, weight_hbm, out_hbm, tokens_ref, weight_ref, total, out_ref,
    token_sems, weight_sems, out_sems,
):
    features = tokens_ref.shape[1]
    width = weight_ref.shape[1]
    steps = features // CHUNK
    parts = 4
    loads = []
    for i in range(steps):
        at = pl.ds(i * CHUNK, CHUNK)
        pair = (
            pltpu.make_async_copy(tokens_hbm.at[:, at], tokens_ref.at[:, at], token_sems.at[i]),
            pltpu.make_async_copy(weight_hbm.at[at], weight_ref.at[at], weight_sems.at[i]),
        )
        for copy in pair:
            copy.start()
        loads.append(pair)
    stores = []
    for i in range(steps):
        for copy in loads[i]:
            copy.wait()
        at = slice(i * CHUNK, (i + 1) * CHUNK)
        for c in range(parts):
            cols = slice(c * width // parts, (c + 1) * width // parts)
            term = dot(tokens_ref[:, at], weight_ref[at, cols])
            if i == 0:
                total[:, cols] = term
            elif i < steps - 1:
                total[:, cols] += term
            else:
                out_ref[cols, :] = (total[:, cols] + term).astype(bf16).T
                rows = pl.ds(c * width // parts, width // parts)
                store = pltpu.make_async_copy(out_ref.at[rows], out_hbm.at[rows], out_sems.at[c])
                store.start()
                stores.append(store)
    for store in stores:
        store.wait()


def weights_kernel(own_hbm, *rest):
    pieces, (out_hbm, held_ref, sems, out_sems) = rest[:-4], rest[-4:]
    rows = own_hbm.shape[0]
    blocks, _, columns = out_hbm.shape
    group = where()[0]
    at = pl.ds(pl.multiple_of(group * (blocks * columns), columns), blocks * columns)
    pairs = [(own_hbm.at[:, at], held_ref.at[pl.ds(0, rows)])]
    for piece in pieces:
        size = piece.shape[0]
        pairs.append((piece, held_ref.at[pl.ds(rows, size)]))
        rows += size
    for copy in start_all(pairs, sems):
        copy.wait()
    stores = start_all(
        [(held_ref.at[:, pl.ds(b * columns, columns)], out_hbm.at[b]) for b in range(blocks)],
        out_sems,
    )
    for copy in stores:
        copy.wait()


def out_kernel(mixed_ref, weight_hbm, out_hbm, turned, weight_ref, out_ref, sems, out_sems):
    steps, _, columns = weight_ref.shape
    loads = start_all([(weight_hbm.at[i], weight_ref.at[i]) for i in range(steps)], sems)
    group, core, x, z = where()
    width = mixed_ref.shape[0]
    rows = width // 2
    size = rows // (2 * PIECES)
    own = mixed_ref[pl.ds(pl.multiple_of(group * rows, rows), rows), :]
    turned[:, :rows] = own.T
    pieces = []
    for half in (core, 1 - core):
        for k in held_pieces(x, z):
            start = (1 - group) * rows + (half * PIECES + k) * size
            pieces.append(mixed_ref[pl.ds(pl.multiple_of(start, size), size), :])
    turned[:, rows:] = jnp.concatenate(pieces, axis=0).T
    stores = []
    for i in range(steps):
        loads[i].wait()
        at = slice(i * columns, (i + 1) * columns)
        if i < steps - 1:
            out_ref[:, at] = dot(turned[...], weight_ref[i]).astype(bf16)
            if i % 2:
                stores.append((slice(None), pl.ds((i - 1) * columns, 2 * columns)))
            elif i == steps - 2:
                stores.append((slice(None), pl.ds(i * columns, columns)))
            else:
                continue
            start_store(out_ref, out_hbm, out_sems, stores)
            continue
        count = turned.shape[0] // LAST_PARTS
        for r in range(LAST_PARTS):
            part = slice(r * count, (r + 1) * count)
            out_ref[part, at] = dot(turned[part, :], weight_ref[i]).astype(bf16)
            stores.append((pl.ds(r * count, count), pl.ds(i * columns, columns)))
            start_store(out_ref, out_hbm, out_sems, stores)
    for i, span in enumerate(stores):
        pltpu.make_async_copy(out_ref.at[span], out_hbm.at[span], out_sems.at[i]).wait()


def start_store(out_ref, out_hbm, out_sems, stores):
    span = stores[-1]
    pltpu.make_async_copy(out_ref.at[span], out_hbm.at[span], out_sems.at[len(stores) - 1]).start()


def vmem(limit):
    return pltpu.CompilerParams(vmem_limit_bytes=limit * MIB)


def cost(flops, size):
    return pl.CostEstimate(flops=flops, bytes_accessed=size, transcendentals=0)


ANY = pl.BlockSpec(memory_space=pl.ANY)
SMEM = pl.BlockSpec(memory_space=pltpu.SMEM)
VMEM = pl.BlockSpec(memory_space=pltpu.VMEM)


def partners(move):
    def place(y, x, z, core):
        return (((y % 2 * 4 + x) * 4 + z) * 2 + core) * 2 + y // 2

    spots = [(y, x, z, c) for y in range(4) for x in range(4) for z in range(4) for c in range(2)]
    return [(place(*spot), place(*move(*spot))) for spot in spots]


def shards(tokens, in_weight, filter_taps, skip_gain, out_weight):
    ctx, ch = lax.axis_size("ctx"), lax.axis_size("ch")
    devices = ctx * ch
    position, features = tokens.shape
    width = in_weight.shape[1]
    channels = width // devices
    rows = out_weight.shape[0]
    table = jnp.asarray(tables(ctx, position))
    lanes = 128
    quarters = position // lanes
    both = ("ctx", "ch")
    across = partners(lambda y, x, z, c: (3 - y, x, z, c))
    other_core = partners(lambda y, x, z, c: (y, x, z, 1 - c))
    along_x = partners(lambda y, x, z, c: (y, x ^ 1, z, c))
    along_z = partners(lambda y, x, z, c: (y, x, z ^ 1, c))
    size = rows // (2 * PIECES)

    piece = jax.ShapeDtypeStruct((size, features), bf16)
    taps, first_piece = pl.pallas_call(
        prepare_kernel,
        in_specs=[ANY] * 2,
        out_specs=[ANY] * 2,
        out_shape=[jax.ShapeDtypeStruct((width // ch, position), bf16), piece],
        scratch_shapes=[
            pltpu.VMEM((position, width // ch), f32),
            pltpu.VMEM((width // ch, position), bf16),
            pltpu.VMEM(piece.shape, bf16),
            pltpu.SemaphoreType.DMA((3,)),
            pltpu.SemaphoreType.DMA((3,)),
        ],
        compiler_params=vmem(60),
        cost_estimate=cost(0, 2 * MIB),
    )(filter_taps, out_weight)
    mine = lax.ppermute(first_piece, both, across)
    taps = lax.all_to_all(
        taps.reshape(ctx, channels, position), "ctx", split_axis=0, concat_axis=0, tiled=True
    )

    partial_value = pl.pallas_call(
        project_kernel,
        in_specs=[ANY] * 2,
        out_specs=ANY,
        out_shape=jax.ShapeDtypeStruct((width, position), bf16),
        scratch_shapes=[
            pltpu.VMEM((position, features), bf16),
            pltpu.VMEM((features, width), bf16),
            pltpu.VMEM((position, width), f32),
            pltpu.VMEM((width, position), bf16),
            pltpu.SemaphoreType.DMA((features // CHUNK,)),
            pltpu.SemaphoreType.DMA((features // CHUNK,)),
            pltpu.SemaphoreType.DMA((4,)),
        ],
        compiler_params=vmem(60),
        cost_estimate=cost(2 * position * features * width, 14 * MIB),
    )(tokens, in_weight)
    partial_value = pl.pallas_call(
        fence_kernel,
        in_specs=[ANY] * 2,
        out_specs=ANY,
        out_shape=jax.ShapeDtypeStruct((width, position), bf16),
        input_output_aliases={0: 0},
        compiler_params=vmem(60),
        cost_estimate=cost(0, 0),
    )(partial_value, mine)
    parts = lax.all_to_all(
        partial_value.reshape(devices, channels, position),
        ("ch", "ctx"), split_axis=0, concat_axis=0, tiled=True,
    ).reshape(ch, ctx, channels, position)

    by_x = lax.ppermute(mine, both, along_x)
    by_z = lax.ppermute(mine, both, along_z)
    last_piece = pl.pallas_call(
        last_piece_kernel,
        in_specs=[ANY] * 2,
        out_specs=ANY,
        out_shape=piece,
        scratch_shapes=[pltpu.VMEM(piece.shape, bf16), pltpu.SemaphoreType.DMA((2,))],
        compiler_params=vmem(60),
        cost_estimate=cost(0, MIB),
    )(out_weight, partial_value)
    last = lax.ppermute(last_piece, both, across)
    pieces = [mine, by_z, by_x, last]
    pieces = pieces + [lax.ppermute(p, both, other_core) for p in pieces]

    lines = channels * 4 * ctx + 4 * TILE
    flat = (quarters, ctx * channels, lanes)
    held = [
        pltpu.VMEM(table.shape, f32),
        pltpu.VMEM((2, ctx + TILE, position), f32),
        pltpu.VMEM((3 * (position // 2), position // 2), bf16),
        pltpu.VMEM(flat, f32),
        pltpu.VMEM((channels, 2 * ctx, position), f32),
        pltpu.VMEM((lines, position), bf16),
        pltpu.VMEM((lines, position // 2), f32),
    ]
    spec = pl.pallas_call(
        spectrum_kernel,
        in_specs=[VMEM, ANY],
        out_specs=ANY,
        out_shape=jax.ShapeDtypeStruct((SPARE * lines, position // 2), f32),
        scratch_shapes=held + [pltpu.SemaphoreType.DMA((2,))],
        compiler_params=vmem(58),
        cost_estimate=cost(4 * 10**9, 4 * MIB),
    )(taps, table)
    mixed = pl.pallas_call(
        conv_kernel,
        in_specs=[SMEM, VMEM] + [ANY] * 2,
        out_specs=ANY,
        out_shape=jax.ShapeDtypeStruct((ch, ctx, channels, position), bf16),
        scratch_shapes=[
            pltpu.VMEM((lines, position // 2), f32),
            *held,
            pltpu.VMEM((channels, 4 * ctx, position), bf16),
            pltpu.VMEM(flat, f32),
            pltpu.VMEM((ctx, channels, position), bf16),
            pltpu.SemaphoreType.DMA((2,)),
            pltpu.SemaphoreType.DMA((4,)),
        ],
        compiler_params=vmem(40),
        cost_estimate=cost(8 * 10**9, 6 * MIB),
    )(skip_gain, parts, spec, table)

    mixed = lax.all_to_all(
        mixed.reshape(devices, channels, position),
        ("ch", "ctx"), split_axis=0, concat_axis=0, tiled=True,
    ).reshape(width, position)

    steps = features // 1024
    weights = pl.pallas_call(
        weights_kernel,
        in_specs=[ANY] * (1 + len(pieces)),
        out_specs=ANY,
        out_shape=jax.ShapeDtypeStruct((steps, width, features // steps), bf16),
        scratch_shapes=[
            pltpu.VMEM((width, features), bf16),
            pltpu.SemaphoreType.DMA((1 + len(pieces),)),
            pltpu.SemaphoreType.DMA((steps,)),
        ],
        compiler_params=vmem(60),
        cost_estimate=cost(0, 16 * MIB),
    )(out_weight, *pieces)

    return pl.pallas_call(
        out_kernel,
        in_specs=[VMEM, ANY],
        out_specs=ANY,
        out_shape=jax.ShapeDtypeStruct((position, features), bf16),
        scratch_shapes=[
            pltpu.VMEM((position, width), bf16),
            pltpu.VMEM((steps, width, features // steps), bf16),
            pltpu.VMEM((position, features), bf16),
            pltpu.SemaphoreType.DMA((steps,)),
            pltpu.SemaphoreType.DMA((steps + LAST_PARTS,)),
        ],
        compiler_params=vmem(48),
        cost_estimate=cost(2 * position * features * width, 13 * MIB),
    )(mixed, weights)


def solution(mesh):
    return jax.shard_map(
        shards,
        mesh=mesh,
        in_specs=(P("ctx", "ch"), P("ch", None), P("ctx", "ch"), P("ch"), P("ch", None)),
        out_specs=P("ctx", "ch"),
        check_vma=False,
    )
```

time: 96 us -> 89.7 us (0.934)
  Pallas kernels: 40.1 us -> 37.9 us
  local copies, waits for them, and re-layouts: 3.81 us -> 1.62 us
  waiting for transfers between devices: 21.8 us -> 20 us
    unnamed x22 -> x18, local copies, waits for them, and re-layouts: 3.81 us -> 1.62 us
    all_to_all x1, waiting for transfers between devices: 8.39 us -> 6.35 us  [shards(): lax.all_to_all(partial_value.reshape(devices, channels, position), ('ch',...]
    pallas_call x1, Pallas kernels: 9.08 us -> 7.59 us  [shards(): pl.pallas_call(out_kernel, in_specs=[VMEM, ANY], out_specs=ANY, out_shape...]
    pallas_call x4 -> x5, Pallas kernels: 23.7 us -> 23 us  [the longest x1 6.73 us: shards(): pl.pallas_call(weights_kernel, in_specs=[ANY] * (1 + len(pieces)), out_sp...]
  transfers between devices with their start and end apart: 11 -> 11, of which waited for: 6 -> 6; matrix products, arithmetic and copies ran while one was open for 0% -> 0% of each run, Pallas kernels for 30% -> 31%
where the time goes in v3:
time: 89.7 us; the launch traced here: 89.3 us
  Pallas kernels  37.9 us (42%)
  starting transfers between devices  29.5 us (33%)
  waiting for transfers between devices  20 us (22%)
  local copies, waits for them, and re-layouts  1.62 us (2%)
    all_to_all x1, starting transfers between devices, shards(): lax.all_to_all(taps.reshape(ctx, channels, position), 'ctx', split_axis=0...  9.28 us
    pallas_call x1, Pallas kernels, shards(): pl.pallas_call(out_kernel, in_specs=[VMEM, ANY], out_specs=ANY, out_shape...  7.59 us
    pallas_call x1, Pallas kernels, shards(): pl.pallas_call(project_kernel, in_specs=[ANY] * 2, out_specs=ANY, out_sha...  7.31 us
    pallas_call x1, Pallas kernels, shards(): pl.pallas_call(weights_kernel, in_specs=[ANY] * (1 + len(pieces)), out_sp...  6.73 us
    pallas_call x1, Pallas kernels, shards(): pl.pallas_call(conv_kernel, in_specs=[SMEM, VMEM] + [ANY] * 2, out_specs=...  6.56 us
    all_to_all x1, waiting for transfers between devices, shards(): lax.all_to_all(mixed.reshape(devices, channels, position), ('ch', 'ctx'),...  6.45 us
    all_to_all x1, waiting for transfers between devices, shards(): lax.all_to_all(partial_value.reshape(devices, channels, position), ('ch',...  6.35 us
    pallas_call x1, Pallas kernels, shards(): pl.pallas_call(spectrum_kernel, in_specs=[VMEM, ANY], out_specs=ANY, out_...  5.42 us
  transfers between devices with their start and end apart: 11, of which 6 were waited for; matrix products, arithmetic and copies ran while one was open for 0% of the time, Pallas kernels for 31%

profile of v3, /device:TPU:1, one launch (start us, length us, event | category | flops | bytes accessed | tf_op | source)
XLA Modules:
  0.0 89.3 jit_solution(8831537336888002331)
XLA Ops:
  0.0 2.3 %shard_map.65 = (bf16[512,512]{1,0:T(8,128)(2,1)}, bf16[64,4096]{1,0:T(8,128)(2,1)}) custom-call(f32[512,512]{1,0:T(8,128)} %taps_hbm.1, bf16[512,8192]{1,0:T(8,128)(2,1)} %own_hbm.1), custom_call_target="tpu_custom_call" | custom-call | bytes 2097152 | tf_op jit(solution)/shard_map/pallas_call | solution.py:501
  2.3 3.6 %collective-permute-start = (bf16[64,4096]{1,0:T(8,128)(2,1)}, bf16[64,4096]{1,0:T(8,128)(2,1)S(1)}, u32[]{:S(2)}, u32[]{:S(2)}) collective-permute-start(bf16[64,4096]{1,0:T(8,128)(2,1)} %get-tuple-element.7), channel_id=1, source_target_pairs={{0,65},{2,67},{4,69},{6,71},{8,73},{10,75},{12,77},{14,79},{16,81}... | collective-permute-start | bytes 1572872 | tf_op jit(solution)/shard_map/ppermute | solution.py:516
  5.9 9.3 %all-to-all-start.1 = ((bf16[64,8,512]{2,1,0:T(8,128)(2,1)}), bf16[64,8,512]{2,1,0:T(8,128)(2,1)S(1)}, u32[]{:S(2)}, u32[]{:S(2)}) async-start(bf16[64,8,512]{2,1,0:T(8,128)(2,1)} %bitcast.8), calls=%async_computation.1 | async-start | bytes 1048576 | tf_op jit(solution)/shard_map/all_to_all | solution.py:517
  15.2 7.3 %shard_map.64.value_ref = bf16[1024,512]{1,0:T(8,128)(2,1)} custom-call(bf16[512,4096]{1,0:T(8,128)(2,1)} %tokens_hbm.1, bf16[4096,1024]{1,0:T(8,128)(2,1)} %weight_hbm.3), custom_call_target="tpu_custom_call" | custom-call | flops 4294967296 | bytes 14680064 | tf_op jit(solution)/shard_map/pallas_call | solution.py:521
  22.5 0.0 collective-permute-done.after_ref.rest_0_
  22.5 0.0 copy-start.2
  22.5 0.8 copy-done.2
  23.3 3.8 %all-to-all-done.1.taps_ref = bf16[64,8,512]{2,1,0:T(8,128)(2,1)S(1)} async-done(((bf16[64,8,512]{2,1,0:T(8,128)(2,1)}), bf16[64,8,512]{2,1,0:T(8,128)(2,1)S(1)}, u32[]{:S(2)}, u32[]{:S(2)}) %all-to-all-start.1) | async-done | bytes 524320 | tf_op jit(solution)/shard_map/all_to_all | solution.py:517
  27.1 0.0 copy-start.4
  27.2 4.1 %all-to-all-start = ((bf16[128,8,512]{2,1,0:T(8,128)(2,1)}), bf16[128,8,512]{2,1,0:T(8,128)(2,1)S(1)}, u32[]{:S(2)}, u32[]{:S(2)}) async-start(bf16[128,8,512]{2,1,0:T(8,128)(2,1)} %bitcast.7), calls=%async_computation | async-start | bytes 2097152 | tf_op jit(solution)/shard_map/all_to_all | solution.py:547
  31.3 0.0 copy-done.4
  31.3 5.4 %shard_map.67.spec_hbm = f32[25344,256]{1,0:T(8,128)} custom-call(bf16[64,8,512]{2,1,0:T(8,128)(2,1)} %copy-done.4, f32[1224,256]{1,0:T(8,128)} %constant.2.clone.table_hbm), custom_call_target="tpu_custom_call" | custom-call | flops 4000000000 | bytes 4194304 | tf_op jit(solution)/shard_map/pallas_call | solution.py:578
  36.7 0.0 copy-start.3
  36.7 0.0 copy-start
  36.7 0.0 copy-start.1
  36.7 2.0 %shard_map.69 = bf16[64,4096]{1,0:T(8,128)(2,1)} custom-call(bf16[512,8192]{1,0:T(8,128)(2,1)} %own_hbm.1, bf16[1024,512]{1,0:T(8,128)(2,1)} %shard_map.66.after_ref), custom_call_target="tpu_custom_call" | custom-call | bytes 1048576 | tf_op jit(solution)/shard_map/pallas_call | solution.py:554
  38.7 2.7 %collective-permute-start.3 = (bf16[64,4096]{1,0:T(8,128)(2,1)}, bf16[64,4096]{1,0:T(8,128)(2,1)S(1)}, u32[]{:S(2)}, u32[]{:S(2)}) collective-permute-start(bf16[64,4096]{1,0:T(8,128)(2,1)} %shard_map.69), channel_id=1, source_target_pairs={{0,65},{2,67},{4,69},{6,71},{8,73},{10,75},{12,77},{14,79},{16,81}... | collective-permute-start | bytes 1572872 | tf_op jit(solution)/shard_map/ppermute | solution.py:563
  41.5 0.0 copy-done.3
  41.5 1.4 %collective-permute-start.1 = (bf16[64,4096]{1,0:T(8,128)(2,1)S(1)}, bf16[64,4096]{1,0:T(8,128)(2,1)}, u32[]{:S(2)}, u32[]{:S(2)}) collective-permute-start(bf16[64,4096]{1,0:T(8,128)(2,1)S(1)} %copy-done.3), channel_id=1, source_target_pairs={{0,4},{2,6},{4,0},{6,2},{8,12},{10,14},{12,8},{14,10},{16,20},{18,... | collective-permute-start | bytes 1572872 | tf_op jit(solution)/shard_map/ppermute | solution.py:553
  42.9 1.2 %collective-permute-start.2 = (bf16[64,4096]{1,0:T(8,128)(2,1)S(1)}, bf16[64,4096]{1,0:T(8,128)(2,1)}, u32[]{:S(2)}, u32[]{:S(2)}) collective-permute-start(bf16[64,4096]{1,0:T(8,128)(2,1)S(1)} %copy-done.3), channel_id=1, source_target_pairs={{0,16},{2,18},{4,20},{6,22},{8,24},{10,26},{12,28},{14,30},{16,0},... | collective-permute-start | bytes 1572872 | tf_op jit(solution)/shard_map/ppermute | solution.py:552
  44.1 6.3 %all-to-all-done = bf16[128,8,512]{2,1,0:T(8,128)(2,1)S(1)} async-done(((bf16[128,8,512]{2,1,0:T(8,128)(2,1)}), bf16[128,8,512]{2,1,0:T(8,128)(2,1)S(1)}, u32[]{:S(2)}, u32[]{:S(2)}) %all-to-all-start) | async-done | bytes 1048608 | tf_op jit(solution)/shard_map/all_to_all | solution.py:547
  50.5 0.0 copy-done
  50.5 0.0 copy-done.1
  50.5 6.6 %shard_map.68 = bf16[2,64,8,512]{3,2,1,0:T(8,128)(2,1)} custom-call(f32[512]{0:T(512)S(1)} %copy-done.1, bf16[2,64,8,512]{3,2,1,0:T(8,128)(2,1)S(1)} %bitcast.6, f32[25344,256]{1,0:T(8,128)} %shard_map.67.spec_hbm, f32[1224,256]{1,0:T(8,128)S(1)} %copy-done), custom_call_target="tpu_custom_call" | custom-call | flops 8000000000 | bytes 6291456 | tf_op jit(solution)/shard_map/pallas_call | solution.py:587
  57.1 5.2 %all-to-all-start.2 = ((bf16[128,8,512]{2,1,0:T(8,128)(2,1)}), bf16[128,8,512]{2,1,0:T(8,128)(2,1)S(1)}, u32[]{:S(2)}, u32[]{:S(2)}) async-start(bf16[128,8,512]{2,1,0:T(8,128)(2,1)} %bitcast.3), calls=%async_computation.2 | async-start | bytes 2097152 | tf_op jit(solution)/shard_map/all_to_all | solution.py:605
  62.2 1.3 %collective-permute-start.4 = (bf16[64,4096]{1,0:T(8,128)(2,1)S(1)}, bf16[64,4096]{1,0:T(8,128)(2,1)S(1)}, u32[]{:S(2)}, u32[]{:S(2)}) collective-permute-start(bf16[64,4096]{1,0:T(8,128)(2,1)S(1)} %copy-done.3), channel_id=1, source_target_pairs={{0,2},{2,0},{4,6},{6,4},{8,10},{10,8},{12,14},{14,12},{16,18},{18,... | collective-permute-start | bytes 1572872 | tf_op jit(solution)/shard_map/ppermute | solution.py:565
  63.5 0.0 collective-permute-done.1.rest_1_
  63.5 0.1 collective-permute-start.5
  63.6 0.0 collective-permute-done.2.rest_2_
  63.6 0.4 collective-permute-start.6
  64.0 0.0 collective-permute-done.3.rest_3_
  64.0 0.0 copy-start.5
  64.0 0.1 collective-permute-start.7
  64.1 0.9 %collective-permute-done.4.rest_4_ = bf16[64,4096]{1,0:T(8,128)(2,1)S(1)} collective-permute-done((bf16[64,4096]{1,0:T(8,128)(2,1)S(1)}, bf16[64,4096]{1,0:T(8,128)(2,1)S(1)}, u32[]{:S(2)}, u32[]{:S(2)}) %collective-permute-start.4) | collective-permute-done | bytes 524320 | tf_op jit(solution)/shard_map/ppermute | solution.py:565
  65.0 0.0 copy-start.6
  65.0 1.7 %collective-permute-done.5.rest_5_ = bf16[64,4096]{1,0:T(8,128)(2,1)S(1)} collective-permute-done((bf16[64,4096]{1,0:T(8,128)(2,1)}, bf16[64,4096]{1,0:T(8,128)(2,1)S(1)}, u32[]{:S(2)}, u32[]{:S(2)}) %collective-permute-start.5) | collective-permute-done | bytes 524320 | tf_op jit(solution)/shard_map/ppermute | solution.py:565
  66.8 0.0 copy-start.7
  66.8 0.7 collective-permute-done.6.rest_6_
  67.5 0.0 copy-start.8
  67.5 0.0 collective-permute-done.7.rest_7_
  67.5 0.0 copy-done.5
  67.5 0.0 copy-done.6
  67.5 0.0 copy-done.7
  67.6 0.8 copy-done.8
  68.3 6.7 %shard_map.70.weight_hbm = bf16[4,1024,1024]{2,1,0:T(8,128)(2,1)} custom-call(bf16[512,8192]{1,0:T(8,128)(2,1)} %own_hbm.1, bf16[64,4096]{1,0:T(8,128)(2,1)} %copy-done.2, bf16[64,4096]{1,0:T(8,128)(2,1)} %collective-permute-done.1.rest_1_, bf16[64,4096]{1,0:T(8,128)(2,1)} %collective-permute-done.2.rest_2_, bf16[64,4096]{1,0:T(8,128)(2,1)} %copy-done.5, ...), custom_call_target="tpu_custom_call" | custom-call | bytes 16777216 | tf_op jit(solution)/shard_map/pallas_call | solution.py:611
  75.1 6.5 %all-to-all-done.2 = bf16[128,8,512]{2,1,0:T(8,128)(2,1)S(1)} async-done(((bf16[128,8,512]{2,1,0:T(8,128)(2,1)}), bf16[128,8,512]{2,1,0:T(8,128)(2,1)S(1)}, u32[]{:S(2)}, u32[]{:S(2)}) %all-to-all-start.2) | async-done | bytes 1048608 | tf_op jit(solution)/shard_map/all_to_all | solution.py:605
  81.5 7.6 %shard_map.71 = bf16[512,4096]{1,0:T(8,128)(2,1)} custom-call(bf16[1024,512]{1,0:T(8,128)(2,1)S(1)} %bitcast.5, bf16[4,1024,1024]{2,1,0:T(8,128)(2,1)} %shard_map.70.weight_hbm), custom_call_target="tpu_custom_call" | custom-call | flops 4294967296 | bytes 13631488 | tf_op jit(solution)/shard_map/pallas_call | solution.py:625
  (1 shorter events, 0.0 us)
Async XLA Ops:
  2.3 20.3 %collective-permute-start = (bf16[64,4096]{1,0:T(8,128)(2,1)}, bf16[64,4096]{1,0:T(8,128)(2,1)S(1)}, u32[]{:S(2)}, u32[]{:S(2)}) collective-permute-start(bf16[64,4096]{1,0:T(8,128)(2,1)} %get-tuple-element.7), channel_id=1, source_target_pairs={{0,65},{2,67},{4,69},{6,71},{8,73},{10,75},{12,77},{14,79},{16,81}... | collective-permute-start | bytes 1572872 | tf_op jit(solution)/shard_map/ppermute | solution.py:516
  5.9 21.2 %all-to-all-start.1 = ((bf16[64,8,512]{2,1,0:T(8,128)(2,1)}), bf16[64,8,512]{2,1,0:T(8,128)(2,1)S(1)}, u32[]{:S(2)}, u32[]{:S(2)}) async-start(bf16[64,8,512]{2,1,0:T(8,128)(2,1)} %bitcast.8), calls=%async_computation.1 | async-start | bytes 1048576 | tf_op jit(solution)/shard_map/all_to_all | solution.py:517
  22.5 0.8 copy-start.2
  27.1 4.1 %copy-start.4 = (bf16[64,8,512]{2,1,0:T(8,128)(2,1)}, bf16[64,8,512]{2,1,0:T(8,128)(2,1)S(1)}, u32[]{:S(2)}) copy-start(bf16[64,8,512]{2,1,0:T(8,128)(2,1)S(1)} %all-to-all-done.1.taps_ref) | copy-start | bytes 1572868
  27.2 23.3 %all-to-all-start = ((bf16[128,8,512]{2,1,0:T(8,128)(2,1)}), bf16[128,8,512]{2,1,0:T(8,128)(2,1)S(1)}, u32[]{:S(2)}, u32[]{:S(2)}) async-start(bf16[128,8,512]{2,1,0:T(8,128)(2,1)} %bitcast.7), calls=%async_computation | async-start | bytes 2097152 | tf_op jit(solution)/shard_map/all_to_all | solution.py:547
  36.7 4.8 %copy-start.3 = (bf16[64,4096]{1,0:T(8,128)(2,1)S(1)}, bf16[64,4096]{1,0:T(8,128)(2,1)}, u32[]{:S(2)}) copy-start(bf16[64,4096]{1,0:T(8,128)(2,1)} %copy-done.2) | copy-start | bytes 1572868
  36.7 13.8 %copy-start = (f32[1224,256]{1,0:T(8,128)S(1)}, f32[1224,256]{1,0:T(8,128)}, u32[]{:S(2)}) copy-start(f32[1224,256]{1,0:T(8,128)} %constant.2.clone.table_hbm) | copy-start | bytes 3760132
  36.7 13.8 %copy-start.1 = (f32[512]{0:T(512)S(1)}, f32[512]{0:T(512)}, u32[]{:S(2)}) copy-start(f32[512]{0:T(512)} %gain_ref.1) | copy-start | bytes 6148
  38.7 25.3 %collective-permute-start.3 = (bf16[64,4096]{1,0:T(8,128)(2,1)}, bf16[64,4096]{1,0:T(8,128)(2,1)S(1)}, u32[]{:S(2)}, u32[]{:S(2)}) collective-permute-start(bf16[64,4096]{1,0:T(8,128)(2,1)} %shard_map.69), channel_id=1, source_target_pairs={{0,65},{2,67},{4,69},{6,71},{8,73},{10,75},{12,77},{14,79},{16,81}... | collective-permute-start | bytes 1572872 | tf_op jit(solution)/shard_map/ppermute | solution.py:563
  41.5 22.0 %collective-permute-start.1 = (bf16[64,4096]{1,0:T(8,128)(2,1)S(1)}, bf16[64,4096]{1,0:T(8,128)(2,1)}, u32[]{:S(2)}, u32[]{:S(2)}) collective-permute-start(bf16[64,4096]{1,0:T(8,128)(2,1)S(1)} %copy-done.3), channel_id=1, source_target_pairs={{0,4},{2,6},{4,0},{6,2},{8,12},{10,14},{12,8},{14,10},{16,20},{18,... | collective-permute-start | bytes 1572872 | tf_op jit(solution)/shard_map/ppermute | solution.py:553
  42.9 20.7 %collective-permute-start.2 = (bf16[64,4096]{1,0:T(8,128)(2,1)S(1)}, bf16[64,4096]{1,0:T(8,128)(2,1)}, u32[]{:S(2)}, u32[]{:S(2)}) collective-permute-start(bf16[64,4096]{1,0:T(8,128)(2,1)S(1)} %copy-done.3), channel_id=1, source_target_pairs={{0,16},{2,18},{4,20},{6,22},{8,24},{10,26},{12,28},{14,30},{16,0},... | collective-permute-start | bytes 1572872 | tf_op jit(solution)/shard_map/ppermute | solution.py:552
  57.1 24.5 %all-to-all-start.2 = ((bf16[128,8,512]{2,1,0:T(8,128)(2,1)}), bf16[128,8,512]{2,1,0:T(8,128)(2,1)S(1)}, u32[]{:S(2)}, u32[]{:S(2)}) async-start(bf16[128,8,512]{2,1,0:T(8,128)(2,1)} %bitcast.3), calls=%async_computation.2 | async-start | bytes 2097152 | tf_op jit(solution)/shard_map/all_to_all | solution.py:605
  62.2 2.8 %collective-permute-start.4 = (bf16[64,4096]{1,0:T(8,128)(2,1)S(1)}, bf16[64,4096]{1,0:T(8,128)(2,1)S(1)}, u32[]{:S(2)}, u32[]{:S(2)}) collective-permute-start(bf16[64,4096]{1,0:T(8,128)(2,1)S(1)} %copy-done.3), channel_id=1, source_target_pairs={{0,2},{2,0},{4,6},{6,4},{8,10},{10,8},{12,14},{14,12},{16,18},{18,... | collective-permute-start | bytes 1572872 | tf_op jit(solution)/shard_map/ppermute | solution.py:565
  63.5 3.2 %collective-permute-start.5 = (bf16[64,4096]{1,0:T(8,128)(2,1)}, bf16[64,4096]{1,0:T(8,128)(2,1)S(1)}, u32[]{:S(2)}, u32[]{:S(2)}) collective-permute-start(bf16[64,4096]{1,0:T(8,128)(2,1)} %collective-permute-done.1.rest_1_), channel_id=1, source_target_pairs={{0,2},{2,0},{4,6},{6,4},{8,10},{10,8},{12,14},{14,12},{16,18},{18,... | collective-permute-start | bytes 1572872 | tf_op jit(solution)/shard_map/ppermute | solution.py:565
  63.6 3.9 %collective-permute-start.6 = (bf16[64,4096]{1,0:T(8,128)(2,1)}, bf16[64,4096]{1,0:T(8,128)(2,1)S(1)}, u32[]{:S(2)}, u32[]{:S(2)}) collective-permute-start(bf16[64,4096]{1,0:T(8,128)(2,1)} %collective-permute-done.2.rest_2_), channel_id=1, source_target_pairs={{0,2},{2,0},{4,6},{6,4},{8,10},{10,8},{12,14},{14,12},{16,18},{18,... | collective-permute-start | bytes 1572872 | tf_op jit(solution)/shard_map/ppermute | solution.py:565
  64.0 3.5 %copy-start.5 = (bf16[64,4096]{1,0:T(8,128)(2,1)}, bf16[64,4096]{1,0:T(8,128)(2,1)S(1)}, u32[]{:S(2)}) copy-start(bf16[64,4096]{1,0:T(8,128)(2,1)S(1)} %collective-permute-done.3.rest_3_) | copy-start | bytes 1572868
  64.0 3.5 %collective-permute-start.7 = (bf16[64,4096]{1,0:T(8,128)(2,1)S(1)}, bf16[64,4096]{1,0:T(8,128)(2,1)}, u32[]{:S(2)}, u32[]{:S(2)}) collective-permute-start(bf16[64,4096]{1,0:T(8,128)(2,1)S(1)} %collective-permute-done.3.rest_3_), channel_id=1, source_target_pairs={{0,2},{2,0},{4,6},{6,4},{8,10},{10,8},{12,14},{14,12},{16,18},{18,... | collective-permute-start | bytes 1572872 | tf_op jit(solution)/shard_map/ppermute | solution.py:565
  65.0 2.5 %copy-start.6 = (bf16[64,4096]{1,0:T(8,128)(2,1)}, bf16[64,4096]{1,0:T(8,128)(2,1)S(1)}, u32[]{:S(2)}) copy-start(bf16[64,4096]{1,0:T(8,128)(2,1)S(1)} %collective-permute-done.4.rest_4_) | copy-start | bytes 1572868
  66.8 0.8 copy-start.7
  67.5 0.8 copy-start.8

commit v4 on v3

--- a/solution.py
+++ b/solution.py
@@ -57,21 +57,25 @@
     )
 
 
-def unpack(table_ref, blocks, line_ref, twist_ref):
+def unpack(table_ref, blocks, line_ref):
     columns = line_ref.shape[1]
-    line_ref[:columns] = table_ref[:columns].astype(bf16)
-    line_ref[columns:] = table_ref[: 2 * columns].astype(bf16)
+    line_ref[:columns] = table_ref[:columns, :].astype(bf16)
+    line_ref[columns:] = table_ref[: 2 * columns, :].astype(bf16)
     at = 2 * columns
     leads = []
     for use in (3 * blocks, 2 * blocks, 4 * blocks):
         leads.append(table_ref[at : at + 2 * blocks, :use].astype(bf16))
         at += 2 * blocks
-    rows = twist_ref.shape[1]
-    for i in range(2):
-        for k in range(2):
-            twist_ref[i, :, columns * k : columns * (k + 1)] = table_ref[at : at + rows]
-            at += rows
-    return (*leads, table_ref[at : at + 8, : columns // 2])
+    rows = blocks + TILE
+    quarter = columns // 2
+
+    def twist(first, p):
+        lanes = slice(quarter * (p % 2), quarter * (p % 2 + 1))
+        start = at + p // 2 * rows + first
+        return [table_ref[start + 2 * i * rows : start + 2 * i * rows + TILE, lanes] for i in range(2)]
+
+    end = at + 4 * rows
+    return (*leads, table_ref[end : end + 8, :quarter], twist)
 
 
 def dot(a, b):
@@ -109,12 +113,12 @@
     return both + dot(rows_ref[span, :size], line_ref[2 * size :, :])
 
 
-def spread(real, imag, freqs, rows_ref, at, twist_ref, fold):
+def spread(real, imag, first, rows_ref, at, twist, fold):
     quarter = real.shape[1] // 4
     parts = []
     for p in range(4):
         lanes = slice(quarter * p, quarter * (p + 1))
-        cos, sin = twist_ref[0, freqs, lanes], twist_ref[1, freqs, lanes]
+        cos, sin = twist(first, p)
         if imag is None:
             parts.append((real[:, lanes] * cos, -real[:, lanes] * sin))
         else:
@@ -125,7 +129,7 @@
         put_rows(rows_ref, at + TILE * r, jnp.concatenate([a, b], axis=1))
 
 
-def gather_back(back_ref, at, freqs, twist_ref, fold):
+def gather_back(back_ref, at, first, twist, fold):
     quarter = back_ref.shape[1] // 2
     got = []
     for r in range(4):
@@ -136,8 +140,7 @@
         got.append((a, b))
     reals, imags = [], []
     for p, (a, b) in enumerate(butterfly(got)):
-        lanes = slice(quarter * p, quarter * (p + 1))
-        a, b = turn_back(a, b, twist_ref[0, freqs, lanes], twist_ref[1, freqs, lanes])
+        a, b = turn_back(a, b, *twist(first, p))
         reals.append(a)
         imags.append(b)
     return jnp.concatenate(reals, axis=1), jnp.concatenate(imags, axis=1)
@@ -160,23 +163,22 @@
     return copies
 
 
-def forward(load, last, lead, lines_ref, rows_ref, spec_ref, twist_ref, fold, line_ref):
+def forward(load, last, lead, lines_ref, rows_ref, spec_ref, twist, fold, line_ref):
     channels = lines_ref.shape[0]
     blocks = lines_ref.shape[1] // 2
     tiles = blocks // TILE
     size = blocks * 4
     end = channels * size
-    spread(last, None, pl.ds(blocks, TILE), rows_ref, end, twist_ref, fold)
+    spread(last, None, blocks, rows_ref, end, twist, fold)
     for step in range(channels // GROUP):
         held = range(GROUP * step, GROUP * (step + 1))
         for c in held:
             lines_ref[c] = dot(lead, load(c))
         for c in held:
             for t in range(tiles):
-                freqs = pl.ds(TILE * t, TILE)
-                real = lines_ref[c, freqs, :]
+                real = lines_ref[c, pl.ds(TILE * t, TILE), :]
                 imag = lines_ref[c, pl.ds(blocks + TILE * t, TILE), :]
-                spread(real, imag, freqs, rows_ref, c * size + 4 * TILE * t, twist_ref, fold)
+                spread(real, imag, TILE * t, rows_ref, c * size + 4 * TILE * t, twist, fold)
         count = GROUP * size + (4 * TILE if step == channels // GROUP - 1 else 0)
         spec_ref[pl.ds(GROUP * size * step, count), :] = transform_rows(
             rows_ref, GROUP * size * step, count, line_ref
@@ -203,7 +205,7 @@
 
 def spectrum_kernel(
     taps_ref, table_hbm, spec_hbm,
-    table_ref, twist_ref, line_ref, flat, lines_ref, rows_ref, spec_ref, sems,
+    table_ref, line_ref, flat, lines_ref, rows_ref, spec_ref, sems,
 ):
     blocks, channels, _ = taps_ref.shape
     copies = start_all([(table_hbm, table_ref)], sems)
@@ -217,16 +219,16 @@
         value = channel_of(flat, c, blocks, channels).astype(bf16)
         return jnp.concatenate([value, value], axis=0)
 
-    _, lead, _, fold = unpack(table_ref, blocks, line_ref, twist_ref)
-    forward(load, last, lead, lines_ref, rows_ref, spec_ref, twist_ref, fold, line_ref)
+    _, lead, _, fold, twist = unpack(table_ref, blocks, line_ref)
+    forward(load, last, lead, lines_ref, rows_ref, spec_ref, twist, fold, line_ref)
     copy = pltpu.make_async_copy(spec_ref, spec_hbm.at[pl.ds(0, spec_ref.shape[0])], sems.at[1])
     copy.start()
     copy.wait()
 
 
 def conv_kernel(
-    gain_ref, parts_ref, spec_hbm, table_hbm, out_hbm,
-    taps_spec_ref, table_ref, twist_ref, line_ref,
+    gain_ref, parts_ref, spec_hbm, table_ref, out_hbm,
+    taps_spec_ref, line_ref,
     flat, lines_ref, rows_ref, spec_ref, packed_ref, mixed_ref, out_ref, sems, out_sems,
 ):
     _, blocks, channels, width = parts_ref.shape
@@ -236,19 +238,18 @@
     tiles = blocks // TILE
     size = blocks * 4
     half = blocks // 2
-    copies = start_all([(table_hbm, table_ref), (spec_hbm.at[pl.ds(0, taps_spec_ref.shape[0])], taps_spec_ref)], sems)
+    copies = start_all([(spec_hbm.at[pl.ds(0, taps_spec_ref.shape[0])], taps_spec_ref)], sems)
     total = parts_ref[0].astype(f32) + parts_ref[1].astype(f32)
     fill(flat, total)
     last = alternating(total)
-    copies[0].wait()
-    lead, _, tail, fold = unpack(table_ref, blocks, line_ref, twist_ref)
+    lead, _, tail, fold, twist = unpack(table_ref, blocks, line_ref)
 
     def load(c):
         high, low = split(channel_of(flat, c, blocks, channels))
         return jnp.concatenate([high, low, high], axis=0)
 
-    forward(load, last, lead, lines_ref, rows_ref, spec_ref, twist_ref, fold, line_ref)
-    copies[1].wait()
+    forward(load, last, lead, lines_ref, rows_ref, spec_ref, twist, fold, line_ref)
+    copies[0].wait()
 
     def multiply(at, gain):
         span = pl.ds(at, 4 * TILE)
@@ -270,7 +271,7 @@
         all_gains = jnp.where(row == c, gain[c], all_gains)
     multiply(end, all_gains)
     spec_ref[pl.ds(end, 4 * TILE), :] = transform_rows(rows_ref, end, 4 * TILE, line_ref)
-    last, _ = gather_back(spec_ref, end, pl.ds(blocks, TILE), twist_ref, fold)
+    last, _ = gather_back(spec_ref, end, blocks, twist, fold)
     first_row = lax.broadcasted_iota(jnp.int32, (TILE, width), 0) == 0
     for step in range(channels // GROUP):
         held = range(GROUP * step, GROUP * (step + 1))
@@ -281,19 +282,18 @@
         spec_ref[pl.ds(at, GROUP * size), :] = transform_rows(rows_ref, at, GROUP * size, line_ref)
         for c in held:
             for t in range(tiles):
-                real, imag = gather_back(
-                    spec_ref, c * size + 4 * TILE * t, pl.ds(TILE * t, TILE), twist_ref, fold
-                )
+                real, imag = gather_back(spec_ref, c * size + 4 * TILE * t, TILE * t, twist, fold)
                 if t == 0:
                     imag = jnp.where(first_row, last[c : c + 1], imag)
                 for at, part in ((TILE * t, real), (blocks + TILE * t, imag)):
                     high, low = split(part)
                     packed_ref[c, pl.ds(at, TILE), :] = high
                     packed_ref[c, pl.ds(2 * blocks + at, TILE), :] = low
-            both = dot(tail, packed_ref[c])
-            value = both[:blocks] + both[blocks:]
-            for q in range(quarters):
-                mixed_ref[q, pl.ds(c, blocks, stride=channels), :] = value[:, lanes * q : lanes * (q + 1)]
+    for c in range(channels):
+        both = dot(tail, packed_ref[c])
+        value = both[:blocks] + both[blocks:]
+        for q in range(quarters):
+            mixed_ref[q, pl.ds(c, blocks, stride=channels), :] = value[:, lanes * q : lanes * (q + 1)]
     stores = []
     for i in range(2):
         span = pl.ds(half * i, half)
@@ -313,19 +313,19 @@
     taps_hbm, weight_hbm, out_hbm, piece_hbm, taps_ref, out_ref, piece_ref, sems, out_sems
 ):
     steps = sems.shape[0] - 1
-    size = taps_ref.shape[1] // steps
+    size = taps_ref.shape[0] // steps
     spans = [pl.ds(i * size, size) for i in range(steps)]
     loads = start_all(
-        [(taps_hbm.at[:, s], taps_ref.at[:, s]) for s in spans]
+        [(taps_hbm.at[s], taps_ref.at[s]) for s in spans]
         + [(piece_source(weight_hbm, piece_hbm, 0), piece_ref)],
         sems,
     )
+    for load in loads[:steps]:
+        load.wait()
     stores = []
-    for i in range(steps):
-        loads[i].wait()
-        at = slice(i * size, (i + 1) * size)
-        out_ref[at, :] = taps_ref[:, at].astype(bf16).T
-        stores.append(pltpu.make_async_copy(out_ref.at[spans[i]], out_hbm.at[spans[i]], out_sems.at[i]))
+    for i, span in enumerate(spans):
+        out_ref[span, :] = taps_ref[:, i * size : (i + 1) * size].astype(bf16).T
+        stores.append(pltpu.make_async_copy(out_ref.at[span], out_hbm.at[span], out_sems.at[i]))
         stores[-1].start()
     loads[steps].wait()
     stores.append(pltpu.make_async_copy(piece_ref, piece_hbm, out_sems.at[steps]))
@@ -417,10 +417,11 @@
 
 def out_kernel(mixed_ref, weight_hbm, out_hbm, turned, weight_ref, out_ref, sems, out_sems):
     steps, _, columns = weight_ref.shape
-    loads = start_all([(weight_hbm.at[i], weight_ref.at[i]) for i in range(steps)], sems)
-    group, core, x, z = where()
     width = mixed_ref.shape[0]
     rows = width // 2
+    parts = [(0, pl.ds(0, rows)), (0, pl.ds(rows, rows)), *range(1, steps)]
+    loads = start_all([(weight_hbm.at[i], weight_ref.at[i]) for i in parts], sems)
+    group, core, x, z = where()
     size = rows // (2 * PIECES)
     own = mixed_ref[pl.ds(pl.multiple_of(group * rows, rows), rows), :]
     turned[:, :rows] = own.T
@@ -430,9 +431,13 @@
             start = (1 - group) * rows + (half * PIECES + k) * size
             pieces.append(mixed_ref[pl.ds(pl.multiple_of(start, size), size), :])
     turned[:, rows:] = jnp.concatenate(pieces, axis=0).T
+    loads[0].wait()
+    own_part = dot(turned[:, :rows], weight_ref[0, :rows])
+    loads[1].wait()
+    out_ref[:, :columns] = (own_part + dot(turned[:, rows:], weight_ref[0, rows:])).astype(bf16)
     stores = []
-    for i in range(steps):
-        loads[i].wait()
+    for i in range(1, steps):
+        loads[i + 1].wait()
         at = slice(i * columns, (i + 1) * columns)
         if i < steps - 1:
             out_ref[:, at] = dot(turned[...], weight_ref[i]).astype(bf16)
@@ -507,8 +512,8 @@
             pltpu.VMEM((position, width // ch), f32),
             pltpu.VMEM((width // ch, position), bf16),
             pltpu.VMEM(piece.shape, bf16),
-            pltpu.SemaphoreType.DMA((3,)),
-            pltpu.SemaphoreType.DMA((3,)),
+            pltpu.SemaphoreType.DMA((5,)),
+            pltpu.SemaphoreType.DMA((5,)),
         ],
         compiler_params=vmem(60),
         cost_estimate=cost(0, 2 * MIB),
@@ -567,8 +572,6 @@
     lines = channels * 4 * ctx + 4 * TILE
     flat = (quarters, ctx * channels, lanes)
     held = [
-        pltpu.VMEM(table.shape, f32),
-        pltpu.VMEM((2, ctx + TILE, position), f32),
         pltpu.VMEM((3 * (position // 2), position // 2), bf16),
         pltpu.VMEM(flat, f32),
         pltpu.VMEM((channels, 2 * ctx, position), f32),
@@ -580,13 +583,13 @@
         in_specs=[VMEM, ANY],
         out_specs=ANY,
         out_shape=jax.ShapeDtypeStruct((SPARE * lines, position // 2), f32),
-        scratch_shapes=held + [pltpu.SemaphoreType.DMA((2,))],
+        scratch_shapes=[pltpu.VMEM(table.shape, f32), *held, pltpu.SemaphoreType.DMA((2,))],
         compiler_params=vmem(58),
         cost_estimate=cost(4 * 10**9, 4 * MIB),
     )(taps, table)
     mixed = pl.pallas_call(
         conv_kernel,
-        in_specs=[SMEM, VMEM] + [ANY] * 2,
+        in_specs=[SMEM, VMEM, ANY, VMEM],
         out_specs=ANY,
         out_shape=jax.ShapeDtypeStruct((ch, ctx, channels, position), bf16),
         scratch_shapes=[
@@ -595,7 +598,7 @@
             pltpu.VMEM((channels, 4 * ctx, position), bf16),
             pltpu.VMEM(flat, f32),
             pltpu.VMEM((ctx, channels, position), bf16),
-            pltpu.SemaphoreType.DMA((2,)),
+            pltpu.SemaphoreType.DMA((1,)),
             pltpu.SemaphoreType.DMA((4,)),
         ],
         compiler_params=vmem(40),
@@ -631,7 +634,7 @@
             pltpu.VMEM((position, width), bf16),
             pltpu.VMEM((steps, width, features // steps), bf16),
             pltpu.VMEM((position, features), bf16),
-            pltpu.SemaphoreType.DMA((steps,)),
+            pltpu.SemaphoreType.DMA((steps + 1,)),
             pltpu.SemaphoreType.DMA((steps + LAST_PARTS,)),
         ],
         compiler_params=vmem(48),

time: 89.7 us -> 88.9 us (level)
  Pallas kernels: 37.9 us -> 37 us
    pallas_call x1, Pallas kernels: 6.56 us -> 5.66 us  [shards(): pl.pallas_call(conv_kernel, in_specs=[SMEM, VMEM, ANY, VMEM], out_specs=A...]
where the time goes in v4:
time: 88.9 us; the launch traced here: 88.4 us
  Pallas kernels  37 us (42%)
  starting transfers between devices  29.5 us (33%)
  waiting for transfers between devices  20 us (22%)
  local copies, waits for them, and re-layouts  1.62 us (2%)
    all_to_all x1, starting transfers between devices, shards(): lax.all_to_all(taps.reshape(ctx, channels, position), 'ctx', split_axis=0...  9.28 us
    pallas_call x1, Pallas kernels, shards(): pl.pallas_call(out_kernel, in_specs=[VMEM, ANY], out_specs=ANY, out_shape...  7.54 us
    pallas_call x1, Pallas kernels, shards(): pl.pallas_call(project_kernel, in_specs=[ANY] * 2, out_specs=ANY, out_sha...  7.31 us
    pallas_call x1, Pallas kernels, shards(): pl.pallas_call(weights_kernel, in_specs=[ANY] * (1 + len(pieces)), out_sp...  6.73 us
    all_to_all x1, waiting for transfers between devices, shards(): lax.all_to_all(mixed.reshape(devices, channels, position), ('ch', 'ctx'),...  6.45 us
    all_to_all x1, waiting for transfers between devices, shards(): lax.all_to_all(partial_value.reshape(devices, channels, position), ('ch',...  6.33 us
    pallas_call x1, Pallas kernels, shards(): pl.pallas_call(conv_kernel, in_specs=[SMEM, VMEM, ANY, VMEM], out_specs=A...  5.66 us
    pallas_call x1, Pallas kernels, shards(): pl.pallas_call(spectrum_kernel, in_specs=[VMEM, ANY], out_specs=ANY, out_...  5.43 us
  transfers between devices with their start and end apart: 11, of which 6 were waited for; matrix products, arithmetic and copies ran while one was open for 0% of the time, Pallas kernels for 31%

profile of v4, /device:TPU:1, one launch (start us, length us, event | category | flops | bytes accessed | tf_op | source)
XLA Modules:
  0.0 88.4 jit_solution(4436988897684727655)
XLA Ops:
  0.0 2.4 %shard_map.65 = (bf16[512,512]{1,0:T(8,128)(2,1)}, bf16[64,4096]{1,0:T(8,128)(2,1)}) custom-call(f32[512,512]{1,0:T(8,128)} %taps_hbm.1, bf16[512,8192]{1,0:T(8,128)(2,1)} %own_hbm.1), custom_call_target="tpu_custom_call" | custom-call | bytes 2097152 | tf_op jit(solution)/shard_map/pallas_call | solution.py:506
  2.4 3.6 %collective-permute-start = (bf16[64,4096]{1,0:T(8,128)(2,1)}, bf16[64,4096]{1,0:T(8,128)(2,1)S(1)}, u32[]{:S(2)}, u32[]{:S(2)}) collective-permute-start(bf16[64,4096]{1,0:T(8,128)(2,1)} %get-tuple-element.7), channel_id=1, source_target_pairs={{0,65},{2,67},{4,69},{6,71},{8,73},{10,75},{12,77},{14,79},{16,81}... | collective-permute-start | bytes 1572872 | tf_op jit(solution)/shard_map/ppermute | solution.py:521
  6.0 9.3 %all-to-all-start.1 = ((bf16[64,8,512]{2,1,0:T(8,128)(2,1)}), bf16[64,8,512]{2,1,0:T(8,128)(2,1)S(1)}, u32[]{:S(2)}, u32[]{:S(2)}) async-start(bf16[64,8,512]{2,1,0:T(8,128)(2,1)} %bitcast.8), calls=%async_computation.1 | async-start | bytes 1048576 | tf_op jit(solution)/shard_map/all_to_all | solution.py:522
  15.3 7.3 %shard_map.64.value_ref = bf16[1024,512]{1,0:T(8,128)(2,1)} custom-call(bf16[512,4096]{1,0:T(8,128)(2,1)} %tokens_hbm.1, bf16[4096,1024]{1,0:T(8,128)(2,1)} %weight_hbm.3), custom_call_target="tpu_custom_call" | custom-call | flops 4294967296 | bytes 14680064 | tf_op jit(solution)/shard_map/pallas_call | solution.py:526
  22.6 0.0 collective-permute-done.after_ref.rest_0_
  22.6 0.0 copy-start.2
  22.6 0.8 copy-done.2
  23.4 3.8 %all-to-all-done.1.taps_ref = bf16[64,8,512]{2,1,0:T(8,128)(2,1)S(1)} async-done(((bf16[64,8,512]{2,1,0:T(8,128)(2,1)}), bf16[64,8,512]{2,1,0:T(8,128)(2,1)S(1)}, u32[]{:S(2)}, u32[]{:S(2)}) %all-to-all-start.1) | async-done | bytes 524320 | tf_op jit(solution)/shard_map/all_to_all | solution.py:522
  27.3 0.0 copy-start.4
  27.3 4.1 %all-to-all-start = ((bf16[128,8,512]{2,1,0:T(8,128)(2,1)}), bf16[128,8,512]{2,1,0:T(8,128)(2,1)S(1)}, u32[]{:S(2)}, u32[]{:S(2)}) async-start(bf16[128,8,512]{2,1,0:T(8,128)(2,1)} %bitcast.7), calls=%async_computation | async-start | bytes 2097152 | tf_op jit(solution)/shard_map/all_to_all | solution.py:552
  31.4 0.0 copy-done.4
  31.4 5.4 %shard_map.67.spec_hbm = f32[25344,256]{1,0:T(8,128)} custom-call(bf16[64,8,512]{2,1,0:T(8,128)(2,1)} %copy-done.4, f32[1224,256]{1,0:T(8,128)} %constant.2.clone.table_hbm.table_ref), custom_call_target="tpu_custom_call" | custom-call | flops 4000000000 | bytes 4194304 | tf_op jit(solution)/shard_map/pallas_call | solution.py:581
  36.8 0.0 copy-start.3
  36.8 0.0 copy-start
  36.8 0.0 copy-start.1
  36.9 2.0 %shard_map.69 = bf16[64,4096]{1,0:T(8,128)(2,1)} custom-call(bf16[512,8192]{1,0:T(8,128)(2,1)} %own_hbm.1, bf16[1024,512]{1,0:T(8,128)(2,1)} %shard_map.66.after_ref), custom_call_target="tpu_custom_call" | custom-call | bytes 1048576 | tf_op jit(solution)/shard_map/pallas_call | solution.py:559
  38.9 2.7 %collective-permute-start.3 = (bf16[64,4096]{1,0:T(8,128)(2,1)}, bf16[64,4096]{1,0:T(8,128)(2,1)S(1)}, u32[]{:S(2)}, u32[]{:S(2)}) collective-permute-start(bf16[64,4096]{1,0:T(8,128)(2,1)} %shard_map.69), channel_id=1, source_target_pairs={{0,65},{2,67},{4,69},{6,71},{8,73},{10,75},{12,77},{14,79},{16,81}... | collective-permute-start | bytes 1572872 | tf_op jit(solution)/shard_map/ppermute | solution.py:568
  41.6 0.0 copy-done.3
  41.6 1.5 %collective-permute-start.1 = (bf16[64,4096]{1,0:T(8,128)(2,1)S(1)}, bf16[64,4096]{1,0:T(8,128)(2,1)}, u32[]{:S(2)}, u32[]{:S(2)}) collective-permute-start(bf16[64,4096]{1,0:T(8,128)(2,1)S(1)} %copy-done.3), channel_id=1, source_target_pairs={{0,4},{2,6},{4,0},{6,2},{8,12},{10,14},{12,8},{14,10},{16,20},{18,... | collective-permute-start | bytes 1572872 | tf_op jit(solution)/shard_map/ppermute | solution.py:558
  43.0 1.2 %collective-permute-start.2 = (bf16[64,4096]{1,0:T(8,128)(2,1)S(1)}, bf16[64,4096]{1,0:T(8,128)(2,1)}, u32[]{:S(2)}, u32[]{:S(2)}) collective-permute-start(bf16[64,4096]{1,0:T(8,128)(2,1)S(1)} %copy-done.3), channel_id=1, source_target_pairs={{0,16},{2,18},{4,20},{6,22},{8,24},{10,26},{12,28},{14,30},{16,0},... | collective-permute-start | bytes 1572872 | tf_op jit(solution)/shard_map/ppermute | solution.py:557
  44.2 6.3 %all-to-all-done = bf16[128,8,512]{2,1,0:T(8,128)(2,1)S(1)} async-done(((bf16[128,8,512]{2,1,0:T(8,128)(2,1)}), bf16[128,8,512]{2,1,0:T(8,128)(2,1)S(1)}, u32[]{:S(2)}, u32[]{:S(2)}) %all-to-all-start) | async-done | bytes 1048608 | tf_op jit(solution)/shard_map/all_to_all | solution.py:552
  50.6 0.0 copy-done
  50.6 0.0 copy-done.1
  50.6 5.7 %shard_map.68 = bf16[2,64,8,512]{3,2,1,0:T(8,128)(2,1)} custom-call(f32[512]{0:T(512)S(1)} %copy-done.1, bf16[2,64,8,512]{3,2,1,0:T(8,128)(2,1)S(1)} %bitcast.6, f32[25344,256]{1,0:T(8,128)} %shard_map.67.spec_hbm, f32[1224,256]{1,0:T(8,128)S(1)} %copy-done), custom_call_target="tpu_custom_call" | custom-call | flops 8000000000 | bytes 6291456 | tf_op jit(solution)/shard_map/pallas_call | solution.py:590
  56.2 5.2 %all-to-all-start.2 = ((bf16[128,8,512]{2,1,0:T(8,128)(2,1)}), bf16[128,8,512]{2,1,0:T(8,128)(2,1)S(1)}, u32[]{:S(2)}, u32[]{:S(2)}) async-start(bf16[128,8,512]{2,1,0:T(8,128)(2,1)} %bitcast.3), calls=%async_computation.2 | async-start | bytes 2097152 | tf_op jit(solution)/shard_map/all_to_all | solution.py:608
  61.4 1.3 %collective-permute-start.4 = (bf16[64,4096]{1,0:T(8,128)(2,1)S(1)}, bf16[64,4096]{1,0:T(8,128)(2,1)S(1)}, u32[]{:S(2)}, u32[]{:S(2)}) collective-permute-start(bf16[64,4096]{1,0:T(8,128)(2,1)S(1)} %copy-done.3), channel_id=1, source_target_pairs={{0,2},{2,0},{4,6},{6,4},{8,10},{10,8},{12,14},{14,12},{16,18},{18,... | collective-permute-start | bytes 1572872 | tf_op jit(solution)/shard_map/ppermute | solution.py:570
  62.7 0.0 collective-permute-done.1.rest_1_
  62.7 0.1 collective-permute-start.5
  62.8 0.0 collective-permute-done.2.rest_2_
  62.8 0.4 collective-permute-start.6
  63.2 0.0 collective-permute-done.3.rest_3_
  63.2 0.0 copy-start.5
  63.2 0.1 collective-permute-start.7
  63.3 0.9 %collective-permute-done.4.rest_4_ = bf16[64,4096]{1,0:T(8,128)(2,1)S(1)} collective-permute-done((bf16[64,4096]{1,0:T(8,128)(2,1)S(1)}, bf16[64,4096]{1,0:T(8,128)(2,1)S(1)}, u32[]{:S(2)}, u32[]{:S(2)}) %collective-permute-start.4) | collective-permute-done | bytes 524320 | tf_op jit(solution)/shard_map/ppermute | solution.py:570
  64.3 0.0 copy-start.6
  64.3 1.7 %collective-permute-done.5.rest_5_ = bf16[64,4096]{1,0:T(8,128)(2,1)S(1)} collective-permute-done((bf16[64,4096]{1,0:T(8,128)(2,1)}, bf16[64,4096]{1,0:T(8,128)(2,1)S(1)}, u32[]{:S(2)}, u32[]{:S(2)}) %collective-permute-start.5) | collective-permute-done | bytes 524320 | tf_op jit(solution)/shard_map/ppermute | solution.py:570
  66.0 0.0 copy-start.7
  66.0 0.7 collective-permute-done.6.rest_6_
  66.7 0.0 copy-start.8
  66.7 0.0 collective-permute-done.7.rest_7_
  66.7 0.0 copy-done.5
  66.7 0.0 copy-done.6
  66.7 0.0 copy-done.7
  66.8 0.8 copy-done.8
  67.5 6.7 %shard_map.70.weight_hbm = bf16[4,1024,1024]{2,1,0:T(8,128)(2,1)} custom-call(bf16[512,8192]{1,0:T(8,128)(2,1)} %own_hbm.1, bf16[64,4096]{1,0:T(8,128)(2,1)} %copy-done.2, bf16[64,4096]{1,0:T(8,128)(2,1)} %collective-permute-done.1.rest_1_, bf16[64,4096]{1,0:T(8,128)(2,1)} %collective-permute-done.2.rest_2_, bf16[64,4096]{1,0:T(8,128)(2,1)} %copy-done.5, ...), custom_call_target="tpu_custom_call" | custom-call | bytes 16777216 | tf_op jit(solution)/shard_map/pallas_call | solution.py:614
  74.3 6.5 %all-to-all-done.2 = bf16[128,8,512]{2,1,0:T(8,128)(2,1)S(1)} async-done(((bf16[128,8,512]{2,1,0:T(8,128)(2,1)}), bf16[128,8,512]{2,1,0:T(8,128)(2,1)S(1)}, u32[]{:S(2)}, u32[]{:S(2)}) %all-to-all-start.2) | async-done | bytes 1048608 | tf_op jit(solution)/shard_map/all_to_all | solution.py:608
  80.7 7.5 %shard_map.71 = bf16[512,4096]{1,0:T(8,128)(2,1)} custom-call(bf16[1024,512]{1,0:T(8,128)(2,1)S(1)} %bitcast.5, bf16[4,1024,1024]{2,1,0:T(8,128)(2,1)} %shard_map.70.weight_hbm), custom_call_target="tpu_custom_call" | custom-call | flops 4294967296 | bytes 13631488 | tf_op jit(solution)/shard_map/pallas_call | solution.py:628
  (1 shorter events, 0.0 us)
Async XLA Ops:
  2.4 20.3 %collective-permute-start = (bf16[64,4096]{1,0:T(8,128)(2,1)}, bf16[64,4096]{1,0:T(8,128)(2,1)S(1)}, u32[]{:S(2)}, u32[]{:S(2)}) collective-permute-start(bf16[64,4096]{1,0:T(8,128)(2,1)} %get-tuple-element.7), channel_id=1, source_target_pairs={{0,65},{2,67},{4,69},{6,71},{8,73},{10,75},{12,77},{14,79},{16,81}... | collective-permute-start | bytes 1572872 | tf_op jit(solution)/shard_map/ppermute | solution.py:521
  6.0 21.2 %all-to-all-start.1 = ((bf16[64,8,512]{2,1,0:T(8,128)(2,1)}), bf16[64,8,512]{2,1,0:T(8,128)(2,1)S(1)}, u32[]{:S(2)}, u32[]{:S(2)}) async-start(bf16[64,8,512]{2,1,0:T(8,128)(2,1)} %bitcast.8), calls=%async_computation.1 | async-start | bytes 1048576 | tf_op jit(solution)/shard_map/all_to_all | solution.py:522
  22.6 0.8 copy-start.2
  27.3 4.1 %copy-start.4 = (bf16[64,8,512]{2,1,0:T(8,128)(2,1)}, bf16[64,8,512]{2,1,0:T(8,128)(2,1)S(1)}, u32[]{:S(2)}) copy-start(bf16[64,8,512]{2,1,0:T(8,128)(2,1)S(1)} %all-to-all-done.1.taps_ref) | copy-start | bytes 1572868
  27.3 23.3 %all-to-all-start = ((bf16[128,8,512]{2,1,0:T(8,128)(2,1)}), bf16[128,8,512]{2,1,0:T(8,128)(2,1)S(1)}, u32[]{:S(2)}, u32[]{:S(2)}) async-start(bf16[128,8,512]{2,1,0:T(8,128)(2,1)} %bitcast.7), calls=%async_computation | async-start | bytes 2097152 | tf_op jit(solution)/shard_map/all_to_all | solution.py:552
  36.8 4.8 %copy-start.3 = (bf16[64,4096]{1,0:T(8,128)(2,1)S(1)}, bf16[64,4096]{1,0:T(8,128)(2,1)}, u32[]{:S(2)}) copy-start(bf16[64,4096]{1,0:T(8,128)(2,1)} %copy-done.2) | copy-start | bytes 1572868
  36.8 13.7 %copy-start = (f32[1224,256]{1,0:T(8,128)S(1)}, f32[1224,256]{1,0:T(8,128)}, u32[]{:S(2)}) copy-start(f32[1224,256]{1,0:T(8,128)} %constant.2.clone.table_hbm.table_ref) | copy-start | bytes 3760132
  36.8 13.7 %copy-start.1 = (f32[512]{0:T(512)S(1)}, f32[512]{0:T(512)}, u32[]{:S(2)}) copy-start(f32[512]{0:T(512)} %gain_ref.1) | copy-start | bytes 6148
  38.9 24.4 %collective-permute-start.3 = (bf16[64,4096]{1,0:T(8,128)(2,1)}, bf16[64,4096]{1,0:T(8,128)(2,1)S(1)}, u32[]{:S(2)}, u32[]{:S(2)}) collective-permute-start(bf16[64,4096]{1,0:T(8,128)(2,1)} %shard_map.69), channel_id=1, source_target_pairs={{0,65},{2,67},{4,69},{6,71},{8,73},{10,75},{12,77},{14,79},{16,81}... | collective-permute-start | bytes 1572872 | tf_op jit(solution)/shard_map/ppermute | solution.py:568
  41.6 21.1 %collective-permute-start.1 = (bf16[64,4096]{1,0:T(8,128)(2,1)S(1)}, bf16[64,4096]{1,0:T(8,128)(2,1)}, u32[]{:S(2)}, u32[]{:S(2)}) collective-permute-start(bf16[64,4096]{1,0:T(8,128)(2,1)S(1)} %copy-done.3), channel_id=1, source_target_pairs={{0,4},{2,6},{4,0},{6,2},{8,12},{10,14},{12,8},{14,10},{16,20},{18,... | collective-permute-start | bytes 1572872 | tf_op jit(solution)/shard_map/ppermute | solution.py:558
  43.0 19.8 %collective-permute-start.2 = (bf16[64,4096]{1,0:T(8,128)(2,1)S(1)}, bf16[64,4096]{1,0:T(8,128)(2,1)}, u32[]{:S(2)}, u32[]{:S(2)}) collective-permute-start(bf16[64,4096]{1,0:T(8,128)(2,1)S(1)} %copy-done.3), channel_id=1, source_target_pairs={{0,16},{2,18},{4,20},{6,22},{8,24},{10,26},{12,28},{14,30},{16,0},... | collective-permute-start | bytes 1572872 | tf_op jit(solution)/shard_map/ppermute | solution.py:557
  56.2 24.5 %all-to-all-start.2 = ((bf16[128,8,512]{2,1,0:T(8,128)(2,1)}), bf16[128,8,512]{2,1,0:T(8,128)(2,1)S(1)}, u32[]{:S(2)}, u32[]{:S(2)}) async-start(bf16[128,8,512]{2,1,0:T(8,128)(2,1)} %bitcast.3), calls=%async_computation.2 | async-start | bytes 2097152 | tf_op jit(solution)/shard_map/all_to_all | solution.py:608
  61.4 2.8 %collective-permute-start.4 = (bf16[64,4096]{1,0:T(8,128)(2,1)S(1)}, bf16[64,4096]{1,0:T(8,128)(2,1)S(1)}, u32[]{:S(2)}, u32[]{:S(2)}) collective-permute-start(bf16[64,4096]{1,0:T(8,128)(2,1)S(1)} %copy-done.3), channel_id=1, source_target_pairs={{0,2},{2,0},{4,6},{6,4},{8,10},{10,8},{12,14},{14,12},{16,18},{18,... | collective-permute-start | bytes 1572872 | tf_op jit(solution)/shard_map/ppermute | solution.py:570
  62.7 3.2 %collective-permute-start.5 = (bf16[64,4096]{1,0:T(8,128)(2,1)}, bf16[64,4096]{1,0:T(8,128)(2,1)S(1)}, u32[]{:S(2)}, u32[]{:S(2)}) collective-permute-start(bf16[64,4096]{1,0:T(8,128)(2,1)} %collective-permute-done.1.rest_1_), channel_id=1, source_target_pairs={{0,2},{2,0},{4,6},{6,4},{8,10},{10,8},{12,14},{14,12},{16,18},{18,... | collective-permute-start | bytes 1572872 | tf_op jit(solution)/shard_map/ppermute | solution.py:570
  62.8 3.9 %collective-permute-start.6 = (bf16[64,4096]{1,0:T(8,128)(2,1)}, bf16[64,4096]{1,0:T(8,128)(2,1)S(1)}, u32[]{:S(2)}, u32[]{:S(2)}) collective-permute-start(bf16[64,4096]{1,0:T(8,128)(2,1)} %collective-permute-done.2.rest_2_), channel_id=1, source_target_pairs={{0,2},{2,0},{4,6},{6,4},{8,10},{10,8},{12,14},{14,12},{16,18},{18,... | collective-permute-start | bytes 1572872 | tf_op jit(solution)/shard_map/ppermute | solution.py:570
  63.2 3.5 %copy-start.5 = (bf16[64,4096]{1,0:T(8,128)(2,1)}, bf16[64,4096]{1,0:T(8,128)(2,1)S(1)}, u32[]{:S(2)}) copy-start(bf16[64,4096]{1,0:T(8,128)(2,1)S(1)} %collective-permute-done.3.rest_3_) | copy-start | bytes 1572868
  63.2 3.5 %collective-permute-start.7 = (bf16[64,4096]{1,0:T(8,128)(2,1)S(1)}, bf16[64,4096]{1,0:T(8,128)(2,1)}, u32[]{:S(2)}, u32[]{:S(2)}) collective-permute-start(bf16[64,4096]{1,0:T(8,128)(2,1)S(1)} %collective-permute-done.3.rest_3_), channel_id=1, source_target_pairs={{0,2},{2,0},{4,6},{6,4},{8,10},{10,8},{12,14},{14,12},{16,18},{18,... | collective-permute-start | bytes 1572872 | tf_op jit(solution)/shard_map/ppermute | solution.py:570
  64.3 2.5 %copy-start.6 = (bf16[64,4096]{1,0:T(8,128)(2,1)}, bf16[64,4096]{1,0:T(8,128)(2,1)S(1)}, u32[]{:S(2)}) copy-start(bf16[64,4096]{1,0:T(8,128)(2,1)S(1)} %collective-permute-done.4.rest_4_) | copy-start | bytes 1572868
  66.0 0.8 copy-start.7
  66.7 0.8 copy-start.8

commit v5 on v4

--- a/solution.py
+++ b/solution.py
@@ -231,7 +231,7 @@
     taps_spec_ref, line_ref,
     flat, lines_ref, rows_ref, spec_ref, packed_ref, mixed_ref, out_ref, sems, out_sems,
 ):
-    _, blocks, channels, width = parts_ref.shape
+    blocks, _, channels, width = parts_ref.shape
     lanes = flat.shape[2]
     quarters = width // lanes
     quarter = spec_ref.shape[1] // 2
@@ -239,7 +239,7 @@
     size = blocks * 4
     half = blocks // 2
     copies = start_all([(spec_hbm.at[pl.ds(0, taps_spec_ref.shape[0])], taps_spec_ref)], sems)
-    total = parts_ref[0].astype(f32) + parts_ref[1].astype(f32)
+    total = parts_ref[:, 0].astype(f32) + parts_ref[:, 1].astype(f32)
     fill(flat, total)
     last = alternating(total)
     lead, _, tail, fold, twist = unpack(table_ref, blocks, line_ref)
@@ -302,7 +302,7 @@
             out_ref[span, :, lanes * q : lanes * (q + 1)] = result.reshape(half, channels, lanes)
         for k in range(2):
             stores.append(
-                pltpu.make_async_copy(out_ref.at[span], out_hbm.at[k, span], out_sems.at[2 * i + k])
+                pltpu.make_async_copy(out_ref.at[span], out_hbm.at[span, k], out_sems.at[2 * i + k])
             )
             stores[-1].start()
     for copy in stores:
@@ -360,6 +360,7 @@
 ):
     features = tokens_ref.shape[1]
     width = weight_ref.shape[1]
+    ctx, ch, channels, _ = out_hbm.shape
     steps = features // CHUNK
     parts = 4
     loads = []
@@ -385,9 +386,12 @@
             elif i < steps - 1:
                 total[:, cols] += term
             else:
-                out_ref[cols, :] = (total[:, cols] + term).astype(bf16).T
-                rows = pl.ds(c * width // parts, width // parts)
-                store = pltpu.make_async_copy(out_ref.at[rows], out_hbm.at[rows], out_sems.at[c])
+                turned = (total[:, cols] + term).astype(bf16).T
+                count = ctx * ch // parts
+                span = pl.ds(c * count, count)
+                out_ref[span] = turned.reshape(count, channels, turned.shape[1])
+                place = out_hbm.at[pl.ds(c * count % ctx, count), c * count // ctx]
+                store = pltpu.make_async_copy(out_ref.at[span], place, out_sems.at[c])
                 store.start()
                 stores.append(store)
     for store in stores:
@@ -417,20 +421,19 @@
 
 def out_kernel(mixed_ref, weight_hbm, out_hbm, turned, weight_ref, out_ref, sems, out_sems):
     steps, _, columns = weight_ref.shape
-    width = mixed_ref.shape[0]
-    rows = width // 2
+    ctx, _, channels, position = mixed_ref.shape
+    rows = ctx * channels
     parts = [(0, pl.ds(0, rows)), (0, pl.ds(rows, rows)), *range(1, steps)]
     loads = start_all([(weight_hbm.at[i], weight_ref.at[i]) for i in parts], sems)
     group, core, x, z = where()
-    size = rows // (2 * PIECES)
-    own = mixed_ref[pl.ds(pl.multiple_of(group * rows, rows), rows), :]
-    turned[:, :rows] = own.T
+    size = ctx // (2 * PIECES)
+    turned[:, :rows] = mixed_ref[:, group].reshape(rows, position).T
     pieces = []
     for half in (core, 1 - core):
         for k in held_pieces(x, z):
-            start = (1 - group) * rows + (half * PIECES + k) * size
-            pieces.append(mixed_ref[pl.ds(pl.multiple_of(start, size), size), :])
-    turned[:, rows:] = jnp.concatenate(pieces, axis=0).T
+            start = (half * PIECES + k) * size
+            pieces.append(mixed_ref[pl.ds(start, size), 1 - group])
+    turned[:, rows:] = jnp.concatenate(pieces, axis=0).reshape(rows, position).T
     loads[0].wait()
     own_part = dot(turned[:, :rows], weight_ref[0, :rows])
     loads[1].wait()
@@ -527,12 +530,12 @@
         project_kernel,
         in_specs=[ANY] * 2,
         out_specs=ANY,
-        out_shape=jax.ShapeDtypeStruct((width, position), bf16),
+        out_shape=jax.ShapeDtypeStruct((ctx, ch, channels, position), bf16),
         scratch_shapes=[
             pltpu.VMEM((position, features), bf16),
             pltpu.VMEM((features, width), bf16),
             pltpu.VMEM((position, width), f32),
-            pltpu.VMEM((width, position), bf16),
+            pltpu.VMEM((devices, channels, position), bf16),
             pltpu.SemaphoreType.DMA((features // CHUNK,)),
             pltpu.SemaphoreType.DMA((features // CHUNK,)),
             pltpu.SemaphoreType.DMA((4,)),
@@ -544,15 +547,15 @@
         fence_kernel,
         in_specs=[ANY] * 2,
         out_specs=ANY,
-        out_shape=jax.ShapeDtypeStruct((width, position), bf16),
+        out_shape=jax.ShapeDtypeStruct(partial_value.shape, bf16),
         input_output_aliases={0: 0},
         compiler_params=vmem(60),
         cost_estimate=cost(0, 0),
     )(partial_value, mine)
     parts = lax.all_to_all(
         partial_value.reshape(devices, channels, position),
-        ("ch", "ctx"), split_axis=0, concat_axis=0, tiled=True,
-    ).reshape(ch, ctx, channels, position)
+        both, split_axis=0, concat_axis=0, tiled=True,
+    ).reshape(ctx, ch, channels, position)
 
     by_x = lax.ppermute(mine, both, along_x)
     by_z = lax.ppermute(mine, both, along_z)
@@ -591,7 +594,7 @@
         conv_kernel,
         in_specs=[SMEM, VMEM, ANY, VMEM],
         out_specs=ANY,
-        out_shape=jax.ShapeDtypeStruct((ch, ctx, channels, position), bf16),
+        out_shape=jax.ShapeDtypeStruct((ctx, ch, channels, position), bf16),
         scratch_shapes=[
             pltpu.VMEM((lines, position // 2), f32),
             *held,
@@ -607,8 +610,8 @@
 
     mixed = lax.all_to_all(
         mixed.reshape(devices, channels, position),
-        ("ch", "ctx"), split_axis=0, concat_axis=0, tiled=True,
-    ).reshape(width, position)
+        both, split_axis=0, concat_axis=0, tiled=True,
+    ).reshape(ctx, ch, channels, position)
 
     steps = features // 1024
     weights = pl.pallas_call(

time: 88.9 us -> 87.9 us (0.989)
  waiting for transfers between devices: 20 us -> 18.6 us
    all_to_all x2, waiting for transfers between devices: 12.8 us -> 11.4 us  [the longest x1 5.75 us: shards(): lax.all_to_all(mixed.reshape(devices, channels, position), both, split_ax...]
where the time goes in v5:
time: 87.9 us; the launch traced here: 87.5 us
  Pallas kernels  37.1 us (42%)
  starting transfers between devices  29.9 us (34%)
  waiting for transfers between devices  18.6 us (21%)
  local copies, waits for them, and re-layouts  1.62 us (2%)
    all_to_all x1, starting transfers between devices, shards(): lax.all_to_all(taps.reshape(ctx, channels, position), 'ctx', split_axis=0...  9.28 us
    pallas_call x1, Pallas kernels, shards(): pl.pallas_call(out_kernel, in_specs=[VMEM, ANY], out_specs=ANY, out_shape...  7.58 us
    pallas_call x1, Pallas kernels, shards(): pl.pallas_call(project_kernel, in_specs=[ANY] * 2, out_specs=ANY, out_sha...  7.31 us
    pallas_call x1, Pallas kernels, shards(): pl.pallas_call(weights_kernel, in_specs=[ANY] * (1 + len(pieces)), out_sp...  6.73 us
    all_to_all x1, waiting for transfers between devices, shards(): lax.all_to_all(mixed.reshape(devices, channels, position), both, split_ax...  5.75 us
    all_to_all x1, starting transfers between devices, shards(): lax.all_to_all(mixed.reshape(devices, channels, position), both, split_ax...  5.7 us
    pallas_call x1, Pallas kernels, shards(): pl.pallas_call(conv_kernel, in_specs=[SMEM, VMEM, ANY, VMEM], out_specs=A...  5.66 us
    all_to_all x1, waiting for transfers between devices, shards(): lax.all_to_all(partial_value.reshape(devices, channels, position), both,...  5.64 us
  transfers between devices with their start and end apart: 11, of which 6 were waited for; matrix products, arithmetic and copies ran while one was open for 0% of the time, Pallas kernels for 31%

profile of v5, /device:TPU:1, one launch (start us, length us, event | category | flops | bytes accessed | tf_op | source)
XLA Modules:
  0.0 87.5 jit_solution(10509037617196203343)
XLA Ops:
  0.0 2.4 %shard_map.65 = (bf16[512,512]{1,0:T(8,128)(2,1)}, bf16[64,4096]{1,0:T(8,128)(2,1)}) custom-call(f32[512,512]{1,0:T(8,128)} %taps_hbm.1, bf16[512,8192]{1,0:T(8,128)(2,1)} %own_hbm.1), custom_call_target="tpu_custom_call" | custom-call | bytes 2097152 | tf_op jit(solution)/shard_map/pallas_call | solution.py:509
  2.4 3.6 %collective-permute-start = (bf16[64,4096]{1,0:T(8,128)(2,1)}, bf16[64,4096]{1,0:T(8,128)(2,1)S(1)}, u32[]{:S(2)}, u32[]{:S(2)}) collective-permute-start(bf16[64,4096]{1,0:T(8,128)(2,1)} %get-tuple-element.7), channel_id=1, source_target_pairs={{0,65},{2,67},{4,69},{6,71},{8,73},{10,75},{12,77},{14,79},{16,81}... | collective-permute-start | bytes 1572872 | tf_op jit(solution)/shard_map/ppermute | solution.py:524
  6.0 9.3 %all-to-all-start.1 = ((bf16[64,8,512]{2,1,0:T(8,128)(2,1)}), bf16[64,8,512]{2,1,0:T(8,128)(2,1)S(1)}, u32[]{:S(2)}, u32[]{:S(2)}) async-start(bf16[64,8,512]{2,1,0:T(8,128)(2,1)} %bitcast.8), calls=%async_computation.1 | async-start | bytes 1048576 | tf_op jit(solution)/shard_map/all_to_all | solution.py:525
  15.3 7.3 %shard_map.64.value_ref = bf16[64,2,8,512]{3,2,1,0:T(8,128)(2,1)} custom-call(bf16[512,4096]{1,0:T(8,128)(2,1)} %tokens_hbm.1, bf16[4096,1024]{1,0:T(8,128)(2,1)} %weight_hbm.3), custom_call_target="tpu_custom_call" | custom-call | flops 4294967296 | bytes 14680064 | tf_op jit(solution)/shard_map/pallas_call | solution.py:529
  22.6 0.0 collective-permute-done.after_ref.rest_0_
  22.6 0.0 copy-start.2
  22.6 0.8 copy-done.2
  23.4 3.8 %all-to-all-done.1.taps_ref = bf16[64,8,512]{2,1,0:T(8,128)(2,1)S(1)} async-done(((bf16[64,8,512]{2,1,0:T(8,128)(2,1)}), bf16[64,8,512]{2,1,0:T(8,128)(2,1)S(1)}, u32[]{:S(2)}, u32[]{:S(2)}) %all-to-all-start.1) | async-done | bytes 524320 | tf_op jit(solution)/shard_map/all_to_all | solution.py:525
  27.3 0.0 copy-start.4
  27.3 4.1 %all-to-all-start = ((bf16[128,8,512]{2,1,0:T(8,128)(2,1)}), bf16[128,8,512]{2,1,0:T(8,128)(2,1)S(1)}, u32[]{:S(2)}, u32[]{:S(2)}) async-start(bf16[128,8,512]{2,1,0:T(8,128)(2,1)} %bitcast.7), calls=%async_computation | async-start | bytes 2097152 | tf_op jit(solution)/shard_map/all_to_all | solution.py:555
  31.4 0.0 copy-done.4
  31.4 5.4 %shard_map.67.spec_hbm = f32[25344,256]{1,0:T(8,128)} custom-call(bf16[64,8,512]{2,1,0:T(8,128)(2,1)} %copy-done.4, f32[1224,256]{1,0:T(8,128)} %constant.2.clone.table_hbm.table_ref), custom_call_target="tpu_custom_call" | custom-call | flops 4000000000 | bytes 4194304 | tf_op jit(solution)/shard_map/pallas_call | solution.py:584
  36.8 0.0 copy-start.3
  36.8 0.0 copy-start
  36.8 0.0 copy-start.1
  36.9 2.0 %shard_map.69 = bf16[64,4096]{1,0:T(8,128)(2,1)} custom-call(bf16[512,8192]{1,0:T(8,128)(2,1)} %own_hbm.1, bf16[64,2,8,512]{3,2,1,0:T(8,128)(2,1)} %shard_map.66.after_ref), custom_call_target="tpu_custom_call" | custom-call | bytes 1048576 | tf_op jit(solution)/shard_map/pallas_call | solution.py:562
  38.9 2.7 %collective-permute-start.3 = (bf16[64,4096]{1,0:T(8,128)(2,1)}, bf16[64,4096]{1,0:T(8,128)(2,1)S(1)}, u32[]{:S(2)}, u32[]{:S(2)}) collective-permute-start(bf16[64,4096]{1,0:T(8,128)(2,1)} %shard_map.69), channel_id=1, source_target_pairs={{0,65},{2,67},{4,69},{6,71},{8,73},{10,75},{12,77},{14,79},{16,81}... | collective-permute-start | bytes 1572872 | tf_op jit(solution)/shard_map/ppermute | solution.py:571
  41.6 0.0 copy-done.3
  41.6 1.5 %collective-permute-start.1 = (bf16[64,4096]{1,0:T(8,128)(2,1)S(1)}, bf16[64,4096]{1,0:T(8,128)(2,1)}, u32[]{:S(2)}, u32[]{:S(2)}) collective-permute-start(bf16[64,4096]{1,0:T(8,128)(2,1)S(1)} %copy-done.3), channel_id=1, source_target_pairs={{0,4},{2,6},{4,0},{6,2},{8,12},{10,14},{12,8},{14,10},{16,20},{18,... | collective-permute-start | bytes 1572872 | tf_op jit(solution)/shard_map/ppermute | solution.py:561
  43.0 1.2 %collective-permute-start.2 = (bf16[64,4096]{1,0:T(8,128)(2,1)S(1)}, bf16[64,4096]{1,0:T(8,128)(2,1)}, u32[]{:S(2)}, u32[]{:S(2)}) collective-permute-start(bf16[64,4096]{1,0:T(8,128)(2,1)S(1)} %copy-done.3), channel_id=1, source_target_pairs={{0,16},{2,18},{4,20},{6,22},{8,24},{10,26},{12,28},{14,30},{16,0},... | collective-permute-start | bytes 1572872 | tf_op jit(solution)/shard_map/ppermute | solution.py:560
  44.2 5.6 %all-to-all-done = bf16[128,8,512]{2,1,0:T(8,128)(2,1)S(1)} async-done(((bf16[128,8,512]{2,1,0:T(8,128)(2,1)}), bf16[128,8,512]{2,1,0:T(8,128)(2,1)S(1)}, u32[]{:S(2)}, u32[]{:S(2)}) %all-to-all-start) | async-done | bytes 1048608 | tf_op jit(solution)/shard_map/all_to_all | solution.py:555
  49.9 0.0 copy-done
  49.9 0.0 copy-done.1
  49.9 5.7 %shard_map.68 = bf16[64,2,8,512]{3,2,1,0:T(8,128)(2,1)} custom-call(f32[512]{0:T(512)S(1)} %copy-done.1, bf16[64,2,8,512]{3,2,1,0:T(8,128)(2,1)S(1)} %bitcast.6, f32[25344,256]{1,0:T(8,128)} %shard_map.67.spec_hbm, f32[1224,256]{1,0:T(8,128)S(1)} %copy-done), custom_call_target="tpu_custom_call" | custom-call | flops 8000000000 | bytes 6291456 | tf_op jit(solution)/shard_map/pallas_call | solution.py:593
  55.6 5.7 %all-to-all-start.2 = ((bf16[128,8,512]{2,1,0:T(8,128)(2,1)}), bf16[128,8,512]{2,1,0:T(8,128)(2,1)S(1)}, u32[]{:S(2)}, u32[]{:S(2)}) async-start(bf16[128,8,512]{2,1,0:T(8,128)(2,1)} %bitcast.3), calls=%async_computation.2 | async-start | bytes 2097152 | tf_op jit(solution)/shard_map/all_to_all | solution.py:611
  61.3 1.1 %collective-permute-start.4 = (bf16[64,4096]{1,0:T(8,128)(2,1)S(1)}, bf16[64,4096]{1,0:T(8,128)(2,1)S(1)}, u32[]{:S(2)}, u32[]{:S(2)}) collective-permute-start(bf16[64,4096]{1,0:T(8,128)(2,1)S(1)} %copy-done.3), channel_id=1, source_target_pairs={{0,2},{2,0},{4,6},{6,4},{8,10},{10,8},{12,14},{14,12},{16,18},{18,... | collective-permute-start | bytes 1572872 | tf_op jit(solution)/shard_map/ppermute | solution.py:573
  62.4 0.0 collective-permute-done.1.rest_1_
  62.4 0.1 collective-permute-start.5
  62.5 0.0 collective-permute-done.2.rest_2_
  62.5 0.4 collective-permute-start.6
  62.9 0.0 collective-permute-done.3.rest_3_
  62.9 0.0 copy-start.5
  62.9 0.1 collective-permute-start.7
  63.0 0.9 %collective-permute-done.4.rest_4_ = bf16[64,4096]{1,0:T(8,128)(2,1)S(1)} collective-permute-done((bf16[64,4096]{1,0:T(8,128)(2,1)S(1)}, bf16[64,4096]{1,0:T(8,128)(2,1)S(1)}, u32[]{:S(2)}, u32[]{:S(2)}) %collective-permute-start.4) | collective-permute-done | bytes 524320 | tf_op jit(solution)/shard_map/ppermute | solution.py:573
  63.9 0.0 copy-start.6
  63.9 1.7 %collective-permute-done.5.rest_5_ = bf16[64,4096]{1,0:T(8,128)(2,1)S(1)} collective-permute-done((bf16[64,4096]{1,0:T(8,128)(2,1)}, bf16[64,4096]{1,0:T(8,128)(2,1)S(1)}, u32[]{:S(2)}, u32[]{:S(2)}) %collective-permute-start.5) | collective-permute-done | bytes 524320 | tf_op jit(solution)/shard_map/ppermute | solution.py:573
  65.7 0.0 copy-start.7
  65.7 0.7 collective-permute-done.6.rest_6_
  66.4 0.0 copy-start.8
  66.4 0.0 collective-permute-done.7.rest_7_
  66.4 0.0 copy-done.5
  66.4 0.0 copy-done.6
  66.4 0.0 copy-done.7
  66.5 0.8 copy-done.8
  67.2 6.7 %shard_map.70.weight_hbm = bf16[4,1024,1024]{2,1,0:T(8,128)(2,1)} custom-call(bf16[512,8192]{1,0:T(8,128)(2,1)} %own_hbm.1, bf16[64,4096]{1,0:T(8,128)(2,1)} %copy-done.2, bf16[64,4096]{1,0:T(8,128)(2,1)} %collective-permute-done.1.rest_1_, bf16[64,4096]{1,0:T(8,128)(2,1)} %collective-permute-done.2.rest_2_, bf16[64,4096]{1,0:T(8,128)(2,1)} %copy-done.5, ...), custom_call_target="tpu_custom_call" | custom-call | bytes 16777216 | tf_op jit(solution)/shard_map/pallas_call | solution.py:617
  74.0 5.8 %all-to-all-done.2 = bf16[128,8,512]{2,1,0:T(8,128)(2,1)S(1)} async-done(((bf16[128,8,512]{2,1,0:T(8,128)(2,1)}), bf16[128,8,512]{2,1,0:T(8,128)(2,1)S(1)}, u32[]{:S(2)}, u32[]{:S(2)}) %all-to-all-start.2) | async-done | bytes 1048608 | tf_op jit(solution)/shard_map/all_to_all | solution.py:611
  79.7 7.6 %shard_map.71 = bf16[512,4096]{1,0:T(8,128)(2,1)} custom-call(bf16[64,2,8,512]{3,2,1,0:T(8,128)(2,1)S(1)} %bitcast.5, bf16[4,1024,1024]{2,1,0:T(8,128)(2,1)} %shard_map.70.weight_hbm), custom_call_target="tpu_custom_call" | custom-call | flops 4294967296 | bytes 13631488 | tf_op jit(solution)/shard_map/pallas_call | solution.py:631
  (1 shorter events, 0.0 us)
Async XLA Ops:
  2.4 20.3 %collective-permute-start = (bf16[64,4096]{1,0:T(8,128)(2,1)}, bf16[64,4096]{1,0:T(8,128)(2,1)S(1)}, u32[]{:S(2)}, u32[]{:S(2)}) collective-permute-start(bf16[64,4096]{1,0:T(8,128)(2,1)} %get-tuple-element.7), channel_id=1, source_target_pairs={{0,65},{2,67},{4,69},{6,71},{8,73},{10,75},{12,77},{14,79},{16,81}... | collective-permute-start | bytes 1572872 | tf_op jit(solution)/shard_map/ppermute | solution.py:524
  6.0 21.2 %all-to-all-start.1 = ((bf16[64,8,512]{2,1,0:T(8,128)(2,1)}), bf16[64,8,512]{2,1,0:T(8,128)(2,1)S(1)}, u32[]{:S(2)}, u32[]{:S(2)}) async-start(bf16[64,8,512]{2,1,0:T(8,128)(2,1)} %bitcast.8), calls=%async_computation.1 | async-start | bytes 1048576 | tf_op jit(solution)/shard_map/all_to_all | solution.py:525
  22.6 0.8 copy-start.2
  27.3 4.1 %copy-start.4 = (bf16[64,8,512]{2,1,0:T(8,128)(2,1)}, bf16[64,8,512]{2,1,0:T(8,128)(2,1)S(1)}, u32[]{:S(2)}) copy-start(bf16[64,8,512]{2,1,0:T(8,128)(2,1)S(1)} %all-to-all-done.1.taps_ref) | copy-start | bytes 1572868
  27.3 22.6 %all-to-all-start = ((bf16[128,8,512]{2,1,0:T(8,128)(2,1)}), bf16[128,8,512]{2,1,0:T(8,128)(2,1)S(1)}, u32[]{:S(2)}, u32[]{:S(2)}) async-start(bf16[128,8,512]{2,1,0:T(8,128)(2,1)} %bitcast.7), calls=%async_computation | async-start | bytes 2097152 | tf_op jit(solution)/shard_map/all_to_all | solution.py:555
  36.8 4.8 %copy-start.3 = (bf16[64,4096]{1,0:T(8,128)(2,1)S(1)}, bf16[64,4096]{1,0:T(8,128)(2,1)}, u32[]{:S(2)}) copy-start(bf16[64,4096]{1,0:T(8,128)(2,1)} %copy-done.2) | copy-start | bytes 1572868
  36.8 13.1 %copy-start = (f32[1224,256]{1,0:T(8,128)S(1)}, f32[1224,256]{1,0:T(8,128)}, u32[]{:S(2)}) copy-start(f32[1224,256]{1,0:T(8,128)} %constant.2.clone.table_hbm.table_ref) | copy-start | bytes 3760132
  36.8 13.0 %copy-start.1 = (f32[512]{0:T(512)S(1)}, f32[512]{0:T(512)}, u32[]{:S(2)}) copy-start(f32[512]{0:T(512)} %gain_ref.1) | copy-start | bytes 6148
  38.9 24.1 %collective-permute-start.3 = (bf16[64,4096]{1,0:T(8,128)(2,1)}, bf16[64,4096]{1,0:T(8,128)(2,1)S(1)}, u32[]{:S(2)}, u32[]{:S(2)}) collective-permute-start(bf16[64,4096]{1,0:T(8,128)(2,1)} %shard_map.69), channel_id=1, source_target_pairs={{0,65},{2,67},{4,69},{6,71},{8,73},{10,75},{12,77},{14,79},{16,81}... | collective-permute-start | bytes 1572872 | tf_op jit(solution)/shard_map/ppermute | solution.py:571
  41.6 20.8 %collective-permute-start.1 = (bf16[64,4096]{1,0:T(8,128)(2,1)S(1)}, bf16[64,4096]{1,0:T(8,128)(2,1)}, u32[]{:S(2)}, u32[]{:S(2)}) collective-permute-start(bf16[64,4096]{1,0:T(8,128)(2,1)S(1)} %copy-done.3), channel_id=1, source_target_pairs={{0,4},{2,6},{4,0},{6,2},{8,12},{10,14},{12,8},{14,10},{16,20},{18,... | collective-permute-start | bytes 1572872 | tf_op jit(solution)/shard_map/ppermute | solution.py:561
  43.0 19.5 %collective-permute-start.2 = (bf16[64,4096]{1,0:T(8,128)(2,1)S(1)}, bf16[64,4096]{1,0:T(8,128)(2,1)}, u32[]{:S(2)}, u32[]{:S(2)}) collective-permute-start(bf16[64,4096]{1,0:T(8,128)(2,1)S(1)} %copy-done.3), channel_id=1, source_target_pairs={{0,16},{2,18},{4,20},{6,22},{8,24},{10,26},{12,28},{14,30},{16,0},... | collective-permute-start | bytes 1572872 | tf_op jit(solution)/shard_map/ppermute | solution.py:560
  55.6 24.2 %all-to-all-start.2 = ((bf16[128,8,512]{2,1,0:T(8,128)(2,1)}), bf16[128,8,512]{2,1,0:T(8,128)(2,1)S(1)}, u32[]{:S(2)}, u32[]{:S(2)}) async-start(bf16[128,8,512]{2,1,0:T(8,128)(2,1)} %bitcast.3), calls=%async_computation.2 | async-start | bytes 2097152 | tf_op jit(solution)/shard_map/all_to_all | solution.py:611
  61.3 2.7 %collective-permute-start.4 = (bf16[64,4096]{1,0:T(8,128)(2,1)S(1)}, bf16[64,4096]{1,0:T(8,128)(2,1)S(1)}, u32[]{:S(2)}, u32[]{:S(2)}) collective-permute-start(bf16[64,4096]{1,0:T(8,128)(2,1)S(1)} %copy-done.3), channel_id=1, source_target_pairs={{0,2},{2,0},{4,6},{6,4},{8,10},{10,8},{12,14},{14,12},{16,18},{18,... | collective-permute-start | bytes 1572872 | tf_op jit(solution)/shard_map/ppermute | solution.py:573
  62.4 3.2 %collective-permute-start.5 = (bf16[64,4096]{1,0:T(8,128)(2,1)}, bf16[64,4096]{1,0:T(8,128)(2,1)S(1)}, u32[]{:S(2)}, u32[]{:S(2)}) collective-permute-start(bf16[64,4096]{1,0:T(8,128)(2,1)} %collective-permute-done.1.rest_1_), channel_id=1, source_target_pairs={{0,2},{2,0},{4,6},{6,4},{8,10},{10,8},{12,14},{14,12},{16,18},{18,... | collective-permute-start | bytes 1572872 | tf_op jit(solution)/shard_map/ppermute | solution.py:573
  62.5 3.9 %collective-permute-start.6 = (bf16[64,4096]{1,0:T(8,128)(2,1)}, bf16[64,4096]{1,0:T(8,128)(2,1)S(1)}, u32[]{:S(2)}, u32[]{:S(2)}) collective-permute-start(bf16[64,4096]{1,0:T(8,128)(2,1)} %collective-permute-done.2.rest_2_), channel_id=1, source_target_pairs={{0,2},{2,0},{4,6},{6,4},{8,10},{10,8},{12,14},{14,12},{16,18},{18,... | collective-permute-start | bytes 1572872 | tf_op jit(solution)/shard_map/ppermute | solution.py:573
  62.9 3.5 %copy-start.5 = (bf16[64,4096]{1,0:T(8,128)(2,1)}, bf16[64,4096]{1,0:T(8,128)(2,1)S(1)}, u32[]{:S(2)}) copy-start(bf16[64,4096]{1,0:T(8,128)(2,1)S(1)} %collective-permute-done.3.rest_3_) | copy-start | bytes 1572868
  62.9 3.5 %collective-permute-start.7 = (bf16[64,4096]{1,0:T(8,128)(2,1)S(1)}, bf16[64,4096]{1,0:T(8,128)(2,1)}, u32[]{:S(2)}, u32[]{:S(2)}) collective-permute-start(bf16[64,4096]{1,0:T(8,128)(2,1)S(1)} %collective-permute-done.3.rest_3_), channel_id=1, source_target_pairs={{0,2},{2,0},{4,6},{6,4},{8,10},{10,8},{12,14},{14,12},{16,18},{18,... | collective-permute-start | bytes 1572872 | tf_op jit(solution)/shard_map/ppermute | solution.py:573
  63.9 2.5 %copy-start.6 = (bf16[64,4096]{1,0:T(8,128)(2,1)}, bf16[64,4096]{1,0:T(8,128)(2,1)S(1)}, u32[]{:S(2)}) copy-start(bf16[64,4096]{1,0:T(8,128)(2,1)S(1)} %collective-permute-done.4.rest_4_) | copy-start | bytes 1572868
  65.7 0.8 copy-start.7
  66.4 0.8 copy-start.8

commit v6 on v5

--- a/solution.py
+++ b/solution.py
@@ -313,19 +313,19 @@
     taps_hbm, weight_hbm, out_hbm, piece_hbm, taps_ref, out_ref, piece_ref, sems, out_sems
 ):
     steps = sems.shape[0] - 1
-    size = taps_ref.shape[0] // steps
+    size = taps_ref.shape[1] // steps
     spans = [pl.ds(i * size, size) for i in range(steps)]
     loads = start_all(
-        [(taps_hbm.at[s], taps_ref.at[s]) for s in spans]
+        [(taps_hbm.at[:, s], taps_ref.at[:, s]) for s in spans]
         + [(piece_source(weight_hbm, piece_hbm, 0), piece_ref)],
         sems,
     )
-    for load in loads[:steps]:
-        load.wait()
     stores = []
-    for i, span in enumerate(spans):
-        out_ref[span, :] = taps_ref[:, i * size : (i + 1) * size].astype(bf16).T
-        stores.append(pltpu.make_async_copy(out_ref.at[span], out_hbm.at[span], out_sems.at[i]))
+    for i in range(steps):
+        loads[i].wait()
+        at = slice(i * size, (i + 1) * size)
+        out_ref[at, :] = taps_ref[:, at].astype(bf16).T
+        stores.append(pltpu.make_async_copy(out_ref.at[spans[i]], out_hbm.at[spans[i]], out_sems.at[i]))
         stores[-1].start()
     loads[steps].wait()
     stores.append(pltpu.make_async_copy(piece_ref, piece_hbm, out_sems.at[steps]))
@@ -428,14 +428,14 @@
     group, core, x, z = where()
     size = ctx // (2 * PIECES)
     turned[:, :rows] = mixed_ref[:, group].reshape(rows, position).T
+    loads[0].wait()
+    own_part = dot(turned[:, :rows], weight_ref[0, :rows])
     pieces = []
     for half in (core, 1 - core):
         for k in held_pieces(x, z):
             start = (half * PIECES + k) * size
             pieces.append(mixed_ref[pl.ds(start, size), 1 - group])
     turned[:, rows:] = jnp.concatenate(pieces, axis=0).reshape(rows, position).T
-    loads[0].wait()
-    own_part = dot(turned[:, :rows], weight_ref[0, :rows])
     loads[1].wait()
     out_ref[:, :columns] = (own_part + dot(turned[:, rows:], weight_ref[0, rows:])).astype(bf16)
     stores = []
@@ -515,8 +515,8 @@
             pltpu.VMEM((position, width // ch), f32),
             pltpu.VMEM((width // ch, position), bf16),
             pltpu.VMEM(piece.shape, bf16),
-            pltpu.SemaphoreType.DMA((5,)),
-            pltpu.SemaphoreType.DMA((5,)),
+            pltpu.SemaphoreType.DMA((3,)),
+            pltpu.SemaphoreType.DMA((3,)),
         ],
         compiler_params=vmem(60),
         cost_estimate=cost(0, 2 * MIB),

time: 87.9 us -> 87.6 us (level)
  no operation moved by 1% of the time
where the time goes in v6:
time: 87.6 us; the launch traced here: 87.2 us
  Pallas kernels  36.8 us (42%)
  starting transfers between devices  29.9 us (34%)
  waiting for transfers between devices  18.6 us (21%)
  local copies, waits for them, and re-layouts  1.62 us (2%)
    all_to_all x1, starting transfers between devices, shards(): lax.all_to_all(taps.reshape(ctx, channels, position), 'ctx', split_axis=0...  9.28 us
    pallas_call x1, Pallas kernels, shards(): pl.pallas_call(out_kernel, in_specs=[VMEM, ANY], out_specs=ANY, out_shape...  7.39 us
    pallas_call x1, Pallas kernels, shards(): pl.pallas_call(project_kernel, in_specs=[ANY] * 2, out_specs=ANY, out_sha...  7.31 us
    pallas_call x1, Pallas kernels, shards(): pl.pallas_call(weights_kernel, in_specs=[ANY] * (1 + len(pieces)), out_sp...  6.73 us
    all_to_all x1, waiting for transfers between devices, shards(): lax.all_to_all(mixed.reshape(devices, channels, position), both, split_ax...  5.75 us
    all_to_all x1, starting transfers between devices, shards(): lax.all_to_all(mixed.reshape(devices, channels, position), both, split_ax...  5.69 us
    pallas_call x1, Pallas kernels, shards(): pl.pallas_call(conv_kernel, in_specs=[SMEM, VMEM, ANY, VMEM], out_specs=A...  5.66 us
    all_to_all x1, waiting for transfers between devices, shards(): lax.all_to_all(partial_value.reshape(devices, channels, position), both,...  5.64 us
  transfers between devices with their start and end apart: 11, of which 6 were waited for; matrix products, arithmetic and copies ran while one was open for 0% of the time, Pallas kernels for 31%

profile of v6, /device:TPU:1, one launch (start us, length us, event | category | flops | bytes accessed | tf_op | source)
XLA Modules:
  0.0 87.2 jit_solution(17596622841422897503)
XLA Ops:
  0.0 2.3 %shard_map.65 = (bf16[512,512]{1,0:T(8,128)(2,1)}, bf16[64,4096]{1,0:T(8,128)(2,1)}) custom-call(f32[512,512]{1,0:T(8,128)} %taps_hbm.1, bf16[512,8192]{1,0:T(8,128)(2,1)} %own_hbm.1), custom_call_target="tpu_custom_call" | custom-call | bytes 2097152 | tf_op jit(solution)/shard_map/pallas_call | solution.py:509
  2.3 3.6 %collective-permute-start = (bf16[64,4096]{1,0:T(8,128)(2,1)}, bf16[64,4096]{1,0:T(8,128)(2,1)S(1)}, u32[]{:S(2)}, u32[]{:S(2)}) collective-permute-start(bf16[64,4096]{1,0:T(8,128)(2,1)} %get-tuple-element.7), channel_id=1, source_target_pairs={{0,65},{2,67},{4,69},{6,71},{8,73},{10,75},{12,77},{14,79},{16,81}... | collective-permute-start | bytes 1572872 | tf_op jit(solution)/shard_map/ppermute | solution.py:524
  5.9 9.3 %all-to-all-start.1 = ((bf16[64,8,512]{2,1,0:T(8,128)(2,1)}), bf16[64,8,512]{2,1,0:T(8,128)(2,1)S(1)}, u32[]{:S(2)}, u32[]{:S(2)}) async-start(bf16[64,8,512]{2,1,0:T(8,128)(2,1)} %bitcast.8), calls=%async_computation.1 | async-start | bytes 1048576 | tf_op jit(solution)/shard_map/all_to_all | solution.py:525
  15.2 7.3 %shard_map.64.value_ref = bf16[64,2,8,512]{3,2,1,0:T(8,128)(2,1)} custom-call(bf16[512,4096]{1,0:T(8,128)(2,1)} %tokens_hbm.1, bf16[4096,1024]{1,0:T(8,128)(2,1)} %weight_hbm.3), custom_call_target="tpu_custom_call" | custom-call | flops 4294967296 | bytes 14680064 | tf_op jit(solution)/shard_map/pallas_call | solution.py:529
  22.5 0.0 collective-permute-done.after_ref.rest_0_
  22.5 0.0 copy-start.2
  22.5 0.8 copy-done.2
  23.3 3.8 %all-to-all-done.1.taps_ref = bf16[64,8,512]{2,1,0:T(8,128)(2,1)S(1)} async-done(((bf16[64,8,512]{2,1,0:T(8,128)(2,1)}), bf16[64,8,512]{2,1,0:T(8,128)(2,1)S(1)}, u32[]{:S(2)}, u32[]{:S(2)}) %all-to-all-start.1) | async-done | bytes 524320 | tf_op jit(solution)/shard_map/all_to_all | solution.py:525
  27.1 0.0 copy-start.4
  27.2 4.1 %all-to-all-start = ((bf16[128,8,512]{2,1,0:T(8,128)(2,1)}), bf16[128,8,512]{2,1,0:T(8,128)(2,1)S(1)}, u32[]{:S(2)}, u32[]{:S(2)}) async-start(bf16[128,8,512]{2,1,0:T(8,128)(2,1)} %bitcast.7), calls=%async_computation | async-start | bytes 2097152 | tf_op jit(solution)/shard_map/all_to_all | solution.py:555
  31.3 0.0 copy-done.4
  31.3 5.4 %shard_map.67.spec_hbm = f32[25344,256]{1,0:T(8,128)} custom-call(bf16[64,8,512]{2,1,0:T(8,128)(2,1)} %copy-done.4, f32[1224,256]{1,0:T(8,128)} %constant.2.clone.table_hbm.table_ref), custom_call_target="tpu_custom_call" | custom-call | flops 4000000000 | bytes 4194304 | tf_op jit(solution)/shard_map/pallas_call | solution.py:584
  36.7 0.0 copy-start.3
  36.7 0.0 copy-start
  36.7 0.0 copy-start.1
  36.8 2.0 %shard_map.69 = bf16[64,4096]{1,0:T(8,128)(2,1)} custom-call(bf16[512,8192]{1,0:T(8,128)(2,1)} %own_hbm.1, bf16[64,2,8,512]{3,2,1,0:T(8,128)(2,1)} %shard_map.66.after_ref), custom_call_target="tpu_custom_call" | custom-call | bytes 1048576 | tf_op jit(solution)/shard_map/pallas_call | solution.py:562
  38.8 2.7 %collective-permute-start.3 = (bf16[64,4096]{1,0:T(8,128)(2,1)}, bf16[64,4096]{1,0:T(8,128)(2,1)S(1)}, u32[]{:S(2)}, u32[]{:S(2)}) collective-permute-start(bf16[64,4096]{1,0:T(8,128)(2,1)} %shard_map.69), channel_id=1, source_target_pairs={{0,65},{2,67},{4,69},{6,71},{8,73},{10,75},{12,77},{14,79},{16,81}... | collective-permute-start | bytes 1572872 | tf_op jit(solution)/shard_map/ppermute | solution.py:571
  41.5 0.0 copy-done.3
  41.5 1.5 %collective-permute-start.1 = (bf16[64,4096]{1,0:T(8,128)(2,1)S(1)}, bf16[64,4096]{1,0:T(8,128)(2,1)}, u32[]{:S(2)}, u32[]{:S(2)}) collective-permute-start(bf16[64,4096]{1,0:T(8,128)(2,1)S(1)} %copy-done.3), channel_id=1, source_target_pairs={{0,4},{2,6},{4,0},{6,2},{8,12},{10,14},{12,8},{14,10},{16,20},{18,... | collective-permute-start | bytes 1572872 | tf_op jit(solution)/shard_map/ppermute | solution.py:561
  42.9 1.2 %collective-permute-start.2 = (bf16[64,4096]{1,0:T(8,128)(2,1)S(1)}, bf16[64,4096]{1,0:T(8,128)(2,1)}, u32[]{:S(2)}, u32[]{:S(2)}) collective-permute-start(bf16[64,4096]{1,0:T(8,128)(2,1)S(1)} %copy-done.3), channel_id=1, source_target_pairs={{0,16},{2,18},{4,20},{6,22},{8,24},{10,26},{12,28},{14,30},{16,0},... | collective-permute-start | bytes 1572872 | tf_op jit(solution)/shard_map/ppermute | solution.py:560
  44.1 5.6 %all-to-all-done = bf16[128,8,512]{2,1,0:T(8,128)(2,1)S(1)} async-done(((bf16[128,8,512]{2,1,0:T(8,128)(2,1)}), bf16[128,8,512]{2,1,0:T(8,128)(2,1)S(1)}, u32[]{:S(2)}, u32[]{:S(2)}) %all-to-all-start) | async-done | bytes 1048608 | tf_op jit(solution)/shard_map/all_to_all | solution.py:555
  49.8 0.0 copy-done
  49.8 0.0 copy-done.1
  49.8 5.7 %shard_map.68 = bf16[64,2,8,512]{3,2,1,0:T(8,128)(2,1)} custom-call(f32[512]{0:T(512)S(1)} %copy-done.1, bf16[64,2,8,512]{3,2,1,0:T(8,128)(2,1)S(1)} %bitcast.6, f32[25344,256]{1,0:T(8,128)} %shard_map.67.spec_hbm, f32[1224,256]{1,0:T(8,128)S(1)} %copy-done), custom_call_target="tpu_custom_call" | custom-call | flops 8000000000 | bytes 6291456 | tf_op jit(solution)/shard_map/pallas_call | solution.py:593
  55.5 5.7 %all-to-all-start.2 = ((bf16[128,8,512]{2,1,0:T(8,128)(2,1)}), bf16[128,8,512]{2,1,0:T(8,128)(2,1)S(1)}, u32[]{:S(2)}, u32[]{:S(2)}) async-start(bf16[128,8,512]{2,1,0:T(8,128)(2,1)} %bitcast.3), calls=%async_computation.2 | async-start | bytes 2097152 | tf_op jit(solution)/shard_map/all_to_all | solution.py:611
  61.2 1.1 %collective-permute-start.4 = (bf16[64,4096]{1,0:T(8,128)(2,1)S(1)}, bf16[64,4096]{1,0:T(8,128)(2,1)S(1)}, u32[]{:S(2)}, u32[]{:S(2)}) collective-permute-start(bf16[64,4096]{1,0:T(8,128)(2,1)S(1)} %copy-done.3), channel_id=1, source_target_pairs={{0,2},{2,0},{4,6},{6,4},{8,10},{10,8},{12,14},{14,12},{16,18},{18,... | collective-permute-start | bytes 1572872 | tf_op jit(solution)/shard_map/ppermute | solution.py:573
  62.3 0.0 collective-permute-done.1.rest_1_
  62.3 0.1 collective-permute-start.5
  62.4 0.0 collective-permute-done.2.rest_2_
  62.4 0.4 collective-permute-start.6
  62.8 0.0 collective-permute-done.3.rest_3_
  62.8 0.0 copy-start.5
  62.8 0.1 collective-permute-start.7
  62.9 0.9 %collective-permute-done.4.rest_4_ = bf16[64,4096]{1,0:T(8,128)(2,1)S(1)} collective-permute-done((bf16[64,4096]{1,0:T(8,128)(2,1)S(1)}, bf16[64,4096]{1,0:T(8,128)(2,1)S(1)}, u32[]{:S(2)}, u32[]{:S(2)}) %collective-permute-start.4) | collective-permute-done | bytes 524320 | tf_op jit(solution)/shard_map/ppermute | solution.py:573
  63.8 0.0 copy-start.6
  63.8 1.7 %collective-permute-done.5.rest_5_ = bf16[64,4096]{1,0:T(8,128)(2,1)S(1)} collective-permute-done((bf16[64,4096]{1,0:T(8,128)(2,1)}, bf16[64,4096]{1,0:T(8,128)(2,1)S(1)}, u32[]{:S(2)}, u32[]{:S(2)}) %collective-permute-start.5) | collective-permute-done | bytes 524320 | tf_op jit(solution)/shard_map/ppermute | solution.py:573
  65.6 0.0 copy-start.7
  65.6 0.7 collective-permute-done.6.rest_6_
  66.3 0.0 copy-start.8
  66.3 0.0 collective-permute-done.7.rest_7_
  66.3 0.0 copy-done.5
  66.3 0.0 copy-done.6
  66.3 0.0 copy-done.7
  66.4 0.8 copy-done.8
  67.1 6.7 %shard_map.70.weight_hbm = bf16[4,1024,1024]{2,1,0:T(8,128)(2,1)} custom-call(bf16[512,8192]{1,0:T(8,128)(2,1)} %own_hbm.1, bf16[64,4096]{1,0:T(8,128)(2,1)} %copy-done.2, bf16[64,4096]{1,0:T(8,128)(2,1)} %collective-permute-done.1.rest_1_, bf16[64,4096]{1,0:T(8,128)(2,1)} %collective-permute-done.2.rest_2_, bf16[64,4096]{1,0:T(8,128)(2,1)} %copy-done.5, ...), custom_call_target="tpu_custom_call" | custom-call | bytes 16777216 | tf_op jit(solution)/shard_map/pallas_call | solution.py:617
  73.9 5.8 %all-to-all-done.2 = bf16[128,8,512]{2,1,0:T(8,128)(2,1)S(1)} async-done(((bf16[128,8,512]{2,1,0:T(8,128)(2,1)}), bf16[128,8,512]{2,1,0:T(8,128)(2,1)S(1)}, u32[]{:S(2)}, u32[]{:S(2)}) %all-to-all-start.2) | async-done | bytes 1048608 | tf_op jit(solution)/shard_map/all_to_all | solution.py:611
  79.6 7.4 %shard_map.71 = bf16[512,4096]{1,0:T(8,128)(2,1)} custom-call(bf16[64,2,8,512]{3,2,1,0:T(8,128)(2,1)S(1)} %bitcast.5, bf16[4,1024,1024]{2,1,0:T(8,128)(2,1)} %shard_map.70.weight_hbm), custom_call_target="tpu_custom_call" | custom-call | flops 4294967296 | bytes 13631488 | tf_op jit(solution)/shard_map/pallas_call | solution.py:631
  (1 shorter events, 0.0 us)
Async XLA Ops:
  2.3 20.3 %collective-permute-start = (bf16[64,4096]{1,0:T(8,128)(2,1)}, bf16[64,4096]{1,0:T(8,128)(2,1)S(1)}, u32[]{:S(2)}, u32[]{:S(2)}) collective-permute-start(bf16[64,4096]{1,0:T(8,128)(2,1)} %get-tuple-element.7), channel_id=1, source_target_pairs={{0,65},{2,67},{4,69},{6,71},{8,73},{10,75},{12,77},{14,79},{16,81}... | collective-permute-start | bytes 1572872 | tf_op jit(solution)/shard_map/ppermute | solution.py:524
  5.9 21.2 %all-to-all-start.1 = ((bf16[64,8,512]{2,1,0:T(8,128)(2,1)}), bf16[64,8,512]{2,1,0:T(8,128)(2,1)S(1)}, u32[]{:S(2)}, u32[]{:S(2)}) async-start(bf16[64,8,512]{2,1,0:T(8,128)(2,1)} %bitcast.8), calls=%async_computation.1 | async-start | bytes 1048576 | tf_op jit(solution)/shard_map/all_to_all | solution.py:525
  22.5 0.8 copy-start.2
  27.1 4.1 %copy-start.4 = (bf16[64,8,512]{2,1,0:T(8,128)(2,1)}, bf16[64,8,512]{2,1,0:T(8,128)(2,1)S(1)}, u32[]{:S(2)}) copy-start(bf16[64,8,512]{2,1,0:T(8,128)(2,1)S(1)} %all-to-all-done.1.taps_ref) | copy-start | bytes 1572868
  27.2 22.6 %all-to-all-start = ((bf16[128,8,512]{2,1,0:T(8,128)(2,1)}), bf16[128,8,512]{2,1,0:T(8,128)(2,1)S(1)}, u32[]{:S(2)}, u32[]{:S(2)}) async-start(bf16[128,8,512]{2,1,0:T(8,128)(2,1)} %bitcast.7), calls=%async_computation | async-start | bytes 2097152 | tf_op jit(solution)/shard_map/all_to_all | solution.py:555
  36.7 4.8 %copy-start.3 = (bf16[64,4096]{1,0:T(8,128)(2,1)S(1)}, bf16[64,4096]{1,0:T(8,128)(2,1)}, u32[]{:S(2)}) copy-start(bf16[64,4096]{1,0:T(8,128)(2,1)} %copy-done.2) | copy-start | bytes 1572868
  36.7 13.1 %copy-start = (f32[1224,256]{1,0:T(8,128)S(1)}, f32[1224,256]{1,0:T(8,128)}, u32[]{:S(2)}) copy-start(f32[1224,256]{1,0:T(8,128)} %constant.2.clone.table_hbm.table_ref) | copy-start | bytes 3760132
  36.7 13.0 %copy-start.1 = (f32[512]{0:T(512)S(1)}, f32[512]{0:T(512)}, u32[]{:S(2)}) copy-start(f32[512]{0:T(512)} %gain_ref.1) | copy-start | bytes 6148
  38.8 24.1 %collective-permute-start.3 = (bf16[64,4096]{1,0:T(8,128)(2,1)}, bf16[64,4096]{1,0:T(8,128)(2,1)S(1)}, u32[]{:S(2)}, u32[]{:S(2)}) collective-permute-start(bf16[64,4096]{1,0:T(8,128)(2,1)} %shard_map.69), channel_id=1, source_target_pairs={{0,65},{2,67},{4,69},{6,71},{8,73},{10,75},{12,77},{14,79},{16,81}... | collective-permute-start | bytes 1572872 | tf_op jit(solution)/shard_map/ppermute | solution.py:571
  41.5 20.8 %collective-permute-start.1 = (bf16[64,4096]{1,0:T(8,128)(2,1)S(1)}, bf16[64,4096]{1,0:T(8,128)(2,1)}, u32[]{:S(2)}, u32[]{:S(2)}) collective-permute-start(bf16[64,4096]{1,0:T(8,128)(2,1)S(1)} %copy-done.3), channel_id=1, source_target_pairs={{0,4},{2,6},{4,0},{6,2},{8,12},{10,14},{12,8},{14,10},{16,20},{18,... | collective-permute-start | bytes 1572872 | tf_op jit(solution)/shard_map/ppermute | solution.py:561
  42.9 19.5 %collective-permute-start.2 = (bf16[64,4096]{1,0:T(8,128)(2,1)S(1)}, bf16[64,4096]{1,0:T(8,128)(2,1)}, u32[]{:S(2)}, u32[]{:S(2)}) collective-permute-start(bf16[64,4096]{1,0:T(8,128)(2,1)S(1)} %copy-done.3), channel_id=1, source_target_pairs={{0,16},{2,18},{4,20},{6,22},{8,24},{10,26},{12,28},{14,30},{16,0},... | collective-permute-start | bytes 1572872 | tf_op jit(solution)/shard_map/ppermute | solution.py:560
  55.5 24.2 %all-to-all-start.2 = ((bf16[128,8,512]{2,1,0:T(8,128)(2,1)}), bf16[128,8,512]{2,1,0:T(8,128)(2,1)S(1)}, u32[]{:S(2)}, u32[]{:S(2)}) async-start(bf16[128,8,512]{2,1,0:T(8,128)(2,1)} %bitcast.3), calls=%async_computation.2 | async-start | bytes 2097152 | tf_op jit(solution)/shard_map/all_to_all | solution.py:611
  61.2 2.7 %collective-permute-start.4 = (bf16[64,4096]{1,0:T(8,128)(2,1)S(1)}, bf16[64,4096]{1,0:T(8,128)(2,1)S(1)}, u32[]{:S(2)}, u32[]{:S(2)}) collective-permute-start(bf16[64,4096]{1,0:T(8,128)(2,1)S(1)} %copy-done.3), channel_id=1, source_target_pairs={{0,2},{2,0},{4,6},{6,4},{8,10},{10,8},{12,14},{14,12},{16,18},{18,... | collective-permute-start | bytes 1572872 | tf_op jit(solution)/shard_map/ppermute | solution.py:573
  62.3 3.2 %collective-permute-start.5 = (bf16[64,4096]{1,0:T(8,128)(2,1)}, bf16[64,4096]{1,0:T(8,128)(2,1)S(1)}, u32[]{:S(2)}, u32[]{:S(2)}) collective-permute-start(bf16[64,4096]{1,0:T(8,128)(2,1)} %collective-permute-done.1.rest_1_), channel_id=1, source_target_pairs={{0,2},{2,0},{4,6},{6,4},{8,10},{10,8},{12,14},{14,12},{16,18},{18,... | collective-permute-start | bytes 1572872 | tf_op jit(solution)/shard_map/ppermute | solution.py:573
  62.4 3.9 %collective-permute-start.6 = (bf16[64,4096]{1,0:T(8,128)(2,1)}, bf16[64,4096]{1,0:T(8,128)(2,1)S(1)}, u32[]{:S(2)}, u32[]{:S(2)}) collective-permute-start(bf16[64,4096]{1,0:T(8,128)(2,1)} %collective-permute-done.2.rest_2_), channel_id=1, source_target_pairs={{0,2},{2,0},{4,6},{6,4},{8,10},{10,8},{12,14},{14,12},{16,18},{18,... | collective-permute-start | bytes 1572872 | tf_op jit(solution)/shard_map/ppermute | solution.py:573
  62.8 3.5 %copy-start.5 = (bf16[64,4096]{1,0:T(8,128)(2,1)}, bf16[64,4096]{1,0:T(8,128)(2,1)S(1)}, u32[]{:S(2)}) copy-start(bf16[64,4096]{1,0:T(8,128)(2,1)S(1)} %collective-permute-done.3.rest_3_) | copy-start | bytes 1572868
  62.8 3.5 %collective-permute-start.7 = (bf16[64,4096]{1,0:T(8,128)(2,1)S(1)}, bf16[64,4096]{1,0:T(8,128)(2,1)}, u32[]{:S(2)}, u32[]{:S(2)}) collective-permute-start(bf16[64,4096]{1,0:T(8,128)(2,1)S(1)} %collective-permute-done.3.rest_3_), channel_id=1, source_target_pairs={{0,2},{2,0},{4,6},{6,4},{8,10},{10,8},{12,14},{14,12},{16,18},{18,... | collective-permute-start | bytes 1572872 | tf_op jit(solution)/shard_map/ppermute | solution.py:573
  63.8 2.5 %copy-start.6 = (bf16[64,4096]{1,0:T(8,128)(2,1)}, bf16[64,4096]{1,0:T(8,128)(2,1)S(1)}, u32[]{:S(2)}) copy-start(bf16[64,4096]{1,0:T(8,128)(2,1)S(1)} %collective-permute-done.4.rest_4_) | copy-start | bytes 1572868
  65.6 0.8 copy-start.7
  66.3 0.8 copy-start.8

commit v7 on v6

--- a/solution.py
+++ b/solution.py
@@ -573,7 +573,7 @@
     pieces = pieces + [lax.ppermute(p, both, other_core) for p in pieces]
 
     lines = channels * 4 * ctx + 4 * TILE
-    flat = (quarters, ctx * channels, lanes)
+    flat = (quarters, ctx * channels + channels, lanes)
     held = [
         pltpu.VMEM((3 * (position // 2), position // 2), bf16),
         pltpu.VMEM(flat, f32),

time: 87.6 us -> 87.6 us (level)
  no operation moved by 1% of the time
where the time goes in v7:
time: 87.6 us; the launch traced here: 87.2 us
  Pallas kernels  36.8 us (42%)
  starting transfers between devices  29.9 us (34%)
  waiting for transfers between devices  18.6 us (21%)
  local copies, waits for them, and re-layouts  1.62 us (2%)
    all_to_all x1, starting transfers between devices, shards(): lax.all_to_all(taps.reshape(ctx, channels, position), 'ctx', split_axis=0...  9.28 us
    pallas_call x1, Pallas kernels, shards(): pl.pallas_call(out_kernel, in_specs=[VMEM, ANY], out_specs=ANY, out_shape...  7.39 us
    pallas_call x1, Pallas kernels, shards(): pl.pallas_call(project_kernel, in_specs=[ANY] * 2, out_specs=ANY, out_sha...  7.31 us
    pallas_call x1, Pallas kernels, shards(): pl.pallas_call(weights_kernel, in_specs=[ANY] * (1 + len(pieces)), out_sp...  6.73 us
    all_to_all x1, waiting for transfers between devices, shards(): lax.all_to_all(mixed.reshape(devices, channels, position), both, split_ax...  5.75 us
    all_to_all x1, starting transfers between devices, shards(): lax.all_to_all(mixed.reshape(devices, channels, position), both, split_ax...  5.69 us
    pallas_call x1, Pallas kernels, shards(): pl.pallas_call(conv_kernel, in_specs=[SMEM, VMEM, ANY, VMEM], out_specs=A...  5.66 us
    all_to_all x1, waiting for transfers between devices, shards(): lax.all_to_all(partial_value.reshape(devices, channels, position), both,...  5.64 us
  transfers between devices with their start and end apart: 11, of which 6 were waited for; matrix products, arithmetic and copies ran while one was open for 0% of the time, Pallas kernels for 31%

profile of v7, /device:TPU:1, one launch (start us, length us, event | category | flops | bytes accessed | tf_op | source)
XLA Modules:
  0.0 87.2 jit_solution(16613810364057230654)
XLA Ops:
  0.0 2.3 %shard_map.65 = (bf16[512,512]{1,0:T(8,128)(2,1)}, bf16[64,4096]{1,0:T(8,128)(2,1)}) custom-call(f32[512,512]{1,0:T(8,128)} %taps_hbm.1, bf16[512,8192]{1,0:T(8,128)(2,1)} %own_hbm.1), custom_call_target="tpu_custom_call" | custom-call | bytes 2097152 | tf_op jit(solution)/shard_map/pallas_call | solution.py:509
  2.3 3.6 %collective-permute-start = (bf16[64,4096]{1,0:T(8,128)(2,1)}, bf16[64,4096]{1,0:T(8,128)(2,1)S(1)}, u32[]{:S(2)}, u32[]{:S(2)}) collective-permute-start(bf16[64,4096]{1,0:T(8,128)(2,1)} %get-tuple-element.7), channel_id=1, source_target_pairs={{0,65},{2,67},{4,69},{6,71},{8,73},{10,75},{12,77},{14,79},{16,81}... | collective-permute-start | bytes 1572872 | tf_op jit(solution)/shard_map/ppermute | solution.py:524
  5.9 9.3 %all-to-all-start.1 = ((bf16[64,8,512]{2,1,0:T(8,128)(2,1)}), bf16[64,8,512]{2,1,0:T(8,128)(2,1)S(1)}, u32[]{:S(2)}, u32[]{:S(2)}) async-start(bf16[64,8,512]{2,1,0:T(8,128)(2,1)} %bitcast.8), calls=%async_computation.1 | async-start | bytes 1048576 | tf_op jit(solution)/shard_map/all_to_all | solution.py:525
  15.2 7.3 %shard_map.64.value_ref = bf16[64,2,8,512]{3,2,1,0:T(8,128)(2,1)} custom-call(bf16[512,4096]{1,0:T(8,128)(2,1)} %tokens_hbm.1, bf16[4096,1024]{1,0:T(8,128)(2,1)} %weight_hbm.3), custom_call_target="tpu_custom_call" | custom-call | flops 4294967296 | bytes 14680064 | tf_op jit(solution)/shard_map/pallas_call | solution.py:529
  22.5 0.0 collective-permute-done.after_ref.rest_0_
  22.5 0.0 copy-start.2
  22.5 0.8 copy-done.2
  23.3 3.8 %all-to-all-done.1.taps_ref = bf16[64,8,512]{2,1,0:T(8,128)(2,1)S(1)} async-done(((bf16[64,8,512]{2,1,0:T(8,128)(2,1)}), bf16[64,8,512]{2,1,0:T(8,128)(2,1)S(1)}, u32[]{:S(2)}, u32[]{:S(2)}) %all-to-all-start.1) | async-done | bytes 524320 | tf_op jit(solution)/shard_map/all_to_all | solution.py:525
  27.1 0.0 copy-start.4
  27.2 4.1 %all-to-all-start = ((bf16[128,8,512]{2,1,0:T(8,128)(2,1)}), bf16[128,8,512]{2,1,0:T(8,128)(2,1)S(1)}, u32[]{:S(2)}, u32[]{:S(2)}) async-start(bf16[128,8,512]{2,1,0:T(8,128)(2,1)} %bitcast.7), calls=%async_computation | async-start | bytes 2097152 | tf_op jit(solution)/shard_map/all_to_all | solution.py:555
  31.3 0.0 copy-done.4
  31.3 5.4 %shard_map.67.spec_hbm = f32[25344,256]{1,0:T(8,128)} custom-call(bf16[64,8,512]{2,1,0:T(8,128)(2,1)} %copy-done.4, f32[1224,256]{1,0:T(8,128)} %constant.2.clone.table_hbm.table_ref), custom_call_target="tpu_custom_call" | custom-call | flops 4000000000 | bytes 4194304 | tf_op jit(solution)/shard_map/pallas_call | solution.py:584
  36.7 0.0 copy-start.3
  36.7 0.0 copy-start
  36.7 0.0 copy-start.1
  36.8 2.0 %shard_map.69 = bf16[64,4096]{1,0:T(8,128)(2,1)} custom-call(bf16[512,8192]{1,0:T(8,128)(2,1)} %own_hbm.1, bf16[64,2,8,512]{3,2,1,0:T(8,128)(2,1)} %shard_map.66.after_ref), custom_call_target="tpu_custom_call" | custom-call | bytes 1048576 | tf_op jit(solution)/shard_map/pallas_call | solution.py:562
  38.8 2.7 %collective-permute-start.3 = (bf16[64,4096]{1,0:T(8,128)(2,1)}, bf16[64,4096]{1,0:T(8,128)(2,1)S(1)}, u32[]{:S(2)}, u32[]{:S(2)}) collective-permute-start(bf16[64,4096]{1,0:T(8,128)(2,1)} %shard_map.69), channel_id=1, source_target_pairs={{0,65},{2,67},{4,69},{6,71},{8,73},{10,75},{12,77},{14,79},{16,81}... | collective-permute-start | bytes 1572872 | tf_op jit(solution)/shard_map/ppermute | solution.py:571
  41.5 0.0 copy-done.3
  41.5 1.5 %collective-permute-start.1 = (bf16[64,4096]{1,0:T(8,128)(2,1)S(1)}, bf16[64,4096]{1,0:T(8,128)(2,1)}, u32[]{:S(2)}, u32[]{:S(2)}) collective-permute-start(bf16[64,4096]{1,0:T(8,128)(2,1)S(1)} %copy-done.3), channel_id=1, source_target_pairs={{0,4},{2,6},{4,0},{6,2},{8,12},{10,14},{12,8},{14,10},{16,20},{18,... | collective-permute-start | bytes 1572872 | tf_op jit(solution)/shard_map/ppermute | solution.py:561
  42.9 1.2 %collective-permute-start.2 = (bf16[64,4096]{1,0:T(8,128)(2,1)S(1)}, bf16[64,4096]{1,0:T(8,128)(2,1)}, u32[]{:S(2)}, u32[]{:S(2)}) collective-permute-start(bf16[64,4096]{1,0:T(8,128)(2,1)S(1)} %copy-done.3), channel_id=1, source_target_pairs={{0,16},{2,18},{4,20},{6,22},{8,24},{10,26},{12,28},{14,30},{16,0},... | collective-permute-start | bytes 1572872 | tf_op jit(solution)/shard_map/ppermute | solution.py:560
  44.1 5.6 %all-to-all-done = bf16[128,8,512]{2,1,0:T(8,128)(2,1)S(1)} async-done(((bf16[128,8,512]{2,1,0:T(8,128)(2,1)}), bf16[128,8,512]{2,1,0:T(8,128)(2,1)S(1)}, u32[]{:S(2)}, u32[]{:S(2)}) %all-to-all-start) | async-done | bytes 1048608 | tf_op jit(solution)/shard_map/all_to_all | solution.py:555
  49.8 0.0 copy-done
  49.8 0.0 copy-done.1
  49.8 5.7 %shard_map.68 = bf16[64,2,8,512]{3,2,1,0:T(8,128)(2,1)} custom-call(f32[512]{0:T(512)S(1)} %copy-done.1, bf16[64,2,8,512]{3,2,1,0:T(8,128)(2,1)S(1)} %bitcast.6, f32[25344,256]{1,0:T(8,128)} %shard_map.67.spec_hbm, f32[1224,256]{1,0:T(8,128)S(1)} %copy-done), custom_call_target="tpu_custom_call" | custom-call | flops 8000000000 | bytes 6291456 | tf_op jit(solution)/shard_map/pallas_call | solution.py:593
  55.5 5.7 %all-to-all-start.2 = ((bf16[128,8,512]{2,1,0:T(8,128)(2,1)}), bf16[128,8,512]{2,1,0:T(8,128)(2,1)S(1)}, u32[]{:S(2)}, u32[]{:S(2)}) async-start(bf16[128,8,512]{2,1,0:T(8,128)(2,1)} %bitcast.3), calls=%async_computation.2 | async-start | bytes 2097152 | tf_op jit(solution)/shard_map/all_to_all | solution.py:611
  61.2 1.1 %collective-permute-start.4 = (bf16[64,4096]{1,0:T(8,128)(2,1)S(1)}, bf16[64,4096]{1,0:T(8,128)(2,1)S(1)}, u32[]{:S(2)}, u32[]{:S(2)}) collective-permute-start(bf16[64,4096]{1,0:T(8,128)(2,1)S(1)} %copy-done.3), channel_id=1, source_target_pairs={{0,2},{2,0},{4,6},{6,4},{8,10},{10,8},{12,14},{14,12},{16,18},{18,... | collective-permute-start | bytes 1572872 | tf_op jit(solution)/shard_map/ppermute | solution.py:573
  62.3 0.0 collective-permute-done.1.rest_1_
  62.3 0.1 collective-permute-start.5
  62.4 0.0 collective-permute-done.2.rest_2_
  62.4 0.4 collective-permute-start.6
  62.8 0.0 collective-permute-done.3.rest_3_
  62.8 0.0 copy-start.5
  62.8 0.1 collective-permute-start.7
  62.9 0.9 %collective-permute-done.4.rest_4_ = bf16[64,4096]{1,0:T(8,128)(2,1)S(1)} collective-permute-done((bf16[64,4096]{1,0:T(8,128)(2,1)S(1)}, bf16[64,4096]{1,0:T(8,128)(2,1)S(1)}, u32[]{:S(2)}, u32[]{:S(2)}) %collective-permute-start.4) | collective-permute-done | bytes 524320 | tf_op jit(solution)/shard_map/ppermute | solution.py:573
  63.8 0.0 copy-start.6
  63.8 1.7 %collective-permute-done.5.rest_5_ = bf16[64,4096]{1,0:T(8,128)(2,1)S(1)} collective-permute-done((bf16[64,4096]{1,0:T(8,128)(2,1)}, bf16[64,4096]{1,0:T(8,128)(2,1)S(1)}, u32[]{:S(2)}, u32[]{:S(2)}) %collective-permute-start.5) | collective-permute-done | bytes 524320 | tf_op jit(solution)/shard_map/ppermute | solution.py:573
  65.6 0.0 copy-start.7
  65.6 0.7 collective-permute-done.6.rest_6_
  66.3 0.0 copy-start.8
  66.3 0.0 collective-permute-done.7.rest_7_
  66.3 0.0 copy-done.5
  66.3 0.0 copy-done.6
  66.3 0.0 copy-done.7
  66.4 0.8 copy-done.8
  67.1 6.7 %shard_map.70.weight_hbm = bf16[4,1024,1024]{2,1,0:T(8,128)(2,1)} custom-call(bf16[512,8192]{1,0:T(8,128)(2,1)} %own_hbm.1, bf16[64,4096]{1,0:T(8,128)(2,1)} %copy-done.2, bf16[64,4096]{1,0:T(8,128)(2,1)} %collective-permute-done.1.rest_1_, bf16[64,4096]{1,0:T(8,128)(2,1)} %collective-permute-done.2.rest_2_, bf16[64,4096]{1,0:T(8,128)(2,1)} %copy-done.5, ...), custom_call_target="tpu_custom_call" | custom-call | bytes 16777216 | tf_op jit(solution)/shard_map/pallas_call | solution.py:617
  73.9 5.8 %all-to-all-done.2 = bf16[128,8,512]{2,1,0:T(8,128)(2,1)S(1)} async-done(((bf16[128,8,512]{2,1,0:T(8,128)(2,1)}), bf16[128,8,512]{2,1,0:T(8,128)(2,1)S(1)}, u32[]{:S(2)}, u32[]{:S(2)}) %all-to-all-start.2) | async-done | bytes 1048608 | tf_op jit(solution)/shard_map/all_to_all | solution.py:611
  79.6 7.4 %shard_map.71 = bf16[512,4096]{1,0:T(8,128)(2,1)} custom-call(bf16[64,2,8,512]{3,2,1,0:T(8,128)(2,1)S(1)} %bitcast.5, bf16[4,1024,1024]{2,1,0:T(8,128)(2,1)} %shard_map.70.weight_hbm), custom_call_target="tpu_custom_call" | custom-call | flops 4294967296 | bytes 13631488 | tf_op jit(solution)/shard_map/pallas_call | solution.py:631
  (1 shorter events, 0.0 us)
Async XLA Ops:
  2.3 20.3 %collective-permute-start = (bf16[64,4096]{1,0:T(8,128)(2,1)}, bf16[64,4096]{1,0:T(8,128)(2,1)S(1)}, u32[]{:S(2)}, u32[]{:S(2)}) collective-permute-start(bf16[64,4096]{1,0:T(8,128)(2,1)} %get-tuple-element.7), channel_id=1, source_target_pairs={{0,65},{2,67},{4,69},{6,71},{8,73},{10,75},{12,77},{14,79},{16,81}... | collective-permute-start | bytes 1572872 | tf_op jit(solution)/shard_map/ppermute | solution.py:524
  5.9 21.2 %all-to-all-start.1 = ((bf16[64,8,512]{2,1,0:T(8,128)(2,1)}), bf16[64,8,512]{2,1,0:T(8,128)(2,1)S(1)}, u32[]{:S(2)}, u32[]{:S(2)}) async-start(bf16[64,8,512]{2,1,0:T(8,128)(2,1)} %bitcast.8), calls=%async_computation.1 | async-start | bytes 1048576 | tf_op jit(solution)/shard_map/all_to_all | solution.py:525
  22.5 0.8 copy-start.2
  27.1 4.1 %copy-start.4 = (bf16[64,8,512]{2,1,0:T(8,128)(2,1)}, bf16[64,8,512]{2,1,0:T(8,128)(2,1)S(1)}, u32[]{:S(2)}) copy-start(bf16[64,8,512]{2,1,0:T(8,128)(2,1)S(1)} %all-to-all-done.1.taps_ref) | copy-start | bytes 1572868
  27.2 22.6 %all-to-all-start = ((bf16[128,8,512]{2,1,0:T(8,128)(2,1)}), bf16[128,8,512]{2,1,0:T(8,128)(2,1)S(1)}, u32[]{:S(2)}, u32[]{:S(2)}) async-start(bf16[128,8,512]{2,1,0:T(8,128)(2,1)} %bitcast.7), calls=%async_computation | async-start | bytes 2097152 | tf_op jit(solution)/shard_map/all_to_all | solution.py:555
  36.7 4.8 %copy-start.3 = (bf16[64,4096]{1,0:T(8,128)(2,1)S(1)}, bf16[64,4096]{1,0:T(8,128)(2,1)}, u32[]{:S(2)}) copy-start(bf16[64,4096]{1,0:T(8,128)(2,1)} %copy-done.2) | copy-start | bytes 1572868
  36.7 13.1 %copy-start = (f32[1224,256]{1,0:T(8,128)S(1)}, f32[1224,256]{1,0:T(8,128)}, u32[]{:S(2)}) copy-start(f32[1224,256]{1,0:T(8,128)} %constant.2.clone.table_hbm.table_ref) | copy-start | bytes 3760132
  36.7 13.0 %copy-start.1 = (f32[512]{0:T(512)S(1)}, f32[512]{0:T(512)}, u32[]{:S(2)}) copy-start(f32[512]{0:T(512)} %gain_ref.1) | copy-start | bytes 6148
  38.8 24.1 %collective-permute-start.3 = (bf16[64,4096]{1,0:T(8,128)(2,1)}, bf16[64,4096]{1,0:T(8,128)(2,1)S(1)}, u32[]{:S(2)}, u32[]{:S(2)}) collective-permute-start(bf16[64,4096]{1,0:T(8,128)(2,1)} %shard_map.69), channel_id=1, source_target_pairs={{0,65},{2,67},{4,69},{6,71},{8,73},{10,75},{12,77},{14,79},{16,81}... | collective-permute-start | bytes 1572872 | tf_op jit(solution)/shard_map/ppermute | solution.py:571
  41.5 20.8 %collective-permute-start.1 = (bf16[64,4096]{1,0:T(8,128)(2,1)S(1)}, bf16[64,4096]{1,0:T(8,128)(2,1)}, u32[]{:S(2)}, u32[]{:S(2)}) collective-permute-start(bf16[64,4096]{1,0:T(8,128)(2,1)S(1)} %copy-done.3), channel_id=1, source_target_pairs={{0,4},{2,6},{4,0},{6,2},{8,12},{10,14},{12,8},{14,10},{16,20},{18,... | collective-permute-start | bytes 1572872 | tf_op jit(solution)/shard_map/ppermute | solution.py:561
  42.9 19.5 %collective-permute-start.2 = (bf16[64,4096]{1,0:T(8,128)(2,1)S(1)}, bf16[64,4096]{1,0:T(8,128)(2,1)}, u32[]{:S(2)}, u32[]{:S(2)}) collective-permute-start(bf16[64,4096]{1,0:T(8,128)(2,1)S(1)} %copy-done.3), channel_id=1, source_target_pairs={{0,16},{2,18},{4,20},{6,22},{8,24},{10,26},{12,28},{14,30},{16,0},... | collective-permute-start | bytes 1572872 | tf_op jit(solution)/shard_map/ppermute | solution.py:560
  55.5 24.2 %all-to-all-start.2 = ((bf16[128,8,512]{2,1,0:T(8,128)(2,1)}), bf16[128,8,512]{2,1,0:T(8,128)(2,1)S(1)}, u32[]{:S(2)}, u32[]{:S(2)}) async-start(bf16[128,8,512]{2,1,0:T(8,128)(2,1)} %bitcast.3), calls=%async_computation.2 | async-start | bytes 2097152 | tf_op jit(solution)/shard_map/all_to_all | solution.py:611
  61.2 2.7 %collective-permute-start.4 = (bf16[64,4096]{1,0:T(8,128)(2,1)S(1)}, bf16[64,4096]{1,0:T(8,128)(2,1)S(1)}, u32[]{:S(2)}, u32[]{:S(2)}) collective-permute-start(bf16[64,4096]{1,0:T(8,128)(2,1)S(1)} %copy-done.3), channel_id=1, source_target_pairs={{0,2},{2,0},{4,6},{6,4},{8,10},{10,8},{12,14},{14,12},{16,18},{18,... | collective-permute-start | bytes 1572872 | tf_op jit(solution)/shard_map/ppermute | solution.py:573
  62.3 3.2 %collective-permute-start.5 = (bf16[64,4096]{1,0:T(8,128)(2,1)}, bf16[64,4096]{1,0:T(8,128)(2,1)S(1)}, u32[]{:S(2)}, u32[]{:S(2)}) collective-permute-start(bf16[64,4096]{1,0:T(8,128)(2,1)} %collective-permute-done.1.rest_1_), channel_id=1, source_target_pairs={{0,2},{2,0},{4,6},{6,4},{8,10},{10,8},{12,14},{14,12},{16,18},{18,... | collective-permute-start | bytes 1572872 | tf_op jit(solution)/shard_map/ppermute | solution.py:573
  62.4 3.9 %collective-permute-start.6 = (bf16[64,4096]{1,0:T(8,128)(2,1)}, bf16[64,4096]{1,0:T(8,128)(2,1)S(1)}, u32[]{:S(2)}, u32[]{:S(2)}) collective-permute-start(bf16[64,4096]{1,0:T(8,128)(2,1)} %collective-permute-done.2.rest_2_), channel_id=1, source_target_pairs={{0,2},{2,0},{4,6},{6,4},{8,10},{10,8},{12,14},{14,12},{16,18},{18,... | collective-permute-start | bytes 1572872 | tf_op jit(solution)/shard_map/ppermute | solution.py:573
  62.8 3.5 %copy-start.5 = (bf16[64,4096]{1,0:T(8,128)(2,1)}, bf16[64,4096]{1,0:T(8,128)(2,1)S(1)}, u32[]{:S(2)}) copy-start(bf16[64,4096]{1,0:T(8,128)(2,1)S(1)} %collective-permute-done.3.rest_3_) | copy-start | bytes 1572868
  62.8 3.5 %collective-permute-start.7 = (bf16[64,4096]{1,0:T(8,128)(2,1)S(1)}, bf16[64,4096]{1,0:T(8,128)(2,1)}, u32[]{:S(2)}, u32[]{:S(2)}) collective-permute-start(bf16[64,4096]{1,0:T(8,128)(2,1)S(1)} %collective-permute-done.3.rest_3_), channel_id=1, source_target_pairs={{0,2},{2,0},{4,6},{6,4},{8,10},{10,8},{12,14},{14,12},{16,18},{18,... | collective-permute-start | bytes 1572872 | tf_op jit(solution)/shard_map/ppermute | solution.py:573
  63.8 2.5 %copy-start.6 = (bf16[64,4096]{1,0:T(8,128)(2,1)}, bf16[64,4096]{1,0:T(8,128)(2,1)S(1)}, u32[]{:S(2)}) copy-start(bf16[64,4096]{1,0:T(8,128)(2,1)S(1)} %collective-permute-done.4.rest_4_) | copy-start | bytes 1572868
  65.6 0.8 copy-start.7
  66.3 0.8 copy-start.8
